TPU v7x, 256 devices: a whole 4x4x8 slice. The times are simulated.
256 devices in a mesh: rows: 32 (over z, y_lo, core), pairs: 8 (over y_hi, x).
Axes of the slice: x: 4, y: 4 (y_hi: 2, y_lo: 2; y = y_hi * 2 + y_lo), z: 8, core: 2. Of those that a mesh axis runs over, the one named last changes fastest.
Arguments:
- sample: float32 [8192, 4096], P('rows', 'pairs'), may hold values from -6 to 6
- column_scale: float32 [4096], P('pairs'), may hold values from 0.3 to 3
- inner_order: int32 [4, 256], replicated, may hold values from 0 to 255, each once within a row
Outputs:
- rotated: float32 [8192, 4096], P('rows', 'pairs')
- basis: float32 [4096, 4096], P('rows', 'pairs')
Inputs may be any that keep to these rules, and one draw needn't show every extreme that they name: `inner_order`: each row is a permutation of 0 to 255.
All inputs are finite; a program needn't handle non-finite values.
Results may differ from a plain program's by a relative error of at most 0.0003.
Values sent between devices are 32-bit elements; how exact they have to be, the bound alone decides.
No kernel may reach another device: no remote copies, remote signals or barrier semaphores. Data moves between devices by JAX's collectives and lax.ppermute only.
A program may use at most 64 MiB of HBM per device.

v0:
```python
import jax
import jax.numpy as jnp
from jax import lax
from jax.sharding import PartitionSpec as P

BLOCK = 128
W = 4096
STEPS = 4
ROUNDS = 8


def from_behind(block, axis, distance):
    devices = range(lax.axis_size(axis))
    route = [((i - distance) % len(devices), i) for i in devices]
    return lax.ppermute(block, axis, route)


def partner_take(matrix, r, axis):
    n = matrix.shape[axis]
    m = n - 1
    main = lax.slice_in_dim(matrix, 0, m, axis=axis)
    rolled = jnp.roll(jnp.flip(main, axis), 2 * r + 1, axis=axis)
    last = lax.slice_in_dim(matrix, m, n, axis=axis)
    at_round = lax.dynamic_slice_in_dim(matrix, r, 1, axis)
    shape = [1] * matrix.ndim
    shape[axis] = m
    marker = (jnp.arange(m, dtype=jnp.int32) == r).reshape(shape)
    rolled = jnp.where(marker, last, rolled)
    return jnp.concatenate([rolled, at_round], axis)


def exact_dot(left, right):
    return jnp.dot(left, right, precision=lax.Precision.HIGHEST, preferred_element_type=jnp.float32)


def jacobi(gram_mat, ordering, count):
    n = gram_mat.shape[0]
    m = n - 1
    values = jnp.arange(n, dtype=jnp.int32)
    permuter = jnp.where(ordering[:, None] == values[None, :], 1.0, 0.0).astype(jnp.float32)
    identity = jnp.where(values[:, None] == values[None, :], 1.0, 0.0).astype(jnp.float32)
    state_g = exact_dot(exact_dot(permuter, gram_mat), permuter.T)
    state_q = identity

    def round_fn(r, state):
        g, q = state
        offset = (values - r) % m
        leading = (offset >= 1) & (offset <= n // 2 - 1) | (values == m)
        diagonal = jnp.sum(g * identity, axis=0)
        diag_other = partner_take(diagonal, r, 0)
        taken = partner_take(g, r, 1)
        across = jnp.sum(taken * identity, axis=0)
        cross = jnp.where(leading, across, partner_take(across, r, 0))
        gpp = jnp.where(leading, diagonal, diag_other)
        gqq = jnp.where(leading, diag_other, diagonal)
        d = gqq - gpp
        root = jnp.sqrt(d * d + 4.0 * cross * cross)
        t = 2.0 * cross * d / ((jnp.abs(d) + root) * root + 1e-06 * (gpp + gqq) * (gpp + gqq))
        c = 1.0 / jnp.sqrt(1.0 + t * t)
        s = t * c
        s_col = jnp.where(leading, -s, s)
        g = c[None, :] * g + s_col[None, :] * taken
        g = c[:, None] * g + s_col[:, None] * partner_take(g, r, 0)
        q = c[None, :] * q + s_col[None, :] * partner_take(q, r, 1)
        return (g, q)

    state_g, state_q = lax.fori_loop(0, count, round_fn, (state_g, state_q))
    back_g = exact_dot(exact_dot(permuter.T, state_g), permuter)
    back_q = exact_dot(exact_dot(permuter.T, state_q), permuter)
    return (back_g, back_q)


def body(sample, column_scale, inner_order):
    data = sample * column_scale[None, :]
    local_rows = data.shape[0]
    width = data.shape[1]
    count = width // (2 * BLOCK)
    basis_rows = W // lax.axis_size("rows")
    row_start = lax.axis_index("rows") * basis_rows
    col_start = lax.axis_index("pairs") * width
    row_ids = jnp.arange(basis_rows, dtype=jnp.int32)[:, None] + row_start
    col_ids = jnp.arange(width, dtype=jnp.int32)[None, :] + col_start
    basis = jnp.where(row_ids == col_ids, 1.0, 0.0).astype(jnp.float32)
    joined = data.reshape(local_rows, count, 2 * BLOCK)
    basis_join = basis.reshape(basis_rows, count, 2 * BLOCK)
    for section in range(STEPS):
        if section > 0:
            top_data = joined[..., :BLOCK]
            low_data = joined[..., BLOCK:]
            top_basis = basis_join[..., :BLOCK]
            low_basis = basis_join[..., BLOCK:]
            leaving_top = jnp.concatenate([top_data[:, -1], top_basis[:, -1]], 0)
            leaving_low = jnp.concatenate([low_data[:, 0], low_basis[:, 0]], 0)
            coming_top = from_behind(leaving_top, "pairs", 1)
            coming_low = from_behind(leaving_low, "pairs", -1)
            edge = local_rows + basis_rows
            top_data = jnp.concatenate(
                [coming_top[None, :local_rows].transpose(1, 0, 2), top_data[:, :-1]], 1
            )
            top_basis = jnp.concatenate(
                [coming_top[None, local_rows:edge].transpose(1, 0, 2), top_basis[:, :-1]], 1
            )
            low_data = jnp.concatenate(
                [low_data[:, 1:], coming_low[None, :local_rows].transpose(1, 0, 2)], 1
            )
            low_basis = jnp.concatenate(
                [low_basis[:, 1:], coming_low[None, local_rows:edge].transpose(1, 0, 2)], 1
            )
            joined = jnp.concatenate([top_data, low_data], -1)
            basis_join = jnp.concatenate([top_basis, low_basis], -1)
        gram = lax.psum(
            jnp.einsum("rpi,rpj->pij", joined, joined, precision=lax.Precision.HIGHEST), "rows"
        )
        rotations = jax.vmap(lambda g: jacobi(g, inner_order[section], ROUNDS)[1])(gram)
        joined = jnp.einsum("rpi,pij->rpj", joined, rotations, precision=lax.Precision.HIGHEST)
        basis_join = jnp.einsum(
            "rpi,pij->rpj", basis_join, rotations, precision=lax.Precision.HIGHEST
        )
    return (joined.reshape(local_rows, width), basis_join.reshape(basis_rows, width))


def solution(mesh):
    return jax.shard_map(
        body,
        mesh=mesh,
        in_specs=(P("rows", "pairs"), P("pairs"), P()),
        out_specs=(P("rows", "pairs"), P("rows", "pairs")),
        check_vma=False,
    )
```

profile of v0, /device:TPU:7, one launch (start us, length us, event | category | flops | bytes accessed | tf_op | source)
XLA Modules:
  0.0 1474.8 jit_solution(16118258789333908882)
XLA Ops:
  12.0 226.8 %all-reduce.5.cloned.1.call-done = f32[2,256,256]{2,1,0:T(8,128)} async-done(((f32[2,256,256]{2,1,0:T(8,128)}), f32[2,256,256]{2,1,0:T(8,128)}) %all-reduce.5.cloned.1.call-update) | async-done | bytes 524304 | tf_op jit(solution)/shard_map/psum | solution.py:111
  241.6 122.3 %while.99 = (s32[]{:T(128)}, f32[2,256,256]{1,0,2:T(2,128)S(1)}, f32[2,256,256]{1,0,2:T(2,128)S(1)}, s32[]{:T(128)}, s32[1]{0:T(128)}, /*index=5*/s32[]{:T(128)}, s32[]{:T(128)}, s32[]{:T(128)}, s32[]{:T(128)}) while((s32[]{:T(128)}, f32[2,256,256]{1,0,2:T(2,128)S(1)}, f32[2,256,256]{1,0,2:T(2,128)S(1)}, s32[]{:T(128)}, ...), condition=%wide.region_4.8_spmd.clone.clone, body=%wide.region_1.7_spmd.clone.clone.sunk | while | flops 3160845 | bytes 17895540 | solution.py:67
  245.0 3.2 fusion.351
  260.3 3.2 fusion.351
  275.6 3.2 fusion.351
  290.9 3.2 fusion.351
  306.2 3.2 fusion.351
  321.4 3.2 fusion.351
  336.7 3.2 fusion.351
  352.0 3.2 fusion.351
  370.2 3.8 collective-permute-done
  374.0 5.6 collective-permute-done.1
  383.8 221.2 %all-reduce.7.cloned.1.call-done = f32[2,256,256]{2,1,0:T(8,128)} async-done(((f32[2,256,256]{2,1,0:T(8,128)}), f32[2,256,256]{2,1,0:T(8,128)}) %all-reduce.7.cloned.1.call-update) | async-done | bytes 524304 | tf_op jit(solution)/shard_map/psum | solution.py:111
  607.9 121.3 %while.100 = (s32[]{:T(128)}, f32[2,256,256]{1,0,2:T(2,128)S(1)}, f32[2,256,256]{1,0,2:T(2,128)S(1)}, s32[]{:T(128)}, s32[1]{0:T(128)}, /*index=5*/s32[]{:T(128)}, s32[]{:T(128)}, s32[]{:T(128)}, s32[]{:T(128)}) while((s32[]{:T(128)}, f32[2,256,256]{1,0,2:T(2,128)S(1)}, f32[2,256,256]{1,0,2:T(2,128)S(1)}, s32[]{:T(128)}, ...), condition=%wide.region_9.13_spmd.clone.clone, body=%wide.region_6.12_spmd.clone.clone.sunk | while | flops 3160845 | bytes 17895540 | solution.py:67
  611.3 3.2 fusion.361
  626.5 3.2 fusion.361
  641.6 3.2 fusion.361
  656.8 3.2 fusion.361
  672.0 3.2 fusion.361
  687.1 3.2 fusion.361
  702.3 3.2 fusion.361
  717.5 3.2 fusion.361
  733.9 2.5 collective-permute-start.2
  736.5 3.8 collective-permute-done.2
  740.3 5.6 collective-permute-done.3
  750.0 221.3 %all-reduce.9.cloned.1.call-done = f32[2,256,256]{2,1,0:T(8,128)} async-done(((f32[2,256,256]{2,1,0:T(8,128)}), f32[2,256,256]{2,1,0:T(8,128)}) %all-reduce.9.cloned.1.call-update) | async-done | bytes 524304 | tf_op jit(solution)/shard_map/psum | solution.py:111
  974.1 121.3 %while.101 = (s32[]{:T(128)}, f32[2,256,256]{1,0,2:T(2,128)S(1)}, f32[2,256,256]{1,0,2:T(2,128)S(1)}, s32[]{:T(128)}, s32[1]{0:T(128)}, /*index=5*/s32[]{:T(128)}, s32[]{:T(128)}, s32[]{:T(128)}, s32[]{:T(128)}) while((s32[]{:T(128)}, f32[2,256,256]{1,0,2:T(2,128)S(1)}, f32[2,256,256]{1,0,2:T(2,128)S(1)}, ...), condition=%wide.region_14.18_spmd.clone.clone, body=%wide.region_11.17_spmd.clone.clone.sunk | while | flops 3160845 | bytes 17895540 | solution.py:67
  977.6 3.2 fusion.371
  992.7 3.2 fusion.371
  1007.9 3.2 fusion.371
  1023.1 3.2 fusion.371
  1038.2 3.2 fusion.371
  1053.4 3.2 fusion.371
  1068.6 3.2 fusion.371
  1083.7 3.2 fusion.371
  1100.2 2.7 collective-permute-start.4
  1103.0 3.8 collective-permute-done.4
  1106.8 5.6 collective-permute-done.5
  1116.2 221.6 %all-reduce.11.cloned.1.call-done = f32[2,256,256]{2,1,0:T(8,128)} async-done(((f32[2,256,256]{2,1,0:T(8,128)}), f32[2,256,256]{2,1,0:T(8,128)}) %all-reduce.11.cloned.1.call-update) | async-done | bytes 524304 | tf_op jit(solution)/shard_map/psum | solution.py:111
  1340.6 121.3 %while.102 = (s32[]{:T(128)}, f32[2,256,256]{1,0,2:T(2,128)S(1)}, f32[2,256,256]{1,0,2:T(2,128)S(1)}, s32[]{:T(128)}, s32[1]{0:T(128)}, /*index=5*/s32[]{:T(128)}, s32[]{:T(128)}, s32[]{:T(128)}, s32[]{:T(128)}) while((s32[]{:T(128)}, f32[2,256,256]{1,0,2:T(2,128)S(1)}, f32[2,256,256]{1,0,2:T(2,128)S(1)}, ...), condition=%wide.region_19.23_spmd.clone.clone, body=%wide.region_16.22_spmd.clone.clone.sunk | while | flops 3160845 | bytes 17895540 | solution.py:67
  1344.3 3.2 fusion.381
  1359.4 3.2 fusion.381
  1374.6 3.2 fusion.381
  1389.7 3.2 fusion.381
  1404.8 3.2 fusion.381
  1420.0 3.2 fusion.381
  1435.1 3.2 fusion.381
  1450.3 3.2 fusion.381
  (1362 shorter events, 427.5 us)
Async XLA Ops:
  7.2 231.6 %all-reduce.5.cloned.1.call-start = ((), (), s32[]{:S(2)}) async-start(), calls=%async_computation | async-start | bytes 1048576 | tf_op jit(solution)/shard_map/psum | solution.py:111
  11.1 594.0 %all-reduce.7.cloned.1.call-start = ((), (), s32[]{:S(2)}) async-start(), calls=%async_computation.1 | async-start | bytes 1048576 | tf_op jit(solution)/shard_map/psum | solution.py:111
  249.1 1.3 copy-start
  264.3 1.3 copy-start
  279.6 1.3 copy-start
  294.9 1.3 copy-start
  310.2 1.3 copy-start
  325.5 1.3 copy-start
  340.8 1.3 copy-start
  356.0 1.3 copy-start
  367.6 12.1 copy-start.20
  367.6 12.1 copy-start.22
  367.6 6.4 collective-permute-start
  370.1 9.5 collective-permute-start.1
  382.2 589.1 %all-reduce.9.cloned.1.call-start = ((), (), s32[]{:S(2)}) async-start(), calls=%async_computation.2 | async-start | bytes 1048576 | tf_op jit(solution)/shard_map/psum | solution.py:111
  615.3 1.3 copy-start.1
  630.4 1.3 copy-start.1
  645.6 1.3 copy-start.1
  660.8 1.3 copy-start.1
  675.9 1.3 copy-start.1
  691.1 1.3 copy-start.1
  706.3 1.3 copy-start.1
  721.4 1.3 copy-start.1
  731.8 14.1 copy-start.16
  731.9 14.1 copy-start.18
  733.9 6.4 collective-permute-start.2
  736.4 9.5 collective-permute-start.3
  748.5 589.3 %all-reduce.11.cloned.1.call-start = ((), (), s32[]{:S(2)}) async-start(), calls=%async_computation.3 | async-start | bytes 1048576 | tf_op jit(solution)/shard_map/psum | solution.py:111
  981.5 1.3 copy-start.2
  996.7 1.3 copy-start.2
  1011.9 1.3 copy-start.2
  1027.0 1.3 copy-start.2
  1042.2 1.3 copy-start.2
  1057.4 1.3 copy-start.2
  1072.5 1.3 copy-start.2
  1087.7 1.3 copy-start.2
  1098.1 14.3 copy-start.12
  1098.1 14.3 copy-start.14
  1100.2 6.6 collective-permute-start.4
  1102.9 9.5 collective-permute-start.5
  1348.3 1.3 copy-start.3
  1363.4 1.3 copy-start.3
  1378.5 1.3 copy-start.3
  1393.7 1.3 copy-start.3
  1408.8 1.3 copy-start.3
  1423.9 1.3 copy-start.3
  1439.1 1.3 copy-start.3
  1454.2 1.3 copy-start.3
  (27 other events, 24.7 us)
Sparse Core Ops, SparseCore 0:
  11.2 227.5 all-reduce.4
  382.3 222.6 all-reduce.6
  748.6 222.6 all-reduce.8
  1115.1 222.6 all-reduce.10
where the time goes:
time: 1490 us; the launch traced here: 1470 us
  waiting for transfers between devices  919 us (62%)
  other arithmetic  253 us (17%)
  local copies, waits for them, and re-layouts  244 us (16%)
  matrix products  28.5 us (2%)
  between operations  15 us (1%)
    psum x4, waiting for transfers between devices, body(): lax.psum(jnp.einsum('rpi,rpj->pij', joined, joined, precision=lax.Precisi...  891 us
    select_n x96, other arithmetic, partner_take(): rolled = jnp.where(marker, last, rolled)  152 us
    while x256, local copies, waits for them, and re-layouts  79.1 us
    broadcast_in_dim x128, local copies, waits for them, and re-layouts, partner_take(): rolled = jnp.where(marker, last, rolled)  46.7 us
    add x32, other arithmetic, round_fn(): q = c[None, :] * q + s_col[None, :] * partner_take(q, r, 1)  45.8 us
  transfers between devices with their start and end apart: 10, of which 10 were waited for; matrix products, arithmetic and copies ran while one was open for 0% of the time, Pallas kernels for 0%

commit v1 on v0

v1 whole, which is shorter than its diff:
```python
import functools

import jax
import jax.numpy as jnp
import numpy as np
from jax import lax
from jax.experimental import pallas as pl
from jax.experimental.pallas import tpu as pltpu
from jax.sharding import PartitionSpec as P

BLOCK = 128
N = 2 * BLOCK
W = 4096
STEPS = 4
ROUNDS = 8
HIGHEST = lax.Precision.HIGHEST


def arrangement(r):
    m = N - 1
    first = [m] + [(r + i) % m for i in range(1, BLOCK)]
    second = [r % m] + [(r - i) % m for i in range(1, BLOCK)]
    return np.array(first + second)


def exact_dot(left, right):
    return jnp.dot(left, right, precision=HIGHEST, preferred_element_type=jnp.float32)


def turn(p, q, c, s):
    return c * p - s * q, s * p + c * q


def advance(p, q, axis):
    at = lax.broadcasted_iota(jnp.int32, p.shape, axis)
    p_back = pltpu.roll(p, BLOCK - 1, axis)
    q_on = pltpu.roll(q, 1, axis)
    new_p = jnp.where(at == 0, p, jnp.where(at == BLOCK - 1, q, p_back))
    new_q = jnp.where(at == 0, p_back, q_on)
    return new_p, new_q


def solve_kernel(g00, g01, g11, rows_ref, cols_ref, x0, x1, y0, y1, q_out, a, b, c_, d_, qp, qq):
    lane = lax.broadcasted_iota(jnp.int32, (N, N), 1).astype(jnp.float32)
    sub = lax.broadcasted_iota(jnp.int32, (N, N), 0).astype(jnp.float32)
    take = jnp.where(sub == rows_ref[0:1, :], 1.0, 0.0).astype(jnp.float32)
    take_t = jnp.where(lane == cols_ref[:, 0:1], 1.0, 0.0).astype(jnp.float32)
    back_t = jnp.where(lane == cols_ref[:, 1:2], 1.0, 0.0).astype(jnp.float32)
    cross = g01[...]
    gram = jnp.concatenate(
        [
            jnp.concatenate([g00[...], cross], axis=1),
            jnp.concatenate([cross.T, g11[...]], axis=1),
        ],
        axis=0,
    )
    placed = exact_dot(take_t, exact_dot(gram, take))
    a[...] = placed[:BLOCK, :BLOCK]
    b[...] = placed[:BLOCK, BLOCK:]
    c_[...] = placed[BLOCK:, :BLOCK]
    d_[...] = placed[BLOCK:, BLOCK:]
    qp[...] = take[:, :BLOCK]
    qq[...] = take[:, BLOCK:]
    i0 = lax.broadcasted_iota(jnp.int32, (BLOCK, BLOCK), 0)
    i1 = lax.broadcasted_iota(jnp.int32, (BLOCK, BLOCK), 1)

    def round_fn(r, carry):
        on = i0 == i1
        ga, gb, gc, gd = a[...], b[...], c_[...], d_[...]

        def diagonal(m):
            return jnp.sum(jnp.where(on, m, 0.0), axis=0, keepdims=True)

        gpp, cr, gqq = diagonal(ga), diagonal(gb), diagonal(gd)
        d = gqq - gpp
        root = jnp.sqrt(d * d + 4.0 * cr * cr)
        t = 2.0 * cr * d / ((jnp.abs(d) + root) * root + 1e-06 * (gpp + gqq) * (gpp + gqq))
        c = 1.0 / jnp.sqrt(1.0 + t * t)
        s = t * c
        c_col = jnp.sum(jnp.where(on, c, 0.0), axis=1, keepdims=True)
        s_col = jnp.sum(jnp.where(on, s, 0.0), axis=1, keepdims=True)
        ga, gb = advance(*turn(ga, gb, c, s), 1)
        gc, gd = advance(*turn(gc, gd, c, s), 1)
        ga, gc = advance(*turn(ga, gc, c_col, s_col), 0)
        gb, gd = advance(*turn(gb, gd, c_col, s_col), 0)
        a[...], b[...], c_[...], d_[...] = ga, gb, gc, gd
        qp[...], qq[...] = advance(*turn(qp[...], qq[...], c, s), 1)
        return carry

    lax.fori_loop(0, ROUNDS, round_fn, 0)
    q = exact_dot(jnp.concatenate([qp[...], qq[...]], axis=1), back_t)
    q_out[...] = q
    x = jnp.concatenate([x0[...], x1[...]], axis=1)
    y = exact_dot(x, q)
    y0[...] = y[:, :BLOCK]
    y1[...] = y[:, BLOCK:]


def solve(g00, g01, g11, rows, cols, x0, x1):
    half = jax.ShapeDtypeStruct(x0.shape, jnp.float32)
    block = pltpu.VMEM((BLOCK, BLOCK), jnp.float32)
    tall = pltpu.VMEM((N, BLOCK), jnp.float32)
    vmem = pl.BlockSpec(memory_space=pltpu.VMEM)
    return pl.pallas_call(
        solve_kernel,
        out_shape=(half, half, jax.ShapeDtypeStruct((N, N), jnp.float32)),
        in_specs=[vmem] * 7,
        out_specs=(vmem,) * 3,
        scratch_shapes=[block] * 4 + [tall] * 2,
        compiler_params=pltpu.CompilerParams(vmem_limit_bytes=32 * 2**20),
    )(g00, g01, g11, rows, cols, x0, x1)


def chip_groups(size):
    return [list(range(core, size, 2)) for core in range(2)]


def sum_over_chips(part):
    groups = chip_groups(lax.axis_size("rows"))
    n = len(groups[0])
    slices = part.reshape(n, -1, BLOCK)
    mine = lax.all_to_all(slices, "rows", 0, 0, axis_index_groups=groups).sum(0)
    spread = jnp.broadcast_to(mine[None], (n,) + mine.shape)
    whole = lax.all_to_all(spread, "rows", 0, 0, axis_index_groups=groups)
    return whole.reshape(part.shape)


def other_core(x):
    return lax.ppermute(x, "rows", [(i, i ^ 1) for i in range(lax.axis_size("rows"))])


def along_pairs(x, sign):
    n_rows, n_pairs = lax.axis_size("rows"), lax.axis_size("pairs")
    route = []
    for r in range(n_rows):
        step = sign if r % 2 else -sign
        for p in range(n_pairs):
            route.append((r * n_pairs + p, r * n_pairs + (p + step) % n_pairs))
    return lax.ppermute(x, ("rows", "pairs"), route)


def body(sample, column_scale, inner_order):
    row, col = lax.axis_index("rows"), lax.axis_index("pairs")
    core = row % 2
    first = core == 0
    data = sample * column_scale[None, :]
    rows = data.shape[0]
    left, right = data[:, :N], data[:, N:]
    own = jnp.where(first, left, right)
    joined = jnp.concatenate([own, other_core(jnp.where(first, right, left))], axis=0)
    height = W // lax.axis_size("rows")
    ids = jnp.arange(height, dtype=jnp.int32)
    row_ids = jnp.concatenate([ids + row * height, ids + (row ^ 1) * height])[:, None]
    col_ids = jnp.arange(BLOCK, dtype=jnp.int32)[None, :] + (2 * col + core) * N
    shift = core * BLOCK
    x0 = jnp.concatenate(
        [
            jnp.where(first, joined[:, :BLOCK], joined[:, BLOCK:]),
            jnp.where(row_ids == col_ids + shift, 1.0, 0.0).astype(jnp.float32),
        ]
    )
    x1 = jnp.concatenate(
        [
            jnp.where(first, joined[:, BLOCK:], joined[:, :BLOCK]),
            jnp.where(row_ids == col_ids + (BLOCK - shift), 1.0, 0.0).astype(jnp.float32),
        ]
    )
    order = ((inner_order + shift) % N).astype(jnp.float32)
    table = np.concatenate([np.eye(N)[:, arrangement(0)], np.eye(N)[:, arrangement(ROUNDS)]], 1)
    table = jnp.asarray(table.astype(np.float32))
    along = exact_dot(order, table).reshape(STEPS, 2, N)
    down = lax.dot_general(
        table, order, (((0,), (1,)), ((), ())), precision=HIGHEST
    ).reshape(2, N, STEPS)
    data_rows = 2 * rows
    for step in range(STEPS):
        d0, d1 = x0[:data_rows], x1[:data_rows]
        dot_t = functools.partial(
            lax.dot_general, dimension_numbers=(((0,), (0,)), ((), ())), precision=HIGHEST
        )
        if step == 0:
            sums = sum_over_chips(jnp.concatenate([dot_t(d0, d0), dot_t(d0, d1), dot_t(d1, d1)]))
            g00, g01, g11 = sums[:BLOCK], sums[BLOCK : 2 * BLOCK], sums[2 * BLOCK :]
        else:
            g01 = sum_over_chips(dot_t(d0, d1))
        y0, y1, q = solve(g00, g01, g11, along[step], down[:, :, step].T, x0, x1)
        x0, x1 = y0, y1
        if step == STEPS - 1:
            break
        gram = jnp.concatenate(
            [jnp.concatenate([g00, g01], 1), jnp.concatenate([g01.T, g11], 1)], 0
        )
        half = exact_dot(gram, q)
        g00 = dot_t(q[:, :BLOCK], half[:, :BLOCK])
        g11 = dot_t(q[:, BLOCK:], half[:, BLOCK:])
        if step % 2 == 0:
            x1 = jnp.concatenate(
                [along_pairs(x1[:data_rows], 1), along_pairs(x1[data_rows:], 1)]
            )
            g11 = along_pairs(g11, 1)
        else:
            x0 = jnp.concatenate(
                [along_pairs(x0[:data_rows], -1), along_pairs(x0[data_rows:], -1)]
            )
            g00 = along_pairs(g00, -1)
    mine0 = jnp.concatenate([x0[:rows], x0[data_rows : data_rows + height]])
    mine1 = jnp.concatenate([x1[:rows], x1[data_rows : data_rows + height]])
    theirs = jnp.concatenate(
        [x0[rows:data_rows], x0[data_rows + height :], x1[rows:data_rows], x1[data_rows + height :]]
    )
    got = other_core(theirs)
    got0, got1 = got[: rows + height], got[rows + height :]
    whole = jnp.where(
        first,
        jnp.concatenate([got1, got0, mine0, mine1], 1),
        jnp.concatenate([mine1, mine0, got0, got1], 1),
    )
    return whole[:rows], whole[rows:]


def solution(mesh):
    return jax.shard_map(
        body,
        mesh=mesh,
        in_specs=(P("rows", "pairs"), P("pairs"), P()),
        out_specs=(P("rows", "pairs"), P("rows", "pairs")),
        check_vma=False,
    )
```

time: 1490 us -> 179 us (0.12)
  waiting for transfers between devices: 919 us -> 65 us
  other arithmetic: 253 us -> 2.29 us
  local copies, waits for them, and re-layouts: 244 us -> 6.8 us
  starting transfers between devices: 8.64 us -> 73 us
  Pallas kernels: 0 us -> 20.7 us
  matrix products: 28.5 us -> 9.47 us
    psum x4 -> x0, waiting for transfers between devices: 891 us -> none  [body(): lax.psum(jnp.einsum('rpi,rpj->pij', joined, joined, precision=lax.Precisi...]
    select_n x161 -> x4, other arithmetic: 153 us -> 0.24 us  [the longest x1 0.1 us: body(): jnp.where(row_ids == col_ids + (BLOCK - shift), 1.0, 0.0)]
    while x288 -> x0, local copies, waits for them, and re-layouts: 97.8 us -> none
    add x66 -> x4, other arithmetic: 63.1 us -> 0.02 us  [the longest x1 0.01 us: body(): col_ids + (BLOCK - shift)]
    all_to_all x0 -> x8, waiting for transfers between devices: none -> 49.1 us  [the longest x4 32.1 us: sum_over_chips(): mine = lax.all_to_all(slices, 'rows', 0, 0, axis_index_groups=groups).sum(0)]
    broadcast_in_dim x132 -> x4, local copies, waits for them, and re-layouts: 47.4 us -> 2.6 us  [sum_over_chips(): spread = jnp.broadcast_to(mine[None], (n,) + mine.shape)]
    all_to_all x0 -> x8, starting transfers between devices: none -> 36.7 us  [the longest x4 22.7 us: sum_over_chips(): mine = lax.all_to_all(slices, 'rows', 0, 0, axis_index_groups=groups).sum(0)]
    slice x132 -> x15, local copies, waits for them, and re-layouts: 38 us -> 1.77 us  [the longest x2 1.55 us: body(): return (whole[:rows], whole[rows:])]
  transfers between devices with their start and end apart: 10 -> 19, of which waited for: 10 -> 14; matrix products, arithmetic and copies ran while one was open for 0% -> 6% of each run, Pallas kernels for 0% -> 0%
where the time goes in v1:
time: 179 us; the launch traced here: 178 us
  starting transfers between devices  73 us (41%)
  waiting for transfers between devices  65 us (36%)
  Pallas kernels  20.7 us (12%)
  matrix products  9.47 us (5%)
  local copies, waits for them, and re-layouts  6.8 us (4%)
  other arithmetic  2.29 us (1%)
    all_to_all x4, waiting for transfers between devices, sum_over_chips(): mine = lax.all_to_all(slices, 'rows', 0, 0, axis_index_groups=groups).sum(0)  32.1 us
    all_to_all x4, starting transfers between devices, sum_over_chips(): mine = lax.all_to_all(slices, 'rows', 0, 0, axis_index_groups=groups).sum(0)  22.7 us
    pallas_call x4, Pallas kernels, solve(): pl.pallas_call(solve_kernel, out_shape=(half, half, jax.ShapeDtypeStruct(...  20.7 us
    ppermute x9, starting transfers between devices, along_pairs(): return lax.ppermute(x, ('rows', 'pairs'), route)  18.3 us
    ppermute x2, starting transfers between devices, other_core(): lax.ppermute(x, 'rows', [(i, i ^ 1) for i in range(lax.axis_size('rows'))])  18 us
    all_to_all x4, waiting for transfers between devices, sum_over_chips(): whole = lax.all_to_all(spread, 'rows', 0, 0, axis_index_groups=groups)  17 us
    ppermute x9, waiting for transfers between devices, along_pairs(): return lax.ppermute(x, ('rows', 'pairs'), route)  14.5 us
    all_to_all x4, starting transfers between devices, sum_over_chips(): whole = lax.all_to_all(spread, 'rows', 0, 0, axis_index_groups=groups)  14 us
  transfers between devices with their start and end apart: 19, of which 14 were waited for; matrix products, arithmetic and copies ran while one was open for 6% of the time, Pallas kernels for 0%

profile of v1, /device:TPU:7, one launch (start us, length us, event | category | flops | bytes accessed | tf_op | source)
XLA Modules:
  0.0 178.4 jit_solution(5411924996109709192)
XLA Ops:
  0.7 0.7 copy-done.2
  1.3 1.1 broadcast_multiply_fusion
  2.5 0.8 collective-permute-start
  4.5 0.6 fusion.68
  5.0 0.6 fusion.69
  5.6 0.6 fusion.70
  6.2 0.7 pad_maximum_fusion.7
  6.9 9.3 %all-to-all-start = ((f32[16,24,128]{2,1,0:T(8,128)}), f32[16,24,128]{2,1,0:T(8,128)S(1)}, u32[]{:S(2)}, u32[]{:S(2)}) async-start(f32[16,24,128]{2,1,0:T(8,128)} %bitcast), calls=%async_computation | async-start | bytes 393216 | tf_op jit(solution)/shard_map/all_to_all | solution.py:122
  16.3 9.6 %all-to-all-done = f32[16,24,128]{2,1,0:T(8,128)S(1)} async-done(((f32[16,24,128]{2,1,0:T(8,128)}), f32[16,24,128]{2,1,0:T(8,128)S(1)}, u32[]{:S(2)}, u32[]{:S(2)}) %all-to-all-start) | async-done | bytes 196640 | tf_op jit(solution)/shard_map/all_to_all | solution.py:122
  25.9 0.7 broadcast_in_dim.18
  26.6 3.5 %all-to-all-start.1 = ((f32[16,24,128]{2,1,0:T(8,128)}), f32[16,24,128]{2,1,0:T(8,128)S(1)}, u32[]{:S(2)}, u32[]{:S(2)}) async-start(f32[16,24,128]{2,1,0:T(8,128)} %broadcast_in_dim.18), calls=%async_computation.1 | async-start | bytes 393216 | tf_op jit(solution)/shard_map/all_to_all | solution.py:124
  30.5 8.7 %all-to-all-done.1 = f32[16,24,128]{2,1,0:T(8,128)S(1)} async-done(((f32[16,24,128]{2,1,0:T(8,128)}), f32[16,24,128]{2,1,0:T(8,128)S(1)}, u32[]{:S(2)}, u32[]{:S(2)}) %all-to-all-start.1) | async-done | bytes 196640 | tf_op jit(solution)/shard_map/all_to_all | solution.py:124
  39.2 5.2 %shard_map.59 = (f32[768,128]{1,0:T(8,128)S(1)}, f32[768,128]{1,0:T(8,128)S(1)}, f32[256,256]{1,0:T(8,128)S(1)}) custom-call(f32[128,128]{1,0:T(8,128)S(1)} %get-tuple-element.45.g00, f32[128,128]{1,0:T(8,128)S(1)} %get-tuple-element.44.g01, f32[128,128]{1,0:T(8,128)S(1)} %get-tuple-element.43.g11, f32[2,256]{1,0:T(2,128)S(1)} %squeeze.24.rows_ref, ...), custom_call_target="tpu_custom_call" | custom-call | tf_op jit(solution)/shard_map/pallas_call | solution.py:104
  44.4 2.6 %collective-permute-start.1 = (f32[512,128]{1,0:T(8,128)S(1)}, f32[512,128]{1,0:T(8,128)S(1)}, u32[]{:S(2)}, u32[]{:S(2)}) collective-permute-start(f32[512,128]{1,0:T(8,128)S(1)} %slice.162), channel_id=1, source_target_pairs={{0,7},{1,0},{2,1},{3,2},{4,3},{5,4},{6,5},{7,6},{8,9},{9,10},{10,1... | collective-permute-start | bytes 786440 | tf_op jit(solution)/shard_map/ppermute | solution.py:139
  47.2 1.3 collective-permute-start.3
  49.0 1.4 collective-permute-done.1
  50.3 1.2 convolution_bitcast_fusion.2
  51.6 3.5 %all-to-all-start.2 = ((f32[16,8,128]{2,1,0:T(8,128)}), f32[16,8,128]{2,1,0:T(8,128)S(1)}, u32[]{:S(2)}, u32[]{:S(2)}) async-start(f32[16,8,128]{2,1,0:T(8,128)} %convolution_bitcast_fusion.2), calls=%async_computation.2 | async-start | bytes 131072 | tf_op jit(solution)/shard_map/all_to_all | solution.py:122
  55.5 7.5 %all-to-all-done.2 = f32[16,8,128]{2,1,0:T(8,128)S(1)} async-done(((f32[16,8,128]{2,1,0:T(8,128)}), f32[16,8,128]{2,1,0:T(8,128)S(1)}, u32[]{:S(2)}, u32[]{:S(2)}) %all-to-all-start.2) | async-done | bytes 65568 | tf_op jit(solution)/shard_map/all_to_all | solution.py:122
  63.0 0.6 broadcast_in_dim.21
  63.6 3.5 %all-to-all-start.3 = ((f32[16,8,128]{2,1,0:T(8,128)}), f32[16,8,128]{2,1,0:T(8,128)S(1)}, u32[]{:S(2)}, u32[]{:S(2)}) async-start(f32[16,8,128]{2,1,0:T(8,128)} %broadcast_in_dim.21), calls=%async_computation.3 | async-start | bytes 131072 | tf_op jit(solution)/shard_map/all_to_all | solution.py:124
  67.5 5.8 %collective-permute-start.2 = (f32[128,128]{1,0:T(8,128)S(1)}, f32[128,128]{1,0:T(8,128)S(1)}, u32[]{:S(2)}, u32[]{:S(2)}) collective-permute-start(f32[128,128]{1,0:T(8,128)S(1)} %fusion.36), channel_id=1, source_target_pairs={{0,7},{1,0},{2,1},{3,2},{4,3},{5,4},{6,5},{7,6},{8,9},{9,10},{10,1... | collective-permute-start | bytes 196616 | tf_op jit(solution)/shard_map/ppermute | solution.py:139
  73.3 1.3 collective-permute-done.2.g11
  75.1 5.2 %shard_map.60 = (f32[768,128]{1,0:T(8,128)S(1)}, f32[768,128]{1,0:T(8,128)S(1)}, f32[256,256]{1,0:T(8,128)S(1)}) custom-call(f32[128,128]{1,0:T(8,128)S(1)} %fusion.38.g00, f32[128,128]{1,0:T(8,128)S(1)} %bitcast.48, f32[128,128]{1,0:T(8,128)S(1)} %collective-permute-done.2.g11, f32[2,256]{1,0:T(2,128)S(1)} %squeeze.26.rows_ref, f32[256,2]{1,0:T(8,128)S(1)} %bitcast.51, ...), custom_call_target="tpu_custom_call" | custom-call | tf_op jit(solution)/shard_map/pallas_call | solution.py:104
  81.3 8.4 %collective-permute-done.5 = f32[512,128]{1,0:T(8,128)S(1)} collective-permute-done((f32[512,128]{1,0:T(8,128)S(1)}, f32[512,128]{1,0:T(8,128)S(1)}, u32[]{:S(2)}, u32[]{:S(2)}) %collective-permute-start.5) | collective-permute-done | bytes 262176 | tf_op jit(solution)/shard_map/ppermute | solution.py:139
  89.6 1.2 convolution_bitcast_fusion.1
  90.9 6.4 %all-to-all-start.4 = ((f32[16,8,128]{2,1,0:T(8,128)}), f32[16,8,128]{2,1,0:T(8,128)S(1)}, u32[]{:S(2)}, u32[]{:S(2)}) async-start(f32[16,8,128]{2,1,0:T(8,128)} %convolution_bitcast_fusion.1), calls=%async_computation.4 | async-start | bytes 131072 | tf_op jit(solution)/shard_map/all_to_all | solution.py:122
  97.7 7.4 %all-to-all-done.4 = f32[16,8,128]{2,1,0:T(8,128)S(1)} async-done(((f32[16,8,128]{2,1,0:T(8,128)}), f32[16,8,128]{2,1,0:T(8,128)S(1)}, u32[]{:S(2)}, u32[]{:S(2)}) %all-to-all-start.4) | async-done | bytes 65568 | tf_op jit(solution)/shard_map/all_to_all | solution.py:122
  105.1 0.6 broadcast_in_dim.22
  105.8 3.5 %all-to-all-start.5 = ((f32[16,8,128]{2,1,0:T(8,128)}), f32[16,8,128]{2,1,0:T(8,128)S(1)}, u32[]{:S(2)}, u32[]{:S(2)}) async-start(f32[16,8,128]{2,1,0:T(8,128)} %broadcast_in_dim.22), calls=%async_computation.5 | async-start | bytes 131072 | tf_op jit(solution)/shard_map/all_to_all | solution.py:124
  109.9 7.3 %all-to-all-done.5 = f32[16,8,128]{2,1,0:T(8,128)S(1)} async-done(((f32[16,8,128]{2,1,0:T(8,128)}), f32[16,8,128]{2,1,0:T(8,128)S(1)}, u32[]{:S(2)}, u32[]{:S(2)}) %all-to-all-start.5) | async-done | bytes 65568 | tf_op jit(solution)/shard_map/all_to_all | solution.py:124
  117.2 5.2 %shard_map.61 = (f32[768,128]{1,0:T(8,128)S(1)}, f32[768,128]{1,0:T(8,128)S(1)}, f32[256,256]{1,0:T(8,128)S(1)}) custom-call(f32[128,128]{1,0:T(8,128)S(1)} %copy.22.g00, f32[128,128]{1,0:T(8,128)S(1)} %bitcast.45, f32[128,128]{1,0:T(8,128)S(1)} %copy.23.g11, f32[2,256]{1,0:T(2,128)S(1)} %squeeze.28.rows_ref, f32[256,2]{1,0:T(8,128)S(1)} %bitcast.52, ...), custom_call_target="tpu_custom_call" | custom-call | tf_op jit(solution)/shard_map/pallas_call | solution.py:104
  122.4 2.4 %collective-permute-start.7 = (f32[512,128]{1,0:T(8,128)S(1)}, f32[512,128]{1,0:T(8,128)S(1)}, u32[]{:S(2)}, u32[]{:S(2)}) collective-permute-start(f32[512,128]{1,0:T(8,128)S(1)} %slice.180), channel_id=1, source_target_pairs={{0,7},{1,0},{2,1},{3,2},{4,3},{5,4},{6,5},{7,6},{8,9},{9,10},{10,1... | collective-permute-start | bytes 786440 | tf_op jit(solution)/shard_map/ppermute | solution.py:139
  125.4 0.6 fusion.17
  126.0 2.1 %collective-permute-done.7 = f32[512,128]{1,0:T(8,128)S(1)} collective-permute-done((f32[512,128]{1,0:T(8,128)S(1)}, f32[512,128]{1,0:T(8,128)S(1)}, u32[]{:S(2)}, u32[]{:S(2)}) %collective-permute-start.7) | collective-permute-done | bytes 262176 | tf_op jit(solution)/shard_map/ppermute | solution.py:139
  128.1 1.2 convolution_bitcast_fusion
  129.3 3.5 %all-to-all-start.6 = ((f32[16,8,128]{2,1,0:T(8,128)}), f32[16,8,128]{2,1,0:T(8,128)S(1)}, u32[]{:S(2)}, u32[]{:S(2)}) async-start(f32[16,8,128]{2,1,0:T(8,128)} %convolution_bitcast_fusion), calls=%async_computation.6 | async-start | bytes 131072 | tf_op jit(solution)/shard_map/all_to_all | solution.py:122
  133.2 7.6 %all-to-all-done.6 = f32[16,8,128]{2,1,0:T(8,128)S(1)} async-done(((f32[16,8,128]{2,1,0:T(8,128)}), f32[16,8,128]{2,1,0:T(8,128)S(1)}, u32[]{:S(2)}, u32[]{:S(2)}) %all-to-all-start.6) | async-done | bytes 65568 | tf_op jit(solution)/shard_map/all_to_all | solution.py:122
  140.9 0.6 broadcast_in_dim.42
  141.5 3.5 %all-to-all-start.7 = ((f32[16,8,128]{2,1,0:T(8,128)}), f32[16,8,128]{2,1,0:T(8,128)S(1)}, u32[]{:S(2)}, u32[]{:S(2)}) async-start(f32[16,8,128]{2,1,0:T(8,128)} %broadcast_in_dim.42), calls=%async_computation.7 | async-start | bytes 131072 | tf_op jit(solution)/shard_map/all_to_all | solution.py:124
  145.4 5.6 %collective-permute-start.8 = (f32[128,128]{1,0:T(8,128)S(1)}, f32[128,128]{1,0:T(8,128)S(1)}, u32[]{:S(2)}, u32[]{:S(2)}) collective-permute-start(f32[128,128]{1,0:T(8,128)S(1)} %fusion.28), channel_id=1, source_target_pairs={{0,7},{1,0},{2,1},{3,2},{4,3},{5,4},{6,5},{7,6},{8,9},{9,10},{10,1... | collective-permute-start | bytes 196616 | tf_op jit(solution)/shard_map/ppermute | solution.py:139
  151.0 1.3 collective-permute-done.8.g11
  152.3 0.6 all-to-all-done.7
  152.9 5.2 %shard_map.62 = (f32[768,128]{1,0:T(8,128)S(1)}, f32[768,128]{1,0:T(8,128)S(1)}, f32[256,256]{1,0:T(8,128)}) custom-call(f32[128,128]{1,0:T(8,128)S(1)} %fusion.30.g00, f32[128,128]{1,0:T(8,128)S(1)} %bitcast.55, f32[128,128]{1,0:T(8,128)S(1)} %collective-permute-done.8.g11, f32[2,256]{1,0:T(2,128)S(1)} %squeeze.30.rows_ref, f32[256,2]{1,0:T(8,128)S(1)} %bitcast.53, ...), custom_call_target="tpu_custom_call" | custom-call | tf_op jit(solution)/shard_map/pallas_call | solution.py:104
  158.2 17.2 %collective-permute-start.10 = (f32[768,128]{1,0:T(8,128)S(1)}, f32[768,128]{1,0:T(8,128)S(1)}, u32[]{:S(2)}, u32[]{:S(2)}) collective-permute-start(f32[768,128]{1,0:T(8,128)S(1)} %pad_maximum_fusion.5), channel_id=1, source_target_pairs={{0,8},{8,0},{16,24},{24,16},{32,40},{40,32},{48,56},{56,48},{64,72... | collective-permute-start | bytes 1179656 | tf_op jit(solution)/shard_map/ppermute | solution.py:129
  175.4 1.3 collective-permute-done.10
  176.9 0.8 slice.221
  177.7 0.7 slice.222
  (69 shorter events, 7.1 us)
Async XLA Ops:
  0.6 0.7 copy-start.2
  2.4 1.0 copy-start
  2.5 1.9 %collective-permute-start = (f32[256,256]{1,0:T(8,128)S(1)}, f32[256,256]{1,0:T(8,128)S(1)}, u32[]{:S(2)}, u32[]{:S(2)}) collective-permute-start(f32[256,256]{1,0:T(8,128)S(1)} %get-tuple-element.31), channel_id=1, source_target_pairs={{0,8},{8,0},{16,24},{24,16},{32,40},{40,32},{48,56},{56,48},{64,72... | collective-permute-start | bytes 786440 | tf_op jit(solution)/shard_map/ppermute | solution.py:129
  3.3 0.7 copy-start.1
  6.9 18.9 %all-to-all-start = ((f32[16,24,128]{2,1,0:T(8,128)}), f32[16,24,128]{2,1,0:T(8,128)S(1)}, u32[]{:S(2)}, u32[]{:S(2)}) async-start(f32[16,24,128]{2,1,0:T(8,128)} %bitcast), calls=%async_computation | async-start | bytes 393216 | tf_op jit(solution)/shard_map/all_to_all | solution.py:122
  26.6 12.6 %all-to-all-start.1 = ((f32[16,24,128]{2,1,0:T(8,128)}), f32[16,24,128]{2,1,0:T(8,128)S(1)}, u32[]{:S(2)}, u32[]{:S(2)}) async-start(f32[16,24,128]{2,1,0:T(8,128)} %broadcast_in_dim.18), calls=%async_computation.1 | async-start | bytes 393216 | tf_op jit(solution)/shard_map/all_to_all | solution.py:124
  44.4 5.9 %collective-permute-start.1 = (f32[512,128]{1,0:T(8,128)S(1)}, f32[512,128]{1,0:T(8,128)S(1)}, u32[]{:S(2)}, u32[]{:S(2)}) collective-permute-start(f32[512,128]{1,0:T(8,128)S(1)} %slice.162), channel_id=1, source_target_pairs={{0,7},{1,0},{2,1},{3,2},{4,3},{5,4},{6,5},{7,6},{8,9},{9,10},{10,1... | collective-permute-start | bytes 786440 | tf_op jit(solution)/shard_map/ppermute | solution.py:139
  47.2 26.1 %collective-permute-start.3 = (f32[256,128]{1,0:T(8,128)S(1)}, f32[256,128]{1,0:T(8,128)S(1)}, u32[]{:S(2)}, u32[]{:S(2)}) collective-permute-start(f32[256,128]{1,0:T(8,128)S(1)} %slice.167), channel_id=1, source_target_pairs={{0,7},{1,0},{2,1},{3,2},{4,3},{5,4},{6,5},{7,6},{8,9},{9,10},{10,1... | collective-permute-start | bytes 393224 | tf_op jit(solution)/shard_map/ppermute | solution.py:139
  51.6 11.4 %all-to-all-start.2 = ((f32[16,8,128]{2,1,0:T(8,128)}), f32[16,8,128]{2,1,0:T(8,128)S(1)}, u32[]{:S(2)}, u32[]{:S(2)}) async-start(f32[16,8,128]{2,1,0:T(8,128)} %convolution_bitcast_fusion.2), calls=%async_computation.2 | async-start | bytes 131072 | tf_op jit(solution)/shard_map/all_to_all | solution.py:122
  63.6 11.4 %all-to-all-start.3 = ((f32[16,8,128]{2,1,0:T(8,128)}), f32[16,8,128]{2,1,0:T(8,128)S(1)}, u32[]{:S(2)}, u32[]{:S(2)}) async-start(f32[16,8,128]{2,1,0:T(8,128)} %broadcast_in_dim.21), calls=%async_computation.3 | async-start | bytes 131072 | tf_op jit(solution)/shard_map/all_to_all | solution.py:124
  67.5 7.1 %collective-permute-start.2 = (f32[128,128]{1,0:T(8,128)S(1)}, f32[128,128]{1,0:T(8,128)S(1)}, u32[]{:S(2)}, u32[]{:S(2)}) collective-permute-start(f32[128,128]{1,0:T(8,128)S(1)} %fusion.36), channel_id=1, source_target_pairs={{0,7},{1,0},{2,1},{3,2},{4,3},{5,4},{6,5},{7,6},{8,9},{9,10},{10,1... | collective-permute-start | bytes 196616 | tf_op jit(solution)/shard_map/ppermute | solution.py:139
  80.3 9.4 %collective-permute-start.5 = (f32[512,128]{1,0:T(8,128)S(1)}, f32[512,128]{1,0:T(8,128)S(1)}, u32[]{:S(2)}, u32[]{:S(2)}) collective-permute-start(f32[512,128]{1,0:T(8,128)S(1)} %slice.170), channel_id=1, source_target_pairs={{0,1},{1,2},{2,3},{3,4},{4,5},{5,6},{6,7},{7,0},{8,15},{9,8},{10,9... | collective-permute-start | bytes 786440 | tf_op jit(solution)/shard_map/ppermute | solution.py:139
  80.5 29.3 %collective-permute-start.6 = (f32[256,128]{1,0:T(8,128)S(1)}, f32[256,128]{1,0:T(8,128)S(1)}, u32[]{:S(2)}, u32[]{:S(2)}) collective-permute-start(f32[256,128]{1,0:T(8,128)S(1)} %slice.176), channel_id=1, source_target_pairs={{0,1},{1,2},{2,3},{3,4},{4,5},{5,6},{6,7},{7,0},{8,15},{9,8},{10,9... | collective-permute-start | bytes 393224 | tf_op jit(solution)/shard_map/ppermute | solution.py:139
  90.9 14.3 %all-to-all-start.4 = ((f32[16,8,128]{2,1,0:T(8,128)}), f32[16,8,128]{2,1,0:T(8,128)S(1)}, u32[]{:S(2)}, u32[]{:S(2)}) async-start(f32[16,8,128]{2,1,0:T(8,128)} %convolution_bitcast_fusion.1), calls=%async_computation.4 | async-start | bytes 131072 | tf_op jit(solution)/shard_map/all_to_all | solution.py:122
  97.6 12.2 %collective-permute-start.4 = (f32[128,128]{0,1:T(8,128)S(1)}, f32[128,128]{0,1:T(8,128)S(1)}, u32[]{:S(2)}, u32[]{:S(2)}) collective-permute-start(f32[128,128]{0,1:T(8,128)S(1)} %fusion.34), channel_id=1, source_target_pairs={{0,1},{1,2},{2,3},{3,4},{4,5},{5,6},{6,7},{7,0},{8,15},{9,8},{10,9... | collective-permute-start | bytes 196616 | tf_op jit(solution)/shard_map/ppermute | solution.py:139
  105.8 11.4 %all-to-all-start.5 = ((f32[16,8,128]{2,1,0:T(8,128)}), f32[16,8,128]{2,1,0:T(8,128)S(1)}, u32[]{:S(2)}, u32[]{:S(2)}) async-start(f32[16,8,128]{2,1,0:T(8,128)} %broadcast_in_dim.22), calls=%async_computation.5 | async-start | bytes 131072 | tf_op jit(solution)/shard_map/all_to_all | solution.py:124
  122.4 5.7 %collective-permute-start.7 = (f32[512,128]{1,0:T(8,128)S(1)}, f32[512,128]{1,0:T(8,128)S(1)}, u32[]{:S(2)}, u32[]{:S(2)}) collective-permute-start(f32[512,128]{1,0:T(8,128)S(1)} %slice.180), channel_id=1, source_target_pairs={{0,7},{1,0},{2,1},{3,2},{4,3},{5,4},{6,5},{7,6},{8,9},{9,10},{10,1... | collective-permute-start | bytes 786440 | tf_op jit(solution)/shard_map/ppermute | solution.py:139
  125.1 25.9 %collective-permute-start.9 = (f32[256,128]{1,0:T(8,128)S(1)}, f32[256,128]{1,0:T(8,128)S(1)}, u32[]{:S(2)}, u32[]{:S(2)}) collective-permute-start(f32[256,128]{1,0:T(8,128)S(1)} %slice.185), channel_id=1, source_target_pairs={{0,7},{1,0},{2,1},{3,2},{4,3},{5,4},{6,5},{7,6},{8,9},{9,10},{10,1... | collective-permute-start | bytes 393224 | tf_op jit(solution)/shard_map/ppermute | solution.py:139
  129.3 11.5 %all-to-all-start.6 = ((f32[16,8,128]{2,1,0:T(8,128)}), f32[16,8,128]{2,1,0:T(8,128)S(1)}, u32[]{:S(2)}, u32[]{:S(2)}) async-start(f32[16,8,128]{2,1,0:T(8,128)} %convolution_bitcast_fusion), calls=%async_computation.6 | async-start | bytes 131072 | tf_op jit(solution)/shard_map/all_to_all | solution.py:122
  141.5 11.4 %all-to-all-start.7 = ((f32[16,8,128]{2,1,0:T(8,128)}), f32[16,8,128]{2,1,0:T(8,128)S(1)}, u32[]{:S(2)}, u32[]{:S(2)}) async-start(f32[16,8,128]{2,1,0:T(8,128)} %broadcast_in_dim.42), calls=%async_computation.7 | async-start | bytes 131072 | tf_op jit(solution)/shard_map/all_to_all | solution.py:124
  145.4 6.9 %collective-permute-start.8 = (f32[128,128]{1,0:T(8,128)S(1)}, f32[128,128]{1,0:T(8,128)S(1)}, u32[]{:S(2)}, u32[]{:S(2)}) collective-permute-start(f32[128,128]{1,0:T(8,128)S(1)} %fusion.28), channel_id=1, source_target_pairs={{0,7},{1,0},{2,1},{3,2},{4,3},{5,4},{6,5},{7,6},{8,9},{9,10},{10,1... | collective-permute-start | bytes 196616 | tf_op jit(solution)/shard_map/ppermute | solution.py:139
  158.2 18.6 %collective-permute-start.10 = (f32[768,128]{1,0:T(8,128)S(1)}, f32[768,128]{1,0:T(8,128)S(1)}, u32[]{:S(2)}, u32[]{:S(2)}) collective-permute-start(f32[768,128]{1,0:T(8,128)S(1)} %pad_maximum_fusion.5), channel_id=1, source_target_pairs={{0,8},{8,0},{16,24},{24,16},{32,40},{40,32},{48,56},{56,48},{64,72... | collective-permute-start | bytes 1179656 | tf_op jit(solution)/shard_map/ppermute | solution.py:129

commit v2 on v1

v2 whole, which is shorter than its diff:
```python
import functools

import jax
import jax.numpy as jnp
import numpy as np
from jax import lax
from jax.experimental import pallas as pl
from jax.experimental.pallas import tpu as pltpu
from jax.sharding import PartitionSpec as P

BLOCK = 128
N = 2 * BLOCK
W = 4096
STEPS = 4
ROUNDS = 8
HIGHEST = lax.Precision.HIGHEST
VMEM = pl.BlockSpec(memory_space=pltpu.VMEM)


def arrangement(r):
    m = N - 1
    first = [m] + [(r + i) % m for i in range(1, BLOCK)]
    second = [r % m] + [(r - i) % m for i in range(1, BLOCK)]
    return np.array(first + second)


def shape(*dims):
    return jax.ShapeDtypeStruct(dims, jnp.float32)


def call(kernel, out_shape, scratch, *operands):
    return pl.pallas_call(
        kernel,
        out_shape=out_shape,
        in_specs=[VMEM] * len(operands),
        out_specs=jax.tree.map(lambda _: VMEM, out_shape),
        scratch_shapes=scratch,
        compiler_params=pltpu.CompilerParams(vmem_limit_bytes=40 * 2**20),
    )(*operands)


def solve_scratch(count):
    block = pltpu.VMEM((count, BLOCK, BLOCK), jnp.float32)
    tall = pltpu.VMEM((count, N, BLOCK), jnp.float32)
    return [block] * 4 + [tall] * 2


def dot(left, right):
    return jnp.dot(left, right, precision=HIGHEST, preferred_element_type=jnp.float32)


def dot_t(left, right):
    return lax.dot_general(
        left,
        right,
        (((0,), (0,)), ((), ())),
        precision=HIGHEST,
        preferred_element_type=jnp.float32,
    )


def beside(*parts):
    return jnp.concatenate(parts, axis=1)


def joined(g00, g01, g11):
    return jnp.concatenate([beside(g00, g01), beside(g01.T, g11)], axis=0)


def turn(p, q, c, s):
    return c * p - s * q, s * p + c * q


def advance(p, q, axis):
    at = lax.broadcasted_iota(jnp.int32, p.shape, axis)
    p_back = pltpu.roll(p, BLOCK - 1, axis)
    q_on = pltpu.roll(q, 1, axis)
    new_p = jnp.where(at == 0, p, jnp.where(at == BLOCK - 1, q, p_back))
    new_q = jnp.where(at == 0, p_back, q_on)
    return new_p, new_q


def solves(grams, along, down, scratch):
    a, b, c_, d_, qp, qq = scratch
    lane = lax.broadcasted_iota(jnp.int32, (N, N), 1).astype(jnp.float32)
    sub = lax.broadcasted_iota(jnp.int32, (N, N), 0).astype(jnp.float32)
    take = jnp.where(sub == along[0:1, :], 1.0, 0.0).astype(jnp.float32)
    take_t = jnp.where(lane == down[:, 0:1], 1.0, 0.0).astype(jnp.float32)
    back_t = jnp.where(lane == down[:, 1:2], 1.0, 0.0).astype(jnp.float32)
    for k, gram in enumerate(grams):
        placed = dot(take_t, dot(gram, take))
        a[k] = placed[:BLOCK, :BLOCK]
        b[k] = placed[:BLOCK, BLOCK:]
        c_[k] = placed[BLOCK:, :BLOCK]
        d_[k] = placed[BLOCK:, BLOCK:]
        qp[k] = take[:, :BLOCK]
        qq[k] = take[:, BLOCK:]
    i0 = lax.broadcasted_iota(jnp.int32, (BLOCK, BLOCK), 0)
    i1 = lax.broadcasted_iota(jnp.int32, (BLOCK, BLOCK), 1)

    def round_fn(r, carry):
        on = i0 == i1

        def diagonal(m):
            return jnp.sum(jnp.where(on, m, 0.0), axis=0, keepdims=True)

        for k in range(len(grams)):
            ga, gb, gc, gd = a[k], b[k], c_[k], d_[k]
            gpp, cr, gqq = diagonal(ga), diagonal(gb), diagonal(gd)
            d = gqq - gpp
            root = jnp.sqrt(d * d + 4.0 * cr * cr)
            t = 2.0 * cr * d / ((jnp.abs(d) + root) * root + 1e-06 * (gpp + gqq) * (gpp + gqq))
            c = 1.0 / jnp.sqrt(1.0 + t * t)
            s = t * c
            c_col = jnp.sum(jnp.where(on, c, 0.0), axis=1, keepdims=True)
            s_col = jnp.sum(jnp.where(on, s, 0.0), axis=1, keepdims=True)
            ga, gb = advance(*turn(ga, gb, c, s), 1)
            gc, gd = advance(*turn(gc, gd, c, s), 1)
            ga, gc = advance(*turn(ga, gc, c_col, s_col), 0)
            gb, gd = advance(*turn(gb, gd, c_col, s_col), 0)
            a[k], b[k], c_[k], d_[k] = ga, gb, gc, gd
            qp[k], qq[k] = advance(*turn(qp[k], qq[k], c, s), 1)
        return carry

    lax.fori_loop(0, ROUNDS, round_fn, 0)
    return [dot(beside(qp[k], qq[k]), back_t) for k in range(len(grams))]


def gram_kernel(own, other, out):
    x = jnp.concatenate([own[...], other[...]], axis=0)
    x0, x1 = x[:, :BLOCK], x[:, BLOCK:]
    out[0], out[1], out[2] = dot_t(x0, x0), dot_t(x0, x1), dot_t(x1, x1)


def mixed_kernel(x, near, out):
    out[...] = dot_t(x[...], near[...])


def first_kernel(sums, along, down, q_out, ship, *scratch):
    gram = joined(sums[0], sums[1], sums[2])
    (q,) = solves([gram], along[...], down[...], scratch)
    q_out[...] = q
    q1 = q[:, BLOCK:]
    ship[:N] = q1
    ship[N:] = dot_t(q1, dot(gram, q1))


def keep_kernel(sums, q, x, g00, kept):
    q0 = q[:, :BLOCK]
    kept[...] = dot(x[...], q0)
    g00[...] = dot_t(q0, dot(joined(sums[0], sums[1], sums[2]), q0))


def second_kernel(mixed, q, ship, g00, kept, near, along, down, x0, x1, gram_out, q_out, *scratch):
    q1 = ship[:N]
    cross = dot_t(q[:, :BLOCK], dot(mixed[...], q1))
    gram = joined(g00[...], cross, ship[N:])
    gram_out[...] = gram
    (turned,) = solves([gram], along[...], down[...], scratch)
    q_out[...] = turned
    y = dot(beside(kept[...], dot(near[...], q1)), turned)
    x0[...] = y[:, :BLOCK]
    x1[...] = y[:, BLOCK:]


def turned_kernel(gram, q, out):
    g = dot_t(q[...], dot(gram[...], q[...]))
    out[0], out[1], out[2] = g[:BLOCK, :BLOCK], g[:BLOCK, BLOCK:], g[BLOCK:, BLOCK:]


def cross_kernel(far0, x0, x1, near1, out):
    f0, s0, s1, n1 = far0[...], x0[...], x1[...], near1[...]
    out[0] = dot_t(f0, s1)
    out[1] = dot_t(s0, n1)
    out[2] = dot_t(f0, s0)
    out[3] = dot_t(f0, n1)
    out[4] = dot_t(s1, n1)


def last_kernel(
    sums, inner, far00, near11, far0, x0, x1, near1, along2, down2, along3, down3, out, *scratch
):
    gram_a = joined(far00[...], sums[0], inner[2])
    gram_b = joined(inner[0], sums[1], near11[...])
    qa, qb = solves([gram_a, gram_b], along2[...], down2[...], scratch)
    qa, qb = qa[:, :BLOCK], qb[:, BLOCK:]
    mixed = jnp.concatenate([beside(sums[2], sums[3]), beside(inner[1].T, sums[4])], axis=0)
    gram = joined(
        dot_t(qa, dot(gram_a, qa)), dot_t(qa, dot(mixed, qb)), dot_t(qb, dot(gram_b, qb))
    )
    (q,) = solves([gram], along3[...], down3[...], scratch)
    ya = dot(beside(far0[...], x1[...]), qa)
    yb = dot(beside(x0[...], near1[...]), qb)
    out[...] = dot(beside(ya, yb), q)


def chip_groups(size):
    return [list(range(core, size, 2)) for core in range(2)]


def sum_slices(part):
    groups = chip_groups(lax.axis_size("rows"))
    n = len(groups[0])
    return lax.all_to_all(
        part.reshape(n, -1, part.shape[-1]), "rows", 0, 0, axis_index_groups=groups
    ).sum(0)


def all_slices(mine, dims):
    groups = chip_groups(lax.axis_size("rows"))
    spread = jnp.broadcast_to(mine[None], (len(groups[0]),) + mine.shape)
    return lax.all_to_all(spread, "rows", 0, 0, axis_index_groups=groups).reshape(dims)


def other_core(x):
    return lax.ppermute(x, "rows", [(i, i ^ 1) for i in range(lax.axis_size("rows"))])


def along_pairs(x, sign):
    n_rows, n_pairs = lax.axis_size("rows"), lax.axis_size("pairs")
    route = []
    for r in range(n_rows):
        step = sign if r % 2 else -sign
        for p in range(n_pairs):
            route.append((r * n_pairs + p, r * n_pairs + (p + step) % n_pairs))
    return lax.ppermute(x, ("rows", "pairs"), route)


def body(sample, column_scale, inner_order):
    row, col = lax.axis_index("rows"), lax.axis_index("pairs")
    core = row % 2
    first = core == 0
    n_pairs = lax.axis_size("pairs")
    data = sample * column_scale[None, :]
    rows = data.shape[0]
    left, right = data[:, :N], data[:, N:]
    own = jnp.where(first, left, beside(right[:, BLOCK:], right[:, :BLOCK]))
    send = jnp.where(first, beside(right[:, BLOCK:], right[:, :BLOCK]), left)
    got = other_core(send)
    x = jnp.concatenate([own, got], axis=0)
    near = along_pairs(x, 1)
    near_col = (col + jnp.where(first, 1, -1)) % n_pairs

    height = W // lax.axis_size("rows")
    ids = jnp.arange(height, dtype=jnp.int32)
    row_ids = jnp.concatenate([ids + row * height, ids + (row ^ 1) * height])[:, None]
    places = (jnp.arange(N, dtype=jnp.int32)[None, :] + core * BLOCK) % N + core * N

    def with_basis(values, at):
        unit = jnp.where(row_ids == places + 2 * N * at, 1.0, 0.0).astype(jnp.float32)
        return jnp.concatenate([values, unit])

    order = ((inner_order + core * BLOCK) % N).astype(jnp.float32)
    table = np.concatenate([np.eye(N)[:, arrangement(0)], np.eye(N)[:, arrangement(ROUNDS)]], 1)
    table = jnp.asarray(table.astype(np.float32))
    along = dot(order, table).reshape(STEPS, 2, N)
    down = dot_t(table, order.T).reshape(2, N, STEPS)
    down = [down[:, :, s].T for s in range(STEPS)]

    blocks = (3, BLOCK, BLOCK)
    sums = sum_slices(call(gram_kernel, shape(*blocks), [], own, got).reshape(-1, BLOCK))
    mixed = call(mixed_kernel, shape(N, N), [], x, near)
    mixed = sum_slices(mixed)
    sums = all_slices(sums, blocks)
    mixed = all_slices(mixed, (N, N))

    x, near = with_basis(x, col), with_basis(near, near_col)
    total = x.shape[0]
    q, ship = call(
        first_kernel,
        (shape(N, N), shape(N + BLOCK, BLOCK)),
        solve_scratch(1),
        sums,
        along[0],
        down[0],
    )
    ship = along_pairs(ship, 1)
    g00, kept = call(keep_kernel, (shape(BLOCK, BLOCK), shape(total, BLOCK)), [], sums, q, x)
    half = shape(total, BLOCK)
    x0, x1, gram, q = call(
        second_kernel,
        (half, half, shape(N, N), shape(N, N)),
        solve_scratch(1),
        mixed,
        q,
        ship,
        g00,
        kept,
        near,
        along[1],
        down[1],
    )

    both = 2 * rows
    far0, near1 = along_pairs(x0[:both], -1), along_pairs(x1[:both], 1)
    cross = call(
        cross_kernel, shape(5, BLOCK, BLOCK), [], far0, x0[:both], x1[:both], near1
    )
    sums = sum_slices(cross.reshape(-1, BLOCK))
    inner = call(turned_kernel, shape(3, BLOCK, BLOCK), [], gram, q)
    far_rest = along_pairs(jnp.concatenate([x0[both:], inner[0]]), -1)
    near_rest = along_pairs(jnp.concatenate([x1[both:], inner[2]]), 1)
    sums = all_slices(sums, (5, BLOCK, BLOCK))
    cut = 2 * height
    far0 = jnp.concatenate([far0, far_rest[:cut]])
    near1 = jnp.concatenate([near1, near_rest[:cut]])
    y = call(
        last_kernel,
        shape(total, N),
        solve_scratch(2),
        sums,
        inner,
        far_rest[cut:],
        near_rest[cut:],
        far0,
        x0,
        x1,
        near1,
        along[2],
        down[2],
        along[3],
        down[3],
    )
    mine = jnp.concatenate([y[:rows], y[both : both + height]])
    theirs = jnp.concatenate([y[rows:both], y[both + height :]])
    got = other_core(theirs)

    def ordered(part, swapped):
        return jnp.where(swapped, beside(part[:, BLOCK:], part[:, :BLOCK]), part)

    mine, got = ordered(mine, core == 1), ordered(got, core == 0)
    whole = jnp.where(first, beside(got, mine), beside(mine, got))
    return whole[:rows], whole[rows:]


def solution(mesh):
    return jax.shard_map(
        body,
        mesh=mesh,
        in_specs=(P("rows", "pairs"), P("pairs"), P()),
        out_specs=(P("rows", "pairs"), P("rows", "pairs")),
        check_vma=False,
    )
```

time: 179 us -> 153 us (0.85)
  starting transfers between devices: 73 us -> 56.7 us
  waiting for transfers between devices: 65 us -> 50.3 us
  Pallas kernels: 20.7 us -> 35.2 us
  matrix products: 9.47 us -> 0.36 us
    pallas_call x4 -> x8, Pallas kernels: 20.7 us -> 35.2 us  [call(): pl.pallas_call(kernel, out_shape=out_shape, in_specs=[VMEM] * len(operand...]
    all_to_all x8 -> x6, waiting for transfers between devices: 49.1 us -> 38.1 us  [the longest x3 29.5 us: sum_slices(): lax.all_to_all(part.reshape(n, -1, part.shape[-1]), 'rows', 0, 0, axis_in...]
    dot_general x16 -> x1, matrix products: 9.47 us -> 0.36 us  [dot(): jnp.dot(left, right, precision=HIGHEST, preferred_element_type=jnp.float32)]
    all_to_all x8 -> x6, starting transfers between devices: 36.7 us -> 29.7 us  [the longest x3 19.1 us: sum_slices(): lax.all_to_all(part.reshape(n, -1, part.shape[-1]), 'rows', 0, 0, axis_in...]
    ppermute x2, starting transfers between devices: 18 us -> 12.3 us  [other_core(): lax.ppermute(x, 'rows', [(i, i ^ 1) for i in range(lax.axis_size('rows'))])]
    ppermute x9 -> x6, waiting for transfers between devices: 14.5 us -> 9.76 us  [along_pairs(): return lax.ppermute(x, ('rows', 'pairs'), route)]
    ppermute x9 -> x6, starting transfers between devices: 18.3 us -> 14.6 us  [along_pairs(): return lax.ppermute(x, ('rows', 'pairs'), route)]
  transfers between devices with their start and end apart: 19 -> 14, of which waited for: 14 -> 9; matrix products, arithmetic and copies ran while one was open for 6% -> 1% of each run, Pallas kernels for 0% -> 7%
where the time goes in v2:
time: 153 us; the launch traced here: 152 us
  starting transfers between devices  56.7 us (37%)
  waiting for transfers between devices  50.3 us (33%)
  Pallas kernels  35.2 us (23%)
  local copies, waits for them, and re-layouts  6.77 us (4%)
  other arithmetic  1.81 us (1%)
    pallas_call x8, Pallas kernels, call(): pl.pallas_call(kernel, out_shape=out_shape, in_specs=[VMEM] * len(operand...  35.2 us
    all_to_all x3, waiting for transfers between devices, sum_slices(): lax.all_to_all(part.reshape(n, -1, part.shape[-1]), 'rows', 0, 0, axis_in...  29.5 us
    all_to_all x3, starting transfers between devices, sum_slices(): lax.all_to_all(part.reshape(n, -1, part.shape[-1]), 'rows', 0, 0, axis_in...  19.1 us
    ppermute x6, starting transfers between devices, along_pairs(): return lax.ppermute(x, ('rows', 'pairs'), route)  14.6 us
    ppermute x2, starting transfers between devices, other_core(): lax.ppermute(x, 'rows', [(i, i ^ 1) for i in range(lax.axis_size('rows'))])  12.3 us
    all_to_all x3, starting transfers between devices, all_slices(): lax.all_to_all(spread, 'rows', 0, 0, axis_index_groups=groups).reshape(dims)  10.6 us
    ppermute x6, waiting for transfers between devices, along_pairs(): return lax.ppermute(x, ('rows', 'pairs'), route)  9.76 us
    all_to_all x3, waiting for transfers between devices, all_slices(): lax.all_to_all(spread, 'rows', 0, 0, axis_index_groups=groups).reshape(dims)  8.58 us
  transfers between devices with their start and end apart: 14, of which 9 were waited for; matrix products, arithmetic and copies ran while one was open for 1% of the time, Pallas kernels for 7%

profile of v2, /device:TPU:7, one launch (start us, length us, event | category | flops | bytes accessed | tf_op | source)
XLA Modules:
  0.0 152.2 jit_solution(9586121839259427331)
XLA Ops:
  0.6 0.7 copy-done.3
  1.3 1.1 broadcast_multiply_fusion
  2.5 0.8 collective-permute-start
  3.3 1.2 collective-permute-done.other
  4.5 2.9 %collective-permute-start.1 = (f32[512,256]{1,0:T(8,128)S(1)}, f32[512,256]{1,0:T(8,128)S(1)}, u32[]{:S(2)}, u32[]{:S(2)}) collective-permute-start(f32[512,256]{1,0:T(8,128)S(1)} %pad_maximum_fusion.3.x), channel_id=1, source_target_pairs={{0,7},{1,0},{2,1},{3,2},{4,3},{5,4},{6,5},{7,6},{8,9},{9,10},{10,1... | collective-permute-start | bytes 1572872 | tf_op jit(solution)/shard_map/ppermute | solution.py:226
  7.4 1.5 shard_map.60
  8.9 8.4 %all-to-all-start.2 = ((f32[16,24,128]{2,1,0:T(8,128)}), f32[16,24,128]{2,1,0:T(8,128)S(1)}, u32[]{:S(2)}, u32[]{:S(2)}) async-start(f32[16,24,128]{2,1,0:T(8,128)} %bitcast.2), calls=%async_computation.2 | async-start | bytes 393216 | tf_op jit(solution)/shard_map/all_to_all | solution.py:204
  17.3 1.4 shard_map.59
  18.7 9.6 %all-to-all-done.2 = f32[16,24,128]{2,1,0:T(8,128)S(1)} async-done(((f32[16,24,128]{2,1,0:T(8,128)}), f32[16,24,128]{2,1,0:T(8,128)S(1)}, u32[]{:S(2)}, u32[]{:S(2)}) %all-to-all-start.2) | async-done | bytes 196640 | tf_op jit(solution)/shard_map/all_to_all | solution.py:204
  28.3 3.5 %all-to-all-start = ((f32[16,16,256]{2,1,0:T(8,128)}), f32[16,16,256]{2,1,0:T(8,128)S(1)}, u32[]{:S(2)}, u32[]{:S(2)}) async-start(f32[16,16,256]{2,1,0:T(8,128)} %bitcast), calls=%async_computation | async-start | bytes 524288 | tf_op jit(solution)/shard_map/all_to_all | solution.py:204
  31.9 0.4 fusion.5
  32.3 10.9 %all-to-all-done = f32[16,16,256]{2,1,0:T(8,128)S(1)} async-done(((f32[16,16,256]{2,1,0:T(8,128)}), f32[16,16,256]{2,1,0:T(8,128)S(1)}, u32[]{:S(2)}, u32[]{:S(2)}) %all-to-all-start) | async-done | bytes 262176 | tf_op jit(solution)/shard_map/all_to_all | solution.py:204
  43.2 0.7 broadcast_in_dim.17
  43.9 3.5 %all-to-all-start.3 = ((f32[16,24,128]{2,1,0:T(8,128)}), f32[16,24,128]{2,1,0:T(8,128)S(1)}, u32[]{:S(2)}, u32[]{:S(2)}) async-start(f32[16,24,128]{2,1,0:T(8,128)} %broadcast_in_dim.17), calls=%async_computation.3 | async-start | bytes 393216 | tf_op jit(solution)/shard_map/all_to_all | solution.py:212
  47.5 0.1 copy.10
  47.6 0.1 copy.11
  47.9 8.6 %all-to-all-done.3 = f32[16,24,128]{2,1,0:T(8,128)S(1)} async-done(((f32[16,24,128]{2,1,0:T(8,128)}), f32[16,24,128]{2,1,0:T(8,128)S(1)}, u32[]{:S(2)}, u32[]{:S(2)}) %all-to-all-start.3) | async-done | bytes 196640 | tf_op jit(solution)/shard_map/all_to_all | solution.py:212
  56.4 0.7 broadcast_in_dim.16
  57.2 3.5 %all-to-all-start.1 = ((f32[16,16,256]{2,1,0:T(8,128)}), f32[16,16,256]{2,1,0:T(8,128)S(1)}, u32[]{:S(2)}, u32[]{:S(2)}) async-start(f32[16,16,256]{2,1,0:T(8,128)} %broadcast_in_dim.16), calls=%async_computation.1 | async-start | bytes 524288 | tf_op jit(solution)/shard_map/all_to_all | solution.py:212
  60.7 0.1 compare_select_fusion
  60.8 5.0 %shard_map.61 = (f32[256,256]{1,0:T(8,128)S(1)}, f32[384,128]{1,0:T(8,128)S(1)}) custom-call(f32[3,128,128]{2,1,0:T(8,128)S(1)} %bitcast.26, f32[2,256]{1,0:T(2,128)S(1)} %squeeze.30.along, f32[256,2]{1,0:T(8,128)S(1)} %bitcast.33), custom_call_target="tpu_custom_call" | custom-call | tf_op jit(solution)/shard_map/pallas_call | solution.py:32
  65.8 0.3 collective-permute-start.2
  66.2 1.2 shard_map.62
  67.5 3.5 %collective-permute-done.2.ship = f32[384,128]{1,0:T(8,128)S(1)} collective-permute-done((f32[384,128]{1,0:T(8,128)S(1)}, f32[384,128]{1,0:T(8,128)S(1)}, u32[]{:S(2)}, u32[]{:S(2)}) %collective-permute-start.2) | collective-permute-done | bytes 196640 | tf_op jit(solution)/shard_map/ppermute | solution.py:226
  70.9 7.0 %shard_map.63 = (f32[768,128]{1,0:T(8,128)S(1)}, f32[768,128]{1,0:T(8,128)S(1)}, f32[256,256]{1,0:T(8,128)S(1)}, f32[256,256]{1,0:T(8,128)S(1)}) custom-call(f32[256,256]{1,0:T(8,128)S(1)} %bitcast.29, f32[256,256]{1,0:T(8,128)S(1)} %get-tuple-element.10.q, f32[384,128]{1,0:T(8,128)S(1)} %collective-permute-done.2.ship, ...), custom_call_target="tpu_custom_call" | custom-call | tf_op jit(solution)/shard_map/pallas_call | solution.py:32
  78.0 0.1 collective-permute-start.3
  78.1 5.1 %collective-permute-start.4 = (f32[512,128]{1,0:T(8,128)S(1)}, f32[512,128]{1,0:T(8,128)S(1)}, u32[]{:S(2)}, u32[]{:S(2)}) collective-permute-start(f32[512,128]{1,0:T(8,128)S(1)} %slice.112.x1), channel_id=1, source_target_pairs={{0,7},{1,0},{2,1},{3,2},{4,3},{5,4},{6,5},{7,6},{8,9},{9,10},{10,1... | collective-permute-start | bytes 786440 | tf_op jit(solution)/shard_map/ppermute | solution.py:226
  83.2 3.7 %collective-permute-done.3.far0 = f32[512,128]{1,0:T(8,128)S(1)} collective-permute-done((f32[512,128]{1,0:T(8,128)S(1)}, f32[512,128]{1,0:T(8,128)S(1)}, u32[]{:S(2)}, u32[]{:S(2)}) %collective-permute-start.3) | collective-permute-done | bytes 262176 | tf_op jit(solution)/shard_map/ppermute | solution.py:226
  86.9 2.0 %shard_map.64 = f32[5,128,128]{2,1,0:T(8,128)} custom-call(f32[512,128]{1,0:T(8,128)S(1)} %collective-permute-done.3.far0, f32[512,128]{1,0:T(8,128)S(1)} %slice.111.x0, f32[512,128]{1,0:T(8,128)S(1)} %slice.112.x1, f32[512,128]{1,0:T(8,128)S(1)} %collective-permute-done.4.near1), custom_call_target="tpu_custom_call" | custom-call | tf_op jit(solution)/shard_map/pallas_call | solution.py:32
  88.9 7.2 %all-to-all-start.4 = ((f32[16,40,128]{2,1,0:T(8,128)}), f32[16,40,128]{2,1,0:T(8,128)S(1)}, u32[]{:S(2)}, u32[]{:S(2)}) async-start(f32[16,40,128]{2,1,0:T(8,128)} %bitcast.11), calls=%async_computation.4 | async-start | bytes 655360 | tf_op jit(solution)/shard_map/all_to_all | solution.py:204
  96.1 1.1 shard_map.65.inner
  97.2 9.1 %all-to-all-done.4 = f32[16,40,128]{2,1,0:T(8,128)S(1)} async-done(((f32[16,40,128]{2,1,0:T(8,128)}), f32[16,40,128]{2,1,0:T(8,128)S(1)}, u32[]{:S(2)}, u32[]{:S(2)}) %all-to-all-start.4) | async-done | bytes 327712 | tf_op jit(solution)/shard_map/all_to_all | solution.py:204
  106.3 0.7 broadcast_in_dim.35
  107.0 3.5 %all-to-all-start.5 = ((f32[16,40,128]{2,1,0:T(8,128)}), f32[16,40,128]{2,1,0:T(8,128)S(1)}, u32[]{:S(2)}, u32[]{:S(2)}) async-start(f32[16,40,128]{2,1,0:T(8,128)} %broadcast_in_dim.35), calls=%async_computation.5 | async-start | bytes 655360 | tf_op jit(solution)/shard_map/all_to_all | solution.py:212
  110.6 0.1 collective-permute-start.5
  110.7 6.2 %collective-permute-start.6 = (f32[384,128]{1,0:T(8,128)S(1)}, f32[384,128]{1,0:T(8,128)S(1)}, u32[]{:S(2)}, u32[]{:S(2)}) collective-permute-start(f32[384,128]{1,0:T(8,128)S(1)} %pad_maximum_fusion.9), channel_id=1, source_target_pairs={{0,7},{1,0},{2,1},{3,2},{4,3},{5,4},{6,5},{7,6},{8,9},{9,10},{10,1... | collective-permute-start | bytes 589832 | tf_op jit(solution)/shard_map/ppermute | solution.py:226
  116.9 0.1 copy.12
  117.1 0.1 copy.13
  117.2 2.6 %collective-permute-done.5 = f32[384,128]{1,0:T(8,128)S(1)} collective-permute-done((f32[384,128]{1,0:T(8,128)S(1)}, f32[384,128]{1,0:T(8,128)S(1)}, u32[]{:S(2)}, u32[]{:S(2)}) %collective-permute-start.5) | collective-permute-done | bytes 196640 | tf_op jit(solution)/shard_map/ppermute | solution.py:226
  119.9 0.7 copy-done.1
  120.6 0.9 slice-done
  121.5 15.9 %shard_map.66 = f32[768,256]{1,0:T(8,128)S(1)} custom-call(f32[5,128,128]{2,1,0:T(8,128)S(1)} %bitcast.28, f32[3,128,128]{2,1,0:T(8,128)S(1)} %shard_map.65.inner, f32[128,128]{1,0:T(8,128)S(1)} %slice.143.far00, f32[128,128]{1,0:T(8,128)S(1)} %slice.145.near11, f32[768,128]{1,0:T(8,128)S(1)} %pad_maximum_fusion.4.far0, ...), custom_call_target="tpu_custom_call" | custom-call | tf_op jit(solution)/shard_map/pallas_call | solution.py:32
  137.6 11.6 %collective-permute-start.7 = (f32[384,256]{1,0:T(8,128)S(1)}, f32[384,256]{1,0:T(8,128)S(1)}, u32[]{:S(2)}, u32[]{:S(2)}) collective-permute-start(f32[384,256]{1,0:T(8,128)S(1)} %pad_maximum_fusion.6), channel_id=1, source_target_pairs={{0,8},{8,0},{16,24},{24,16},{32,40},{40,32},{48,56},{56,48},{64,72... | collective-permute-start | bytes 1179656 | tf_op jit(solution)/shard_map/ppermute | solution.py:216
  149.2 0.1 fusion
  149.2 1.3 collective-permute-done.7
  150.6 0.1 maximum_select_fusion
  150.7 0.8 slice.162
  151.5 0.7 slice.163
  (47 shorter events, 0.8 us)
Async XLA Ops:
  0.6 0.7 copy-start.3
  2.5 1.9 %collective-permute-start = (f32[256,256]{1,0:T(8,128)S(1)}, f32[256,256]{1,0:T(8,128)S(1)}, u32[]{:S(2)}, u32[]{:S(2)}) collective-permute-start(f32[256,256]{1,0:T(8,128)S(1)} %get-tuple-element.27), channel_id=1, source_target_pairs={{0,8},{8,0},{16,24},{24,16},{32,40},{40,32},{48,56},{56,48},{64,72... | collective-permute-start | bytes 786440 | tf_op jit(solution)/shard_map/ppermute | solution.py:216
  4.5 12.8 %collective-permute-start.1 = (f32[512,256]{1,0:T(8,128)S(1)}, f32[512,256]{1,0:T(8,128)S(1)}, u32[]{:S(2)}, u32[]{:S(2)}) collective-permute-start(f32[512,256]{1,0:T(8,128)S(1)} %pad_maximum_fusion.3.x), channel_id=1, source_target_pairs={{0,7},{1,0},{2,1},{3,2},{4,3},{5,4},{6,5},{7,6},{8,9},{9,10},{10,1... | collective-permute-start | bytes 1572872 | tf_op jit(solution)/shard_map/ppermute | solution.py:226
  8.9 19.4 %all-to-all-start.2 = ((f32[16,24,128]{2,1,0:T(8,128)}), f32[16,24,128]{2,1,0:T(8,128)S(1)}, u32[]{:S(2)}, u32[]{:S(2)}) async-start(f32[16,24,128]{2,1,0:T(8,128)} %bitcast.2), calls=%async_computation.2 | async-start | bytes 393216 | tf_op jit(solution)/shard_map/all_to_all | solution.py:204
  17.3 14.6 %copy-start.2 = (s32[4,256]{1,0:T(4,128)S(1)}, s32[4,256]{1,0:T(4,128)}, u32[]{:S(2)}) copy-start(s32[4,256]{1,0:T(4,128)} %param.6) | copy-start | bytes 12292
  18.7 13.1 %copy-start = (f32[256,512]{1,0:T(8,128)S(1)}, f32[256,512]{1,0:T(8,128)}, u32[]{:S(2)}) copy-start(f32[256,512]{1,0:T(8,128)} %constant.68.clone) | copy-start | bytes 1572868
  28.3 14.8 %all-to-all-start = ((f32[16,16,256]{2,1,0:T(8,128)}), f32[16,16,256]{2,1,0:T(8,128)S(1)}, u32[]{:S(2)}, u32[]{:S(2)}) async-start(f32[16,16,256]{2,1,0:T(8,128)} %bitcast), calls=%async_computation | async-start | bytes 524288 | tf_op jit(solution)/shard_map/all_to_all | solution.py:204
  43.9 12.6 %all-to-all-start.3 = ((f32[16,24,128]{2,1,0:T(8,128)}), f32[16,24,128]{2,1,0:T(8,128)S(1)}, u32[]{:S(2)}, u32[]{:S(2)}) async-start(f32[16,24,128]{2,1,0:T(8,128)} %broadcast_in_dim.17), calls=%async_computation.3 | async-start | bytes 393216 | tf_op jit(solution)/shard_map/all_to_all | solution.py:212
  57.2 13.8 %all-to-all-start.1 = ((f32[16,16,256]{2,1,0:T(8,128)}), f32[16,16,256]{2,1,0:T(8,128)S(1)}, u32[]{:S(2)}, u32[]{:S(2)}) async-start(f32[16,16,256]{2,1,0:T(8,128)} %broadcast_in_dim.16), calls=%async_computation.1 | async-start | bytes 524288 | tf_op jit(solution)/shard_map/all_to_all | solution.py:212
  65.8 5.1 %collective-permute-start.2 = (f32[384,128]{1,0:T(8,128)S(1)}, f32[384,128]{1,0:T(8,128)S(1)}, u32[]{:S(2)}, u32[]{:S(2)}) collective-permute-start(f32[384,128]{1,0:T(8,128)S(1)} %get-tuple-element.11), channel_id=1, source_target_pairs={{0,7},{1,0},{2,1},{3,2},{4,3},{5,4},{6,5},{7,6},{8,9},{9,10},{10,1... | collective-permute-start | bytes 589832 | tf_op jit(solution)/shard_map/ppermute | solution.py:226
  78.0 8.9 %collective-permute-start.3 = (f32[512,128]{1,0:T(8,128)S(1)}, f32[512,128]{1,0:T(8,128)S(1)}, u32[]{:S(2)}, u32[]{:S(2)}) collective-permute-start(f32[512,128]{1,0:T(8,128)S(1)} %slice.111.x0), channel_id=1, source_target_pairs={{0,1},{1,2},{2,3},{3,4},{4,5},{5,6},{6,7},{7,0},{8,15},{9,8},{10,9... | collective-permute-start | bytes 786440 | tf_op jit(solution)/shard_map/ppermute | solution.py:226
  78.1 8.8 %collective-permute-start.4 = (f32[512,128]{1,0:T(8,128)S(1)}, f32[512,128]{1,0:T(8,128)S(1)}, u32[]{:S(2)}, u32[]{:S(2)}) collective-permute-start(f32[512,128]{1,0:T(8,128)S(1)} %slice.112.x1), channel_id=1, source_target_pairs={{0,7},{1,0},{2,1},{3,2},{4,3},{5,4},{6,5},{7,6},{8,9},{9,10},{10,1... | collective-permute-start | bytes 786440 | tf_op jit(solution)/shard_map/ppermute | solution.py:226
  88.9 17.4 %all-to-all-start.4 = ((f32[16,40,128]{2,1,0:T(8,128)}), f32[16,40,128]{2,1,0:T(8,128)S(1)}, u32[]{:S(2)}, u32[]{:S(2)}) async-start(f32[16,40,128]{2,1,0:T(8,128)} %bitcast.11), calls=%async_computation.4 | async-start | bytes 655360 | tf_op jit(solution)/shard_map/all_to_all | solution.py:204
  107.0 14.5 %all-to-all-start.5 = ((f32[16,40,128]{2,1,0:T(8,128)}), f32[16,40,128]{2,1,0:T(8,128)S(1)}, u32[]{:S(2)}, u32[]{:S(2)}) async-start(f32[16,40,128]{2,1,0:T(8,128)} %broadcast_in_dim.35), calls=%async_computation.5 | async-start | bytes 655360 | tf_op jit(solution)/shard_map/all_to_all | solution.py:212
  110.6 9.2 %collective-permute-start.5 = (f32[384,128]{1,0:T(8,128)S(1)}, f32[384,128]{1,0:T(8,128)S(1)}, u32[]{:S(2)}, u32[]{:S(2)}) collective-permute-start(f32[384,128]{1,0:T(8,128)S(1)} %pad_maximum_fusion.8), channel_id=1, source_target_pairs={{0,1},{1,2},{2,3},{3,4},{4,5},{5,6},{6,7},{7,0},{8,15},{9,8},{10,9... | collective-permute-start | bytes 589832 | tf_op jit(solution)/shard_map/ppermute | solution.py:226
  110.7 9.8 %collective-permute-start.6 = (f32[384,128]{1,0:T(8,128)S(1)}, f32[384,128]{1,0:T(8,128)S(1)}, u32[]{:S(2)}, u32[]{:S(2)}) collective-permute-start(f32[384,128]{1,0:T(8,128)S(1)} %pad_maximum_fusion.9), channel_id=1, source_target_pairs={{0,7},{1,0},{2,1},{3,2},{4,3},{5,4},{6,5},{7,6},{8,9},{9,10},{10,1... | collective-permute-start | bytes 589832 | tf_op jit(solution)/shard_map/ppermute | solution.py:226
  119.9 0.7 copy-start.1
  120.5 0.9 slice-start
  137.6 12.9 %collective-permute-start.7 = (f32[384,256]{1,0:T(8,128)S(1)}, f32[384,256]{1,0:T(8,128)S(1)}, u32[]{:S(2)}, u32[]{:S(2)}) collective-permute-start(f32[384,256]{1,0:T(8,128)S(1)} %pad_maximum_fusion.6), channel_id=1, source_target_pairs={{0,8},{8,0},{16,24},{24,16},{32,40},{40,32},{48,56},{56,48},{64,72... | collective-permute-start | bytes 1179656 | tf_op jit(solution)/shard_map/ppermute | solution.py:216

commit v3 on v2

--- a/solution.py
+++ b/solution.py
@@ -40,9 +40,8 @@
 
 
 def solve_scratch(count):
-    block = pltpu.VMEM((count, BLOCK, BLOCK), jnp.float32)
-    tall = pltpu.VMEM((count, N, BLOCK), jnp.float32)
-    return [block] * 4 + [tall] * 2
+    block = pltpu.VMEM((2, count, BLOCK + 16, BLOCK), jnp.float32)
+    return [block] * 8
 
 
 def dot(left, right):
@@ -67,63 +66,135 @@
     return jnp.concatenate([beside(g00, g01), beside(g01.T, g11)], axis=0)
 
 
+def thirds(x):
+    high = x.astype(jnp.bfloat16)
+    rest = x - high.astype(jnp.float32)
+    middle = rest.astype(jnp.bfloat16)
+    return high, middle, (rest - middle.astype(jnp.float32)).astype(jnp.bfloat16)
+
+
+def dot_16(left, right):
+    return jnp.dot(left, right, preferred_element_type=jnp.float32)
+
+
+def pick_columns(x, units):
+    high, middle, low = thirds(x)
+    return dot_16(high, units) + (dot_16(middle, units) + dot_16(low, units))
+
+
+def pick_rows(units, x):
+    high, middle, low = thirds(x)
+    return dot_16(units, high) + (dot_16(units, middle) + dot_16(units, low))
+
+
 def turn(p, q, c, s):
     return c * p - s * q, s * p + c * q
 
 
-def advance(p, q, axis):
-    at = lax.broadcasted_iota(jnp.int32, p.shape, axis)
-    p_back = pltpu.roll(p, BLOCK - 1, axis)
-    q_on = pltpu.roll(q, 1, axis)
+def advance(p, q):
+    at = lax.broadcasted_iota(jnp.int32, p.shape, 1)
+    p_back = pltpu.roll(p, BLOCK - 1, 1)
+    q_on = pltpu.roll(q, 1, 1)
     new_p = jnp.where(at == 0, p, jnp.where(at == BLOCK - 1, q, p_back))
     new_q = jnp.where(at == 0, p_back, q_on)
     return new_p, new_q
 
 
+def angles(gpp, cross, gqq):
+    d = gqq - gpp
+    root = jnp.sqrt(d * d + 4.0 * cross * cross)
+    t = 2.0 * cross * d / ((jnp.abs(d) + root) * root + 1e-06 * (gpp + gqq) * (gpp + gqq))
+    w = 1.0 + t * t
+    c = lax.rsqrt(w)
+    c = c * (1.5 - 0.5 * w * c * c)
+    return c, t * c
+
+
 def solves(grams, along, down, scratch):
-    a, b, c_, d_, qp, qq = scratch
+    ga, gb, gc, gd, qa, qb, qc, qd = scratch
+    count = len(grams)
     lane = lax.broadcasted_iota(jnp.int32, (N, N), 1).astype(jnp.float32)
     sub = lax.broadcasted_iota(jnp.int32, (N, N), 0).astype(jnp.float32)
-    take = jnp.where(sub == along[0:1, :], 1.0, 0.0).astype(jnp.float32)
-    take_t = jnp.where(lane == down[:, 0:1], 1.0, 0.0).astype(jnp.float32)
-    back_t = jnp.where(lane == down[:, 1:2], 1.0, 0.0).astype(jnp.float32)
-    for k, gram in enumerate(grams):
-        placed = dot(take_t, dot(gram, take))
-        a[k] = placed[:BLOCK, :BLOCK]
-        b[k] = placed[:BLOCK, BLOCK:]
-        c_[k] = placed[BLOCK:, :BLOCK]
-        d_[k] = placed[BLOCK:, BLOCK:]
-        qp[k] = take[:, :BLOCK]
-        qq[k] = take[:, BLOCK:]
+    take = jnp.where(sub == along[0:1, :], 1.0, 0.0).astype(jnp.bfloat16)
+    take_t = jnp.where(lane == down[:, 0:1], 1.0, 0.0)
+    back_t = jnp.where(lane == down[:, 1:2], 1.0, 0.0).astype(jnp.bfloat16)
     i0 = lax.broadcasted_iota(jnp.int32, (BLOCK, BLOCK), 0)
     i1 = lax.broadcasted_iota(jnp.int32, (BLOCK, BLOCK), 1)
-
-    def round_fn(r, carry):
+    at = lax.broadcasted_iota(jnp.int32, (1, BLOCK), 1)
+    body = pl.ds(8, BLOCK)
+    state = []
+    for k, gram in enumerate(grams):
+        placed = pick_rows(take_t.astype(jnp.bfloat16), pick_columns(gram, take))
+        a, b = placed[:BLOCK, :BLOCK], placed[:BLOCK, BLOCK:]
+        c_, d_ = placed[BLOCK:, :BLOCK], placed[BLOCK:, BLOCK:]
+        ga[0, k, body], gb[0, k, body], gc[0, k, body], gd[0, k, body] = a, b, c_, d_
+        qa[0, k, body], qb[0, k, body] = take_t[:BLOCK, :BLOCK], take_t[:BLOCK, BLOCK:]
+        qc[0, k, body], qd[0, k, body] = take_t[BLOCK:, :BLOCK], take_t[BLOCK:, BLOCK:]
         on = i0 == i1
 
         def diagonal(m):
             return jnp.sum(jnp.where(on, m, 0.0), axis=0, keepdims=True)
 
-        for k in range(len(grams)):
-            ga, gb, gc, gd = a[k], b[k], c_[k], d_[k]
-            gpp, cr, gqq = diagonal(ga), diagonal(gb), diagonal(gd)
-            d = gqq - gpp
-            root = jnp.sqrt(d * d + 4.0 * cr * cr)
-            t = 2.0 * cr * d / ((jnp.abs(d) + root) * root + 1e-06 * (gpp + gqq) * (gpp + gqq))
-            c = 1.0 / jnp.sqrt(1.0 + t * t)
-            s = t * c
-            c_col = jnp.sum(jnp.where(on, c, 0.0), axis=1, keepdims=True)
-            s_col = jnp.sum(jnp.where(on, s, 0.0), axis=1, keepdims=True)
-            ga, gb = advance(*turn(ga, gb, c, s), 1)
-            gc, gd = advance(*turn(gc, gd, c, s), 1)
-            ga, gc = advance(*turn(ga, gc, c_col, s_col), 0)
-            gb, gd = advance(*turn(gb, gd, c_col, s_col), 0)
-            a[k], b[k], c_[k], d_[k] = ga, gb, gc, gd
-            qp[k], qq[k] = advance(*turn(qp[k], qq[k], c, s), 1)
-        return carry
-
-    lax.fori_loop(0, ROUNDS, round_fn, 0)
-    return [dot(beside(qp[k], qq[k]), back_t) for k in range(len(grams))]
+        state.append((diagonal(a), diagonal(b), diagonal(d_)))
+
+    def one_round(old, new, k, gpp, cross, gqq):
+        c, s = angles(gpp, cross, gqq)
+        a, b, c_, d_ = ga[old, k, body], gb[old, k, body], gc[old, k, body], gd[old, k, body]
+        on = i0 == i1
+        c_col = jnp.sum(jnp.where(on, c, 0.0), axis=1, keepdims=True)
+        s_col = jnp.sum(jnp.where(on, s, 0.0), axis=1, keepdims=True)
+        low = c * gpp - s * cross
+        new_pp = c * low - s * (c * cross - s * gqq)
+        new_qq = s * (s * gpp + c * cross) + c * (s * cross + c * gqq)
+        new_pp, new_qq = advance(new_pp, new_qq)
+        off = (i0 == i1 + 2) | ((i0 == BLOCK - 1) & (i1 == BLOCK - 2))
+
+        def beyond(m):
+            return jnp.sum(jnp.where(off, m, 0.0), axis=0, keepdims=True)
+
+        ea, eb, ec, ed = (pltpu.roll(beyond(m), 1, 1) for m in (a, b, c_, d_))
+        ra, rb, rc, rd = (pltpu.roll(m[0:1], BLOCK - 1, 1) for m in (a, b, c_, d_))
+        end, start = at == BLOCK - 1, at == 0
+        cl, sl = pltpu.roll(c, 1, 1), pltpu.roll(s, 1, 1)
+        cr, sr = pltpu.roll(c, BLOCK - 1, 1), pltpu.roll(s, BLOCK - 1, 1)
+        cu, su = jnp.where(end, s, cr), jnp.where(end, -c, sr)
+        main = cu * (sl * ea + cl * eb) - su * (sl * ec + cl * ed)
+        tip = c * (cr * ra - sr * rb) - s * (cr * rc - sr * rd)
+        new_cross = jnp.where(start, tip, main)
+        a, b = advance(*turn(a, b, c, s))
+        c_, d_ = advance(*turn(c_, d_, c, s))
+        qs = [x[old, k, body] for x in (qa, qc, qb, qd)]
+        for first, second, top, bottom in (
+            (a, c_, ga, gc),
+            (b, d_, gb, gd),
+            (qs[0], qs[1], qa, qc),
+            (qs[2], qs[3], qb, qd),
+        ):
+            up, under = turn(first, second, c_col, s_col)
+            top[new, k, pl.ds(7, BLOCK)] = up
+            top[new, k, pl.ds(8, 1)] = up[0:1]
+            top[new, k, pl.ds(BLOCK + 7, 1)] = under[BLOCK - 1 :]
+            bottom[new, k, pl.ds(9, BLOCK)] = under
+            bottom[new, k, pl.ds(8, 1)] = up[1:2]
+        return new_pp, new_cross, new_qq
+
+    def two_rounds(_, state):
+        state = [one_round(0, 1, k, *state[k]) for k in range(count)]
+        return [one_round(1, 0, k, *state[k]) for k in range(count)]
+
+    if count == 1:
+        lax.fori_loop(0, ROUNDS // 2, two_rounds, state)
+    else:
+        for pair in range(ROUNDS // 2):
+            state = two_rounds(pair, state)
+    turned = [
+        [jnp.concatenate([top[0, k, body], bottom[0, k, body]], axis=0).T for k in range(count)]
+        for top, bottom in ((qa, qc), (qb, qd))
+    ]
+    return [
+        pick_columns(jnp.concatenate([turned[0][k], turned[1][k]], axis=0), back_t)
+        for k in range(count)
+    ]
 
 
 def gram_kernel(own, other, out):
@@ -133,11 +204,27 @@
 
 
 def mixed_kernel(x, near, out):
-    out[...] = dot_t(x[...], near[...])
-
-
-def first_kernel(sums, along, down, q_out, ship, *scratch):
-    gram = joined(sums[0], sums[1], sums[2])
+    mixed = dot_t(x[...], near[...])
+    out[0], out[1] = mixed[:, :BLOCK], mixed[:, BLOCK:]
+
+
+def spread_kernel(parts, mixed, out):
+    n, m = parts.shape[0], parts.shape[1]
+    total = parts[0]
+    for k in range(1, n):
+        total = total + parts[k]
+    for k in range(n):
+        out[k, :m] = total
+    out[:, m:] = mixed[...]
+
+
+def first_gram(landed, m):
+    sums = landed[:, :m].reshape(3, BLOCK, BLOCK)
+    return joined(sums[0], sums[1], sums[2])
+
+
+def first_kernel(landed, along, down, q_out, ship, *scratch):
+    gram = first_gram(landed, 3 * BLOCK // landed.shape[0])
     (q,) = solves([gram], along[...], down[...], scratch)
     q_out[...] = q
     q1 = q[:, BLOCK:]
@@ -145,15 +232,15 @@
     ship[N:] = dot_t(q1, dot(gram, q1))
 
 
-def keep_kernel(sums, q, x, g00, kept):
+def keep_kernel(landed, q, x, g00, kept):
     q0 = q[:, :BLOCK]
     kept[...] = dot(x[...], q0)
-    g00[...] = dot_t(q0, dot(joined(sums[0], sums[1], sums[2]), q0))
+    g00[...] = dot_t(q0, dot(first_gram(landed, 3 * BLOCK // landed.shape[0]), q0))
 
 
 def second_kernel(mixed, q, ship, g00, kept, near, along, down, x0, x1, gram_out, q_out, *scratch):
     q1 = ship[:N]
-    cross = dot_t(q[:, :BLOCK], dot(mixed[...], q1))
+    cross = dot_t(q[:, :BLOCK], dot(beside(mixed[0], mixed[1]), q1))
     gram = joined(g00[...], cross, ship[N:])
     gram_out[...] = gram
     (turned,) = solves([gram], along[...], down[...], scratch)
@@ -178,7 +265,23 @@
 
 
 def last_kernel(
-    sums, inner, far00, near11, far0, x0, x1, near1, along2, down2, along3, down3, out, *scratch
+    sums,
+    inner,
+    far00,
+    near11,
+    far0,
+    x0,
+    x1,
+    near1,
+    along2,
+    down2,
+    along3,
+    down3,
+    swapped,
+    mine_data,
+    mine_basis,
+    theirs,
+    *scratch,
 ):
     gram_a = joined(far00[...], sums[0], inner[2])
     gram_b = joined(inner[0], sums[1], near11[...])
@@ -191,25 +294,29 @@
     (q,) = solves([gram], along3[...], down3[...], scratch)
     ya = dot(beside(far0[...], x1[...]), qa)
     yb = dot(beside(x0[...], near1[...]), qb)
-    out[...] = dot(beside(ya, yb), q)
+    y = dot(beside(ya, yb), q)
+    swap = swapped[...] > 0.0
+    y = beside(
+        jnp.where(swap, y[:, BLOCK:], y[:, :BLOCK]), jnp.where(swap, y[:, :BLOCK], y[:, BLOCK:])
+    )
+    rows, height = mine_data.shape[0], mine_basis.shape[0]
+    mine_data[...] = y[:rows]
+    theirs[:rows] = y[rows : 2 * rows]
+    mine_basis[...] = y[2 * rows : 2 * rows + height]
+    theirs[rows:] = y[2 * rows + height :]
 
 
 def chip_groups(size):
     return [list(range(core, size, 2)) for core in range(2)]
 
 
-def sum_slices(part):
+def trade(parts):
     groups = chip_groups(lax.axis_size("rows"))
-    n = len(groups[0])
-    return lax.all_to_all(
-        part.reshape(n, -1, part.shape[-1]), "rows", 0, 0, axis_index_groups=groups
-    ).sum(0)
-
-
-def all_slices(mine, dims):
-    groups = chip_groups(lax.axis_size("rows"))
-    spread = jnp.broadcast_to(mine[None], (len(groups[0]),) + mine.shape)
-    return lax.all_to_all(spread, "rows", 0, 0, axis_index_groups=groups).reshape(dims)
+    return lax.all_to_all(parts, "rows", 0, 0, axis_index_groups=groups)
+
+
+def all_slices(mine, n):
+    return trade(jnp.broadcast_to(mine[None], (n,) + mine.shape))
 
 
 def other_core(x):
@@ -257,12 +364,14 @@
     down = dot_t(table, order.T).reshape(2, N, STEPS)
     down = [down[:, :, s].T for s in range(STEPS)]
 
-    blocks = (3, BLOCK, BLOCK)
-    sums = sum_slices(call(gram_kernel, shape(*blocks), [], own, got).reshape(-1, BLOCK))
-    mixed = call(mixed_kernel, shape(N, N), [], x, near)
-    mixed = sum_slices(mixed)
-    sums = all_slices(sums, blocks)
-    mixed = all_slices(mixed, (N, N))
+    chips = lax.axis_size("rows") // 2
+    gram_rows, mixed_rows = 3 * BLOCK // chips, 2 * N // chips
+    parts = trade(call(gram_kernel, shape(3, BLOCK, BLOCK), [], own, got).reshape(chips, -1, BLOCK))
+    mixed = call(mixed_kernel, shape(2, N, BLOCK), [], x, near).reshape(chips, -1, BLOCK)
+    landed = trade(
+        call(spread_kernel, shape(chips, gram_rows + mixed_rows, BLOCK), [], parts, mixed)
+    )
+    mixed = all_slices(landed[:, gram_rows:].sum(0), chips).reshape(2, N, BLOCK)
 
     x, near = with_basis(x, col), with_basis(near, near_col)
     total = x.shape[0]
@@ -270,12 +379,12 @@
         first_kernel,
         (shape(N, N), shape(N + BLOCK, BLOCK)),
         solve_scratch(1),
-        sums,
+        landed,
         along[0],
         down[0],
     )
     ship = along_pairs(ship, 1)
-    g00, kept = call(keep_kernel, (shape(BLOCK, BLOCK), shape(total, BLOCK)), [], sums, q, x)
+    g00, kept = call(keep_kernel, (shape(BLOCK, BLOCK), shape(total, BLOCK)), [], landed, q, x)
     half = shape(total, BLOCK)
     x0, x1, gram, q = call(
         second_kernel,
@@ -296,17 +405,17 @@
     cross = call(
         cross_kernel, shape(5, BLOCK, BLOCK), [], far0, x0[:both], x1[:both], near1
     )
-    sums = sum_slices(cross.reshape(-1, BLOCK))
+    sums = trade(cross.reshape(chips, -1, BLOCK)).sum(0)
     inner = call(turned_kernel, shape(3, BLOCK, BLOCK), [], gram, q)
     far_rest = along_pairs(jnp.concatenate([x0[both:], inner[0]]), -1)
     near_rest = along_pairs(jnp.concatenate([x1[both:], inner[2]]), 1)
-    sums = all_slices(sums, (5, BLOCK, BLOCK))
+    sums = all_slices(sums, chips).reshape(5, BLOCK, BLOCK)
     cut = 2 * height
     far0 = jnp.concatenate([far0, far_rest[:cut]])
     near1 = jnp.concatenate([near1, near_rest[:cut]])
-    y = call(
+    mine_data, mine_basis, theirs = call(
         last_kernel,
-        shape(total, N),
+        (shape(rows, N), shape(height, N), shape(rows + height, N)),
         solve_scratch(2),
         sums,
         inner,
@@ -320,17 +429,14 @@
         down[2],
         along[3],
         down[3],
-    )
-    mine = jnp.concatenate([y[:rows], y[both : both + height]])
-    theirs = jnp.concatenate([y[rows:both], y[both + height :]])
+        jnp.full((1, BLOCK), core, jnp.float32),
+    )
     got = other_core(theirs)
 
-    def ordered(part, swapped):
-        return jnp.where(swapped, beside(part[:, BLOCK:], part[:, :BLOCK]), part)
-
-    mine, got = ordered(mine, core == 1), ordered(got, core == 0)
-    whole = jnp.where(first, beside(got, mine), beside(mine, got))
-    return whole[:rows], whole[rows:]
+    def placed(got, mine):
+        return jnp.where(first, beside(got, mine), beside(mine, got))
+
+    return placed(got[:rows], mine_data), placed(got[rows:], mine_basis)
 
 
 def solution(mesh):

time: 153 us -> 146 us (0.954)
  the two profiles are of different devices: /device:TPU:7 before, /device:TPU:25 now
where the time goes in v3:
time: 146 us
  starting transfers between devices  62.2 us (43%)
  waiting for transfers between devices  38.4 us (26%)
  Pallas kernels  32.1 us (22%)
  local copies, waits for them, and re-layouts  8.43 us (6%)
  other arithmetic  3.1 us (2%)
    pallas_call x9, Pallas kernels, call(): pl.pallas_call(kernel, out_shape=out_shape, in_specs=[VMEM] * len(operand...  32.1 us
    all_to_all x5, starting transfers between devices, trade(): return lax.all_to_all(parts, 'rows', 0, 0, axis_index_groups=groups)  31.3 us
    all_to_all x5, waiting for transfers between devices, trade(): return lax.all_to_all(parts, 'rows', 0, 0, axis_index_groups=groups)  24.4 us
    ppermute x6, starting transfers between devices, along_pairs(): return lax.ppermute(x, ('rows', 'pairs'), route)  17.2 us
    ppermute x2, starting transfers between devices, other_core(): lax.ppermute(x, 'rows', [(i, i ^ 1) for i in range(lax.axis_size('rows'))])  13.7 us
    ppermute x6, waiting for transfers between devices, along_pairs(): return lax.ppermute(x, ('rows', 'pairs'), route)  11.5 us
    unnamed x20, local copies, waits for them, and re-layouts  4.4 us
  transfers between devices with their start and end apart: 13, of which 8 were waited for; matrix products, arithmetic and copies ran while one was open for 1% of the time, Pallas kernels for 6%

profile of v3, /device:TPU:25, one launch (start us, length us, event | category | flops | bytes accessed | tf_op | source)
XLA Modules:
  0.0 145.6 jit_solution(3940447515585514624)
XLA Ops:
  0.7 0.7 copy-done.7
  1.3 1.1 broadcast_multiply_fusion
  2.5 0.8 collective-permute-start
  3.3 1.2 collective-permute-done.other
  4.5 1.3 collective-permute-start.1
  5.8 1.5 %shard_map.59 = f32[3,128,128]{2,1,0:T(8,128)} custom-call(f32[256,256]{1,0:T(8,128)S(1)} %get-tuple-element.29.own, f32[256,256]{1,0:T(8,128)S(1)} %collective-permute-done.other), custom_call_target="tpu_custom_call" | custom-call | tf_op jit(solution)/shard_map/pallas_call | solution.py:32
  7.3 9.4 %all-to-all-start = ((f32[16,24,128]{2,1,0:T(8,128)}), f32[16,24,128]{2,1,0:T(8,128)S(1)}, u32[]{:S(2)}, u32[]{:S(2)}) async-start(f32[16,24,128]{2,1,0:T(8,128)} %bitcast), calls=%async_computation | async-start | bytes 393216 | tf_op jit(solution)/shard_map/all_to_all | solution.py:315
  16.7 0.7 shard_map.60
  17.4 7.5 %all-to-all-done.parts = f32[16,24,128]{2,1,0:T(8,128)S(1)} async-done(((f32[16,24,128]{2,1,0:T(8,128)}), f32[16,24,128]{2,1,0:T(8,128)S(1)}, u32[]{:S(2)}, u32[]{:S(2)}) %all-to-all-start) | async-done | bytes 196640 | tf_op jit(solution)/shard_map/all_to_all | solution.py:315
  24.9 0.8 shard_map.61
  25.7 4.5 %all-to-all-start.1 = ((f32[16,56,128]{2,1,0:T(8,128)}), f32[16,56,128]{2,1,0:T(8,128)S(1)}, u32[]{:S(2)}, u32[]{:S(2)}) async-start(f32[16,56,128]{2,1,0:T(8,128)} %shard_map.61), calls=%async_computation.1 | async-start | bytes 917504 | tf_op jit(solution)/shard_map/all_to_all | solution.py:315
  30.2 0.4 fusion.2
  30.6 0.1 copy.10
  30.7 0.6 slice_reduce_fusion.1
  31.4 0.1 copy.11
  31.6 8.9 %all-to-all-done.1.landed = f32[16,56,128]{2,1,0:T(8,128)S(1)} async-done(((f32[16,56,128]{2,1,0:T(8,128)}), f32[16,56,128]{2,1,0:T(8,128)S(1)}, u32[]{:S(2)}, u32[]{:S(2)}) %all-to-all-start.1) | async-done | bytes 458784 | tf_op jit(solution)/shard_map/all_to_all | solution.py:315
  40.5 0.7 broadcast_in_dim.28
  41.2 5.4 %all-to-all-start.2 = ((f32[16,32,128]{2,1,0:T(8,128)}), f32[16,32,128]{2,1,0:T(8,128)S(1)}, u32[]{:S(2)}, u32[]{:S(2)}) async-start(f32[16,32,128]{2,1,0:T(8,128)} %broadcast_in_dim.28), calls=%async_computation.2 | async-start | bytes 524288 | tf_op jit(solution)/shard_map/all_to_all | solution.py:315
  46.8 3.7 %shard_map.62 = (f32[256,256]{1,0:T(8,128)S(1)}, f32[384,128]{1,0:T(8,128)S(1)}) custom-call(f32[16,56,128]{2,1,0:T(8,128)S(1)} %all-to-all-done.1.landed, f32[2,256]{1,0:T(2,128)S(1)} %squeeze.30.along, f32[256,2]{1,0:T(8,128)S(1)} %bitcast.31), custom_call_target="tpu_custom_call" | custom-call | tf_op jit(solution)/shard_map/pallas_call | solution.py:32
  50.5 4.9 %collective-permute-start.2 = (f32[384,128]{1,0:T(8,128)S(1)}, f32[384,128]{1,0:T(8,128)S(1)}, u32[]{:S(2)}, u32[]{:S(2)}) collective-permute-start(f32[384,128]{1,0:T(8,128)S(1)} %get-tuple-element.14), channel_id=1, source_target_pairs={{0,7},{1,0},{2,1},{3,2},{4,3},{5,4},{6,5},{7,6},{8,9},{9,10},{10,1... | collective-permute-start | bytes 589832 | tf_op jit(solution)/shard_map/ppermute | solution.py:333
  55.5 1.2 shard_map.63
  56.7 0.6 copy-done
  57.4 5.6 %collective-permute-done.2.ship = f32[384,128]{1,0:T(8,128)S(1)} collective-permute-done((f32[384,128]{1,0:T(8,128)S(1)}, f32[384,128]{1,0:T(8,128)S(1)}, u32[]{:S(2)}, u32[]{:S(2)}) %collective-permute-start.2) | collective-permute-done | bytes 196640 | tf_op jit(solution)/shard_map/ppermute | solution.py:333
  62.9 0.8 copy-done.1
  63.8 5.8 %shard_map.64 = (f32[768,128]{1,0:T(8,128)S(1)}, f32[768,128]{1,0:T(8,128)S(1)}, f32[256,256]{1,0:T(8,128)S(1)}, f32[256,256]{1,0:T(8,128)S(1)}) custom-call(f32[2,256,128]{2,1,0:T(8,128)S(1)} %bitcast.27, f32[256,256]{1,0:T(8,128)S(1)} %get-tuple-element.13.q, f32[384,128]{1,0:T(8,128)S(1)} %collective-permute-done.2.ship, f32[128,128]{1,0:T(8,128)S(1)} %copy-done.1, ...), custom_call_target="tpu_custom_call" | custom-call | tf_op jit(solution)/shard_map/pallas_call | solution.py:32
  69.7 0.3 collective-permute-start.4
  70.0 5.1 %collective-permute-start.3 = (f32[512,128]{1,0:T(8,128)S(1)}, f32[512,128]{1,0:T(8,128)S(1)}, u32[]{:S(2)}, u32[]{:S(2)}) collective-permute-start(f32[512,128]{1,0:T(8,128)S(1)} %slice.91.x0), channel_id=1, source_target_pairs={{0,1},{1,2},{2,3},{3,4},{4,5},{5,6},{6,7},{7,0},{8,15},{9,8},{10,9... | collective-permute-start | bytes 786440 | tf_op jit(solution)/shard_map/ppermute | solution.py:333
  75.1 3.7 %collective-permute-done.4.near1 = f32[512,128]{1,0:T(8,128)S(1)} collective-permute-done((f32[512,128]{1,0:T(8,128)S(1)}, f32[512,128]{1,0:T(8,128)S(1)}, u32[]{:S(2)}, u32[]{:S(2)}) %collective-permute-start.4) | collective-permute-done | bytes 262176 | tf_op jit(solution)/shard_map/ppermute | solution.py:333
  78.8 2.0 %shard_map.65 = f32[5,128,128]{2,1,0:T(8,128)} custom-call(f32[512,128]{1,0:T(8,128)S(1)} %collective-permute-done.3.far0, f32[512,128]{1,0:T(8,128)S(1)} %slice.91.x0, f32[512,128]{1,0:T(8,128)S(1)} %slice.92.x1, f32[512,128]{1,0:T(8,128)S(1)} %collective-permute-done.4.near1), custom_call_target="tpu_custom_call" | custom-call | tf_op jit(solution)/shard_map/pallas_call | solution.py:32
  80.7 7.4 %all-to-all-start.3 = ((f32[16,40,128]{2,1,0:T(8,128)}), f32[16,40,128]{2,1,0:T(8,128)S(1)}, u32[]{:S(2)}, u32[]{:S(2)}) async-start(f32[16,40,128]{2,1,0:T(8,128)} %bitcast.10), calls=%async_computation.3 | async-start | bytes 655360 | tf_op jit(solution)/shard_map/all_to_all | solution.py:315
  88.1 1.1 shard_map.66.inner
  89.2 7.9 %all-to-all-done.3 = f32[16,40,128]{2,1,0:T(8,128)S(1)} async-done(((f32[16,40,128]{2,1,0:T(8,128)}), f32[16,40,128]{2,1,0:T(8,128)S(1)}, u32[]{:S(2)}, u32[]{:S(2)}) %all-to-all-start.3) | async-done | bytes 327712 | tf_op jit(solution)/shard_map/all_to_all | solution.py:315
  97.2 0.7 broadcast_in_dim.31
  97.9 4.6 %all-to-all-start.4 = ((f32[16,40,128]{2,1,0:T(8,128)}), f32[16,40,128]{2,1,0:T(8,128)S(1)}, u32[]{:S(2)}, u32[]{:S(2)}) async-start(f32[16,40,128]{2,1,0:T(8,128)} %broadcast_in_dim.31), calls=%async_computation.4 | async-start | bytes 655360 | tf_op jit(solution)/shard_map/all_to_all | solution.py:315
  102.7 5.6 %collective-permute-start.5 = (f32[384,128]{1,0:T(8,128)S(1)}, f32[384,128]{1,0:T(8,128)S(1)}, u32[]{:S(2)}, u32[]{:S(2)}) collective-permute-start(f32[384,128]{1,0:T(8,128)S(1)} %pad_maximum_fusion.6), channel_id=1, source_target_pairs={{0,1},{1,2},{2,3},{3,4},{4,5},{5,6},{6,7},{7,0},{8,15},{9,8},{10,9... | collective-permute-start | bytes 589832 | tf_op jit(solution)/shard_map/ppermute | solution.py:333
  108.2 0.1 copy.12
  108.4 0.1 copy.13
  108.5 0.4 copy-done.5
  108.9 2.3 %collective-permute-done.6 = f32[384,128]{1,0:T(8,128)S(1)} collective-permute-done((f32[384,128]{1,0:T(8,128)S(1)}, f32[384,128]{1,0:T(8,128)S(1)}, u32[]{:S(2)}, u32[]{:S(2)}) %collective-permute-start.6) | collective-permute-done | bytes 196640 | tf_op jit(solution)/shard_map/ppermute | solution.py:333
  111.2 0.7 copy-done.3
  111.9 0.7 copy-done.4
  112.6 0.9 slice-done
  113.5 0.9 slice-done.1
  114.4 15.2 %shard_map.67 = (f32[256,256]{1,0:T(8,128)S(1)}, f32[128,256]{1,0:T(8,128)S(1)}, f32[384,256]{1,0:T(8,128)S(1)}) custom-call(f32[5,128,128]{2,1,0:T(8,128)S(1)} %bitcast.25, f32[3,128,128]{2,1,0:T(8,128)S(1)} %shard_map.66.inner, f32[128,128]{1,0:T(8,128)S(1)} %slice.116.far00, f32[128,128]{1,0:T(8,128)S(1)} %slice.118.near11, ...), custom_call_target="tpu_custom_call" | custom-call | tf_op jit(solution)/shard_map/pallas_call | solution.py:32
  129.7 13.0 %collective-permute-start.7 = (f32[384,256]{1,0:T(8,128)S(1)}, f32[384,256]{1,0:T(8,128)S(1)}, u32[]{:S(2)}, u32[]{:S(2)}) collective-permute-start(f32[384,256]{1,0:T(8,128)S(1)} %get-tuple-element.21), channel_id=1, source_target_pairs={{0,8},{8,0},{16,24},{24,16},{32,40},{40,32},{48,56},{56,48},{64,72... | collective-permute-start | bytes 1179656 | tf_op jit(solution)/shard_map/ppermute | solution.py:323
  142.6 1.3 collective-permute-done.7
  144.0 0.7 maximum_select_fusion.1
  144.7 0.8 maximum_select_fusion
  (48 shorter events, 0.8 us)
Async XLA Ops:
  0.6 0.7 copy-start.7
  2.5 1.9 %collective-permute-start = (f32[256,256]{1,0:T(8,128)S(1)}, f32[256,256]{1,0:T(8,128)S(1)}, u32[]{:S(2)}, u32[]{:S(2)}) collective-permute-start(f32[256,256]{1,0:T(8,128)S(1)} %get-tuple-element.28), channel_id=1, source_target_pairs={{0,8},{8,0},{16,24},{24,16},{32,40},{40,32},{48,56},{56,48},{64,72... | collective-permute-start | bytes 786440 | tf_op jit(solution)/shard_map/ppermute | solution.py:323
  4.5 12.2 %collective-permute-start.1 = (f32[512,256]{1,0:T(8,128)S(1)}, f32[512,256]{1,0:T(8,128)S(1)}, u32[]{:S(2)}, u32[]{:S(2)}) collective-permute-start(f32[512,256]{1,0:T(8,128)S(1)} %pad_maximum_fusion.2.x), channel_id=1, source_target_pairs={{0,7},{1,0},{2,1},{3,2},{4,3},{5,4},{6,5},{7,6},{8,9},{9,10},{10,1... | collective-permute-start | bytes 1572872 | tf_op jit(solution)/shard_map/ppermute | solution.py:333
  7.3 17.6 %all-to-all-start = ((f32[16,24,128]{2,1,0:T(8,128)}), f32[16,24,128]{2,1,0:T(8,128)S(1)}, u32[]{:S(2)}, u32[]{:S(2)}) async-start(f32[16,24,128]{2,1,0:T(8,128)} %bitcast), calls=%async_computation | async-start | bytes 393216 | tf_op jit(solution)/shard_map/all_to_all | solution.py:315
  25.7 4.5 %copy-start.2 = (f32[256,512]{1,0:T(8,128)S(1)}, f32[256,512]{1,0:T(8,128)}, u32[]{:S(2)}) copy-start(f32[256,512]{1,0:T(8,128)} %constant.68.clone) | copy-start | bytes 1572868
  25.7 4.5 %copy-start.6 = (s32[4,256]{1,0:T(4,128)S(1)}, s32[4,256]{1,0:T(4,128)}, u32[]{:S(2)}) copy-start(s32[4,256]{1,0:T(4,128)} %param.6) | copy-start | bytes 12292
  25.7 14.8 %all-to-all-start.1 = ((f32[16,56,128]{2,1,0:T(8,128)}), f32[16,56,128]{2,1,0:T(8,128)S(1)}, u32[]{:S(2)}, u32[]{:S(2)}) async-start(f32[16,56,128]{2,1,0:T(8,128)} %shard_map.61), calls=%async_computation.1 | async-start | bytes 917504 | tf_op jit(solution)/shard_map/all_to_all | solution.py:315
  41.2 21.7 %all-to-all-start.2 = ((f32[16,32,128]{2,1,0:T(8,128)}), f32[16,32,128]{2,1,0:T(8,128)S(1)}, u32[]{:S(2)}, u32[]{:S(2)}) async-start(f32[16,32,128]{2,1,0:T(8,128)} %broadcast_in_dim.28), calls=%async_computation.2 | async-start | bytes 524288 | tf_op jit(solution)/shard_map/all_to_all | solution.py:315
  50.5 12.4 %collective-permute-start.2 = (f32[384,128]{1,0:T(8,128)S(1)}, f32[384,128]{1,0:T(8,128)S(1)}, u32[]{:S(2)}, u32[]{:S(2)}) collective-permute-start(f32[384,128]{1,0:T(8,128)S(1)} %get-tuple-element.14), channel_id=1, source_target_pairs={{0,7},{1,0},{2,1},{3,2},{4,3},{5,4},{6,5},{7,6},{8,9},{9,10},{10,1... | collective-permute-start | bytes 589832 | tf_op jit(solution)/shard_map/ppermute | solution.py:333
  56.7 0.6 copy-start
  62.9 0.8 copy-start.1
  69.7 9.1 %collective-permute-start.4 = (f32[512,128]{1,0:T(8,128)S(1)}, f32[512,128]{1,0:T(8,128)S(1)}, u32[]{:S(2)}, u32[]{:S(2)}) collective-permute-start(f32[512,128]{1,0:T(8,128)S(1)} %slice.92.x1), channel_id=1, source_target_pairs={{0,7},{1,0},{2,1},{3,2},{4,3},{5,4},{6,5},{7,6},{8,9},{9,10},{10,1... | collective-permute-start | bytes 786440 | tf_op jit(solution)/shard_map/ppermute | solution.py:333
  70.0 8.8 %collective-permute-start.3 = (f32[512,128]{1,0:T(8,128)S(1)}, f32[512,128]{1,0:T(8,128)S(1)}, u32[]{:S(2)}, u32[]{:S(2)}) collective-permute-start(f32[512,128]{1,0:T(8,128)S(1)} %slice.91.x0), channel_id=1, source_target_pairs={{0,1},{1,2},{2,3},{3,4},{4,5},{5,6},{6,7},{7,0},{8,15},{9,8},{10,9... | collective-permute-start | bytes 786440 | tf_op jit(solution)/shard_map/ppermute | solution.py:333
  80.7 16.4 %all-to-all-start.3 = ((f32[16,40,128]{2,1,0:T(8,128)}), f32[16,40,128]{2,1,0:T(8,128)S(1)}, u32[]{:S(2)}, u32[]{:S(2)}) async-start(f32[16,40,128]{2,1,0:T(8,128)} %bitcast.10), calls=%async_computation.3 | async-start | bytes 655360 | tf_op jit(solution)/shard_map/all_to_all | solution.py:315
  97.9 16.4 %all-to-all-start.4 = ((f32[16,40,128]{2,1,0:T(8,128)}), f32[16,40,128]{2,1,0:T(8,128)S(1)}, u32[]{:S(2)}, u32[]{:S(2)}) async-start(f32[16,40,128]{2,1,0:T(8,128)} %broadcast_in_dim.31), calls=%async_computation.4 | async-start | bytes 655360 | tf_op jit(solution)/shard_map/all_to_all | solution.py:315
  102.6 8.6 %collective-permute-start.6 = (f32[384,128]{1,0:T(8,128)S(1)}, f32[384,128]{1,0:T(8,128)S(1)}, u32[]{:S(2)}, u32[]{:S(2)}) collective-permute-start(f32[384,128]{1,0:T(8,128)S(1)} %pad_maximum_fusion.7), channel_id=1, source_target_pairs={{0,7},{1,0},{2,1},{3,2},{4,3},{5,4},{6,5},{7,6},{8,9},{9,10},{10,1... | collective-permute-start | bytes 589832 | tf_op jit(solution)/shard_map/ppermute | solution.py:333
  102.7 9.2 %collective-permute-start.5 = (f32[384,128]{1,0:T(8,128)S(1)}, f32[384,128]{1,0:T(8,128)S(1)}, u32[]{:S(2)}, u32[]{:S(2)}) collective-permute-start(f32[384,128]{1,0:T(8,128)S(1)} %pad_maximum_fusion.6), channel_id=1, source_target_pairs={{0,1},{1,2},{2,3},{3,4},{4,5},{5,6},{6,7},{7,0},{8,15},{9,8},{10,9... | collective-permute-start | bytes 589832 | tf_op jit(solution)/shard_map/ppermute | solution.py:333
  108.2 0.7 copy-start.5
  111.2 0.7 copy-start.3
  111.9 0.7 copy-start.4
  112.6 0.9 slice-start
  113.5 0.9 slice-start.1
  129.7 14.3 %collective-permute-start.7 = (f32[384,256]{1,0:T(8,128)S(1)}, f32[384,256]{1,0:T(8,128)S(1)}, u32[]{:S(2)}, u32[]{:S(2)}) collective-permute-start(f32[384,256]{1,0:T(8,128)S(1)} %get-tuple-element.21), channel_id=1, source_target_pairs={{0,8},{8,0},{16,24},{24,16},{32,40},{40,32},{48,56},{56,48},{64,72... | collective-permute-start | bytes 1179656 | tf_op jit(solution)/shard_map/ppermute | solution.py:323

commit v4 on v3

--- a/solution.py
+++ b/solution.py
@@ -85,6 +85,12 @@
 def pick_rows(units, x):
     high, middle, low = thirds(x)
     return dot_16(units, high) + (dot_16(units, middle) + dot_16(units, low))
+
+
+def dot_3(left, right):
+    l_high, l_low, _ = thirds(left)
+    r_high, r_low, _ = thirds(right)
+    return dot_16(l_high, r_high) + (dot_16(l_high, r_low) + dot_16(l_low, r_high))
 
 
 def turn(p, q, c, s):
@@ -182,11 +188,7 @@
         state = [one_round(0, 1, k, *state[k]) for k in range(count)]
         return [one_round(1, 0, k, *state[k]) for k in range(count)]
 
-    if count == 1:
-        lax.fori_loop(0, ROUNDS // 2, two_rounds, state)
-    else:
-        for pair in range(ROUNDS // 2):
-            state = two_rounds(pair, state)
+    lax.fori_loop(0, ROUNDS // 2, two_rounds, state)
     turned = [
         [jnp.concatenate([top[0, k, body], bottom[0, k, body]], axis=0).T for k in range(count)]
         for top, bottom in ((qa, qc), (qb, qd))
@@ -197,14 +199,25 @@
     ]
 
 
+def start_kernel(sample, scale, swapped, own, send):
+    x = sample[...] * scale[...]
+    blocks = [x[:, k * BLOCK : (k + 1) * BLOCK] for k in range(4)]
+    swap = swapped[...] > 0.0
+    for k, far in ((0, 3), (1, 2)):
+        at = slice(k * BLOCK, (k + 1) * BLOCK)
+        own[:, at] = jnp.where(swap, blocks[far], blocks[k])
+        send[:, at] = jnp.where(swap, blocks[k], blocks[far])
+
+
 def gram_kernel(own, other, out):
     x = jnp.concatenate([own[...], other[...]], axis=0)
-    x0, x1 = x[:, :BLOCK], x[:, BLOCK:]
-    out[0], out[1], out[2] = dot_t(x0, x0), dot_t(x0, x1), dot_t(x1, x1)
-
-
-def mixed_kernel(x, near, out):
-    mixed = dot_t(x[...], near[...])
+    gram = dot_t(x, x)
+    out[0], out[1], out[2] = gram[:BLOCK, :BLOCK], gram[:BLOCK, BLOCK:], gram[BLOCK:, BLOCK:]
+
+
+def mixed_kernel(own, other, near, out):
+    x = jnp.concatenate([own[...], other[...]], axis=0)
+    mixed = dot_t(x, near[...])
     out[0], out[1] = mixed[:, :BLOCK], mixed[:, BLOCK:]
 
 
@@ -232,15 +245,16 @@
     ship[N:] = dot_t(q1, dot(gram, q1))
 
 
-def keep_kernel(landed, q, x, g00, kept):
+def keep_kernel(landed, q, own, other, unit, g00, kept, kept_basis):
     q0 = q[:, :BLOCK]
-    kept[...] = dot(x[...], q0)
+    kept[...] = dot(jnp.concatenate([own[...], other[...]], axis=0), q0)
+    kept_basis[...] = dot(unit[...], q0)
     g00[...] = dot_t(q0, dot(first_gram(landed, 3 * BLOCK // landed.shape[0]), q0))
 
 
 def second_kernel(mixed, q, ship, g00, kept, near, along, down, x0, x1, gram_out, q_out, *scratch):
     q1 = ship[:N]
-    cross = dot_t(q[:, :BLOCK], dot(beside(mixed[0], mixed[1]), q1))
+    cross = dot(q[:, :BLOCK].T, dot(beside(mixed[0], mixed[1]), q1))
     gram = joined(g00[...], cross, ship[N:])
     gram_out[...] = gram
     (turned,) = solves([gram], along[...], down[...], scratch)
@@ -250,29 +264,36 @@
     x1[...] = y[:, BLOCK:]
 
 
-def turned_kernel(gram, q, out):
+def basis_kernel(kept, unit, ship, q, gram, far, near, out):
+    y = dot(beside(kept[...], dot(unit[...], ship[:N])), q[...])
     g = dot_t(q[...], dot(gram[...], q[...]))
-    out[0], out[1], out[2] = g[:BLOCK, :BLOCK], g[:BLOCK, BLOCK:], g[BLOCK:, BLOCK:]
+    rows = y.shape[0]
+    far[:rows], near[:rows] = y[:, :BLOCK], y[:, BLOCK:]
+    far[rows:], near[rows:] = g[:BLOCK, :BLOCK], g[BLOCK:, BLOCK:]
+    out[...] = g[:BLOCK, BLOCK:]
 
 
 def cross_kernel(far0, x0, x1, near1, out):
-    f0, s0, s1, n1 = far0[...], x0[...], x1[...], near1[...]
-    out[0] = dot_t(f0, s1)
-    out[1] = dot_t(s0, n1)
-    out[2] = dot_t(f0, s0)
+    f0, n1 = far0[...], near1[...]
+    both = dot_t(beside(f0, n1), beside(x1[...], x0[...]))
+    out[0] = both[:BLOCK, :BLOCK]
+    out[1] = both[BLOCK:, BLOCK:]
+    out[2] = both[:BLOCK, BLOCK:]
     out[3] = dot_t(f0, n1)
-    out[4] = dot_t(s1, n1)
+    out[4] = both[BLOCK:, :BLOCK]
 
 
 def last_kernel(
     sums,
     inner,
-    far00,
-    near11,
     far0,
     x0,
     x1,
     near1,
+    far_rest,
+    rest0,
+    rest1,
+    near_rest,
     along2,
     down2,
     along3,
@@ -283,18 +304,24 @@
     theirs,
     *scratch,
 ):
-    gram_a = joined(far00[...], sums[0], inner[2])
-    gram_b = joined(inner[0], sums[1], near11[...])
+    basis_rows = far_rest.shape[0] - BLOCK
+    gram_a = joined(far_rest[basis_rows:], sums[0], rest1[basis_rows:])
+    gram_b = joined(rest0[basis_rows:], sums[1].T, near_rest[basis_rows:])
+    mixed = jnp.concatenate(
+        [beside(sums[2], sums[3]), beside(inner[...].T, sums[4].T)], axis=0
+    )
     qa, qb = solves([gram_a, gram_b], along2[...], down2[...], scratch)
     qa, qb = qa[:, :BLOCK], qb[:, BLOCK:]
-    mixed = jnp.concatenate([beside(sums[2], sums[3]), beside(inner[1].T, sums[4])], axis=0)
-    gram = joined(
-        dot_t(qa, dot(gram_a, qa)), dot_t(qa, dot(mixed, qb)), dot_t(qb, dot(gram_b, qb))
-    )
+    left = dot(qa.T, beside(gram_a, mixed))
+    gram = joined(dot(left[:, :N], qa), dot(left[:, N:], qb), dot(dot(qb.T, gram_b), qb))
     (q,) = solves([gram], along3[...], down3[...], scratch)
-    ya = dot(beside(far0[...], x1[...]), qa)
-    yb = dot(beside(x0[...], near1[...]), qb)
-    y = dot(beside(ya, yb), q)
+
+    def whole(data, rest):
+        return jnp.concatenate([data[...], rest[:basis_rows]], axis=0)
+
+    ya = dot_3(beside(whole(far0, far_rest), whole(x1, rest1)), qa)
+    yb = dot_3(beside(whole(x0, rest0), whole(near1, near_rest)), qb)
+    y = dot_3(beside(ya, yb), q)
     swap = swapped[...] > 0.0
     y = beside(
         jnp.where(swap, y[:, BLOCK:], y[:, :BLOCK]), jnp.where(swap, y[:, :BLOCK], y[:, BLOCK:])
@@ -304,6 +331,18 @@
     theirs[:rows] = y[rows : 2 * rows]
     mine_basis[...] = y[2 * rows : 2 * rows + height]
     theirs[rows:] = y[2 * rows + height :]
+
+
+def place_kernel(got, mine_data, mine_basis, swapped, data, basis):
+    swap = swapped[...] > 0.0
+    swap = beside(swap, swap)
+    rows = mine_data.shape[0]
+    for mine, theirs, out in (
+        (mine_data[...], got[:rows], data),
+        (mine_basis[...], got[rows:], basis),
+    ):
+        out[:, :N] = jnp.where(swap, mine, theirs)
+        out[:, N:] = jnp.where(swap, theirs, mine)
 
 
 def chip_groups(size):
@@ -336,26 +375,27 @@
 def body(sample, column_scale, inner_order):
     row, col = lax.axis_index("rows"), lax.axis_index("pairs")
     core = row % 2
-    first = core == 0
     n_pairs = lax.axis_size("pairs")
-    data = sample * column_scale[None, :]
-    rows = data.shape[0]
-    left, right = data[:, :N], data[:, N:]
-    own = jnp.where(first, left, beside(right[:, BLOCK:], right[:, :BLOCK]))
-    send = jnp.where(first, beside(right[:, BLOCK:], right[:, :BLOCK]), left)
-    got = other_core(send)
-    x = jnp.concatenate([own, got], axis=0)
-    near = along_pairs(x, 1)
-    near_col = (col + jnp.where(first, 1, -1)) % n_pairs
-
+    rows, width = sample.shape
     height = W // lax.axis_size("rows")
+    swapped = jnp.full((1, BLOCK), core, jnp.float32)
+    own, send = call(
+        start_kernel,
+        (shape(rows, N), shape(rows, N)),
+        [],
+        sample,
+        column_scale.reshape(1, width),
+        swapped,
+    )
+    other = other_core(send)
+    near = along_pairs(jnp.concatenate([own, other], axis=0), 1)
+    near_col = (col + jnp.where(core == 0, 1, -1)) % n_pairs
+
     ids = jnp.arange(height, dtype=jnp.int32)
     row_ids = jnp.concatenate([ids + row * height, ids + (row ^ 1) * height])[:, None]
     places = (jnp.arange(N, dtype=jnp.int32)[None, :] + core * BLOCK) % N + core * N
-
-    def with_basis(values, at):
-        unit = jnp.where(row_ids == places + 2 * N * at, 1.0, 0.0).astype(jnp.float32)
-        return jnp.concatenate([values, unit])
+    unit = jnp.where(row_ids == places + 2 * N * col, 1.0, 0.0).astype(jnp.float32)
+    near_unit = jnp.where(row_ids == places + 2 * N * near_col, 1.0, 0.0).astype(jnp.float32)
 
     order = ((inner_order + core * BLOCK) % N).astype(jnp.float32)
     table = np.concatenate([np.eye(N)[:, arrangement(0)], np.eye(N)[:, arrangement(ROUNDS)]], 1)
@@ -366,15 +406,20 @@
 
     chips = lax.axis_size("rows") // 2
     gram_rows, mixed_rows = 3 * BLOCK // chips, 2 * N // chips
-    parts = trade(call(gram_kernel, shape(3, BLOCK, BLOCK), [], own, got).reshape(chips, -1, BLOCK))
-    mixed = call(mixed_kernel, shape(2, N, BLOCK), [], x, near).reshape(chips, -1, BLOCK)
+    gram = call(gram_kernel, shape(3, BLOCK, BLOCK), [], own, other)
+    parts = trade(gram.reshape(chips, -1, BLOCK))
+    mixed = call(mixed_kernel, shape(2, N, BLOCK), [], own, other, near)
     landed = trade(
-        call(spread_kernel, shape(chips, gram_rows + mixed_rows, BLOCK), [], parts, mixed)
+        call(
+            spread_kernel,
+            shape(chips, gram_rows + mixed_rows, BLOCK),
+            [],
+            parts,
+            mixed.reshape(chips, -1, BLOCK),
+        )
     )
     mixed = all_slices(landed[:, gram_rows:].sum(0), chips).reshape(2, N, BLOCK)
 
-    x, near = with_basis(x, col), with_basis(near, near_col)
-    total = x.shape[0]
     q, ship = call(
         first_kernel,
         (shape(N, N), shape(N + BLOCK, BLOCK)),
@@ -384,8 +429,17 @@
         down[0],
     )
     ship = along_pairs(ship, 1)
-    g00, kept = call(keep_kernel, (shape(BLOCK, BLOCK), shape(total, BLOCK)), [], landed, q, x)
-    half = shape(total, BLOCK)
+    half, half_basis = shape(2 * rows, BLOCK), shape(2 * height, BLOCK)
+    g00, kept, kept_basis = call(
+        keep_kernel,
+        (shape(BLOCK, BLOCK), half, half_basis),
+        [],
+        landed,
+        q,
+        own,
+        other,
+        unit,
+    )
     x0, x1, gram, q = call(
         second_kernel,
         (half, half, shape(N, N), shape(N, N)),
@@ -400,43 +454,51 @@
         down[1],
     )
 
-    both = 2 * rows
-    far0, near1 = along_pairs(x0[:both], -1), along_pairs(x1[:both], 1)
-    cross = call(
-        cross_kernel, shape(5, BLOCK, BLOCK), [], far0, x0[:both], x1[:both], near1
-    )
+    far0, near1 = along_pairs(x0, -1), along_pairs(x1, 1)
+    rest = shape(2 * height + BLOCK, BLOCK)
+    rest0, rest1, inner = call(
+        basis_kernel,
+        (rest, rest, shape(BLOCK, BLOCK)),
+        [],
+        kept_basis,
+        near_unit,
+        ship,
+        q,
+        gram,
+    )
+    cross = call(cross_kernel, shape(5, BLOCK, BLOCK), [], far0, x0, x1, near1)
     sums = trade(cross.reshape(chips, -1, BLOCK)).sum(0)
-    inner = call(turned_kernel, shape(3, BLOCK, BLOCK), [], gram, q)
-    far_rest = along_pairs(jnp.concatenate([x0[both:], inner[0]]), -1)
-    near_rest = along_pairs(jnp.concatenate([x1[both:], inner[2]]), 1)
+    far_rest, near_rest = along_pairs(rest0, -1), along_pairs(rest1, 1)
     sums = all_slices(sums, chips).reshape(5, BLOCK, BLOCK)
-    cut = 2 * height
-    far0 = jnp.concatenate([far0, far_rest[:cut]])
-    near1 = jnp.concatenate([near1, near_rest[:cut]])
     mine_data, mine_basis, theirs = call(
         last_kernel,
         (shape(rows, N), shape(height, N), shape(rows + height, N)),
         solve_scratch(2),
         sums,
         inner,
-        far_rest[cut:],
-        near_rest[cut:],
         far0,
         x0,
         x1,
         near1,
+        far_rest,
+        rest0,
+        rest1,
+        near_rest,
         along[2],
         down[2],
         along[3],
         down[3],
-        jnp.full((1, BLOCK), core, jnp.float32),
-    )
-    got = other_core(theirs)
-
-    def placed(got, mine):
-        return jnp.where(first, beside(got, mine), beside(mine, got))
-
-    return placed(got[:rows], mine_data), placed(got[rows:], mine_basis)
+        swapped,
+    )
+    return call(
+        place_kernel,
+        (shape(rows, width), shape(height, width)),
+        [],
+        other_core(theirs),
+        mine_data,
+        mine_basis,
+        swapped,
+    )
 
 
 def solution(mesh):

time: 146 us -> 134 us (0.918)
  the two profiles are of different devices: /device:TPU:25 before, /device:TPU:7 now
where the time goes in v4:
time: 134 us; the launch traced here: 133 us
  starting transfers between devices  46.2 us (34%)
  waiting for transfers between devices  36.2 us (27%)
  Pallas kernels  26.1 us (19%)
  blocking collectives  15.3 us (11%)
  local copies, waits for them, and re-layouts  7.74 us (6%)
    pallas_call x11, Pallas kernels, call(): pl.pallas_call(kernel, out_shape=out_shape, in_specs=[VMEM] * len(operand...  26.1 us
    all_to_all x4, waiting for transfers between devices, trade(): return lax.all_to_all(parts, 'rows', 0, 0, axis_index_groups=groups)  24.2 us
    all_to_all x4, starting transfers between devices, trade(): return lax.all_to_all(parts, 'rows', 0, 0, axis_index_groups=groups)  19.7 us
    all_to_all x1, blocking collectives, trade(): return lax.all_to_all(parts, 'rows', 0, 0, axis_index_groups=groups)  15.3 us
    ppermute x6, starting transfers between devices, along_pairs(): return lax.ppermute(x, ('rows', 'pairs'), route)  14.8 us
    ppermute x2, starting transfers between devices, other_core(): lax.ppermute(x, 'rows', [(i, i ^ 1) for i in range(lax.axis_size('rows'))])  11.7 us
    ppermute x6, waiting for transfers between devices, along_pairs(): return lax.ppermute(x, ('rows', 'pairs'), route)  9.43 us
    unnamed x20, local copies, waits for them, and re-layouts  5.58 us
  transfers between devices with their start and end apart: 12, of which 9 were waited for; matrix products, arithmetic and copies ran while one was open for 1% of the time, Pallas kernels for 6%

profile of v4, /device:TPU:7, one launch (start us, length us, event | category | flops | bytes accessed | tf_op | source)
XLA Modules:
  0.0 133.0 jit_solution(7082601968454031837)
XLA Ops:
  0.7 0.7 copy-done.3
  1.3 1.0 copy-done
  2.4 0.8 collective-permute-start
  3.2 1.2 collective-permute-done.other
  4.4 2.9 %collective-permute-start.1 = (f32[512,256]{1,0:T(8,128)S(1)}, f32[512,256]{1,0:T(8,128)S(1)}, u32[]{:S(2)}, u32[]{:S(2)}) collective-permute-start(f32[512,256]{1,0:T(8,128)S(1)} %pad_maximum_fusion), channel_id=1, source_target_pairs={{0,7},{1,0},{2,1},{3,2},{4,3},{5,4},{6,5},{7,6},{8,9},{9,10},{10,1... | collective-permute-start | bytes 1572872 | tf_op jit(solution)/shard_map/ppermute | solution.py:372
  7.3 1.4 %shard_map.60 = f32[3,128,128]{2,1,0:T(8,128)} custom-call(f32[256,256]{1,0:T(8,128)S(1)} %get-tuple-element.19.own, f32[256,256]{1,0:T(8,128)S(1)} %collective-permute-done.other), custom_call_target="tpu_custom_call" | custom-call | tf_op jit(solution)/shard_map/pallas_call | solution.py:32
  8.7 8.4 %all-to-all-start = ((f32[16,24,128]{2,1,0:T(8,128)}), f32[16,24,128]{2,1,0:T(8,128)S(1)}, u32[]{:S(2)}, u32[]{:S(2)}) async-start(f32[16,24,128]{2,1,0:T(8,128)} %bitcast.1), calls=%async_computation | async-start | bytes 393216 | tf_op jit(solution)/shard_map/all_to_all | solution.py:354
  17.1 0.7 shard_map.61
  17.8 10.3 %all-to-all-done.parts = f32[16,24,128]{2,1,0:T(8,128)S(1)} async-done(((f32[16,24,128]{2,1,0:T(8,128)}), f32[16,24,128]{2,1,0:T(8,128)S(1)}, u32[]{:S(2)}, u32[]{:S(2)}) %all-to-all-start) | async-done | bytes 196640 | tf_op jit(solution)/shard_map/all_to_all | solution.py:354
  28.1 0.8 shard_map.62
  29.0 3.7 %all-to-all-start.1 = ((f32[16,56,128]{2,1,0:T(8,128)}), f32[16,56,128]{2,1,0:T(8,128)S(1)}, u32[]{:S(2)}, u32[]{:S(2)}) async-start(f32[16,56,128]{2,1,0:T(8,128)} %shard_map.62), calls=%async_computation.1 | async-start | bytes 917504 | tf_op jit(solution)/shard_map/all_to_all | solution.py:354
  32.7 0.7 copy-done.7
  33.3 0.4 fusion.2
  33.7 0.6 slice_reduce_fusion.1
  34.3 13.2 %all-to-all-done.1.landed = f32[16,56,128]{2,1,0:T(8,128)S(1)} async-done(((f32[16,56,128]{2,1,0:T(8,128)}), f32[16,56,128]{2,1,0:T(8,128)S(1)}, u32[]{:S(2)}, u32[]{:S(2)}) %all-to-all-start.1) | async-done | bytes 458784 | tf_op jit(solution)/shard_map/all_to_all | solution.py:354
  47.6 0.7 broadcast_in_dim.28
  48.3 4.0 %all-to-all-start.2 = ((f32[16,32,128]{2,1,0:T(8,128)}), f32[16,32,128]{2,1,0:T(8,128)S(1)}, u32[]{:S(2)}, u32[]{:S(2)}) async-start(f32[16,32,128]{2,1,0:T(8,128)} %broadcast_in_dim.28), calls=%async_computation.2 | async-start | bytes 524288 | tf_op jit(solution)/shard_map/all_to_all | solution.py:354
  52.4 0.1 copy.10
  52.6 0.1 copy.11
  52.8 3.7 %shard_map.63 = (f32[256,256]{1,0:T(8,128)S(1)}, f32[384,128]{1,0:T(8,128)S(1)}) custom-call(f32[16,56,128]{2,1,0:T(8,128)S(1)} %all-to-all-done.1.landed, f32[2,256]{1,0:T(2,128)S(1)} %squeeze.24.along, f32[256,2]{1,0:T(8,128)S(1)} %bitcast.28), custom_call_target="tpu_custom_call" | custom-call | tf_op jit(solution)/shard_map/pallas_call | solution.py:32
  56.5 0.1 collective-permute-start.2
  56.6 0.1 compare_select_fusion
  56.7 1.2 shard_map.64
  58.0 0.6 copy-done.1
  58.6 2.8 %collective-permute-done.2.ship = f32[384,128]{1,0:T(8,128)S(1)} collective-permute-done((f32[384,128]{1,0:T(8,128)S(1)}, f32[384,128]{1,0:T(8,128)S(1)}, u32[]{:S(2)}, u32[]{:S(2)}) %collective-permute-start.2) | collective-permute-done | bytes 196640 | tf_op jit(solution)/shard_map/ppermute | solution.py:372
  61.4 0.7 all-to-all-done.2
  62.1 0.8 copy-done.2
  62.9 5.1 %shard_map.65 = (f32[512,128]{1,0:T(8,128)S(1)}, f32[512,128]{1,0:T(8,128)S(1)}, f32[256,256]{1,0:T(8,128)S(1)}, f32[256,256]{1,0:T(8,128)S(1)}) custom-call(f32[2,256,128]{2,1,0:T(8,128)S(1)} %bitcast.25, f32[256,256]{1,0:T(8,128)S(1)} %get-tuple-element.21.q, f32[384,128]{1,0:T(8,128)S(1)} %collective-permute-done.2.ship, f32[128,128]{1,0:T(8,128)S(1)} %copy-done.2, ...), custom_call_target="tpu_custom_call" | custom-call | tf_op jit(solution)/shard_map/pallas_call | solution.py:32
  68.0 0.1 collective-permute-start.3
  68.1 5.1 %collective-permute-start.4 = (f32[512,128]{1,0:T(8,128)S(1)}, f32[512,128]{1,0:T(8,128)S(1)}, u32[]{:S(2)}, u32[]{:S(2)}) collective-permute-start(f32[512,128]{1,0:T(8,128)S(1)} %get-tuple-element.26.x1), channel_id=1, source_target_pairs={{0,7},{1,0},{2,1},{3,2},{4,3},{5,4},{6,5},{7,6},{8,9},{9,10},{10,1... | collective-permute-start | bytes 786440 | tf_op jit(solution)/shard_map/ppermute | solution.py:372
  73.2 3.8 %collective-permute-done.3.far0 = f32[512,128]{1,0:T(8,128)S(1)} collective-permute-done((f32[512,128]{1,0:T(8,128)S(1)}, f32[512,128]{1,0:T(8,128)S(1)}, u32[]{:S(2)}, u32[]{:S(2)}) %collective-permute-start.3) | collective-permute-done | bytes 262176 | tf_op jit(solution)/shard_map/ppermute | solution.py:372
  77.0 1.4 %collective-permute-done.4.near1 = f32[512,128]{1,0:T(8,128)S(1)} collective-permute-done((f32[512,128]{1,0:T(8,128)S(1)}, f32[512,128]{1,0:T(8,128)S(1)}, u32[]{:S(2)}, u32[]{:S(2)}) %collective-permute-start.4) | collective-permute-done | bytes 262176 | tf_op jit(solution)/shard_map/ppermute | solution.py:372
  78.4 0.8 shard_map.66
  79.2 15.3 %all_to_all.25 = f32[16,40,128]{2,1,0:T(8,128)S(1)} all-to-all(f32[16,40,128]{2,1,0:T(8,128)S(1)} %bitcast.22), channel_id=1, replica_groups={{0,16,32,48,64,80,96,112,128,144,160,176,192,208,224,240},{8,24,40,56,7..., dimensions={0} | all-to-all | bytes 655360 | tf_op jit(solution)/shard_map/all_to_all | solution.py:354
  94.5 0.7 broadcast_in_dim.31
  95.3 3.5 %all-to-all-start.4 = ((f32[16,40,128]{2,1,0:T(8,128)}), f32[16,40,128]{2,1,0:T(8,128)S(1)}, u32[]{:S(2)}, u32[]{:S(2)}) async-start(f32[16,40,128]{2,1,0:T(8,128)} %broadcast_in_dim.31), calls=%async_computation.4 | async-start | bytes 655360 | tf_op jit(solution)/shard_map/all_to_all | solution.py:354
  98.8 1.5 %shard_map.67 = (f32[384,128]{1,0:T(8,128)S(1)}, f32[384,128]{1,0:T(8,128)S(1)}, f32[128,128]{1,0:T(8,128)S(1)}) custom-call(f32[256,128]{1,0:T(8,128)S(1)} %get-tuple-element.27.kept, f32[256,256]{1,0:T(8,128)S(1)} %get-tuple-element.44.unit, f32[384,128]{1,0:T(8,128)S(1)} %collective-permute-done.2.ship, f32[256,256]{1,0:T(8,128)S(1)} %get-tuple-element.28.q, ...), custom_call_target="tpu_custom_call" | custom-call | tf_op jit(solution)/shard_map/pallas_call | solution.py:32
  100.3 0.1 collective-permute-start.5
  100.4 6.5 %collective-permute-start.6 = (f32[384,128]{1,0:T(8,128)S(1)}, f32[384,128]{1,0:T(8,128)S(1)}, u32[]{:S(2)}, u32[]{:S(2)}) collective-permute-start(f32[384,128]{1,0:T(8,128)S(1)} %get-tuple-element.32.rest1), channel_id=1, source_target_pairs={{0,7},{1,0},{2,1},{3,2},{4,3},{5,4},{6,5},{7,6},{8,9},{9,10},{10,1... | collective-permute-start | bytes 589832 | tf_op jit(solution)/shard_map/ppermute | solution.py:372
  106.9 0.1 copy.12
  107.1 0.1 copy.13
  107.2 0.5 copy-done.6
  107.8 0.7 copy-done.5
  108.5 1.4 %collective-permute-done.5.far_rest = f32[384,128]{1,0:T(8,128)S(1)} collective-permute-done((f32[384,128]{1,0:T(8,128)S(1)}, f32[384,128]{1,0:T(8,128)S(1)}, u32[]{:S(2)}, u32[]{:S(2)}) %collective-permute-start.5) | collective-permute-done | bytes 196640 | tf_op jit(solution)/shard_map/ppermute | solution.py:372
  109.9 9.8 %shard_map.68 = (f32[256,256]{1,0:T(8,128)S(1)}, f32[128,256]{1,0:T(8,128)S(1)}, f32[384,256]{1,0:T(8,128)S(1)}) custom-call(f32[5,128,128]{2,1,0:T(8,128)S(1)} %bitcast.23, f32[128,128]{1,0:T(8,128)S(1)} %get-tuple-element.30.inner, f32[512,128]{1,0:T(8,128)S(1)} %collective-permute-done.3.far0, f32[512,128]{1,0:T(8,128)S(1)} %get-tuple-element.25.x0, ...), custom_call_target="tpu_custom_call" | custom-call | tf_op jit(solution)/shard_map/pallas_call | solution.py:32
  119.7 11.0 %collective-permute-start.7 = (f32[384,256]{1,0:T(8,128)S(1)}, f32[384,256]{1,0:T(8,128)S(1)}, u32[]{:S(2)}, u32[]{:S(2)}) collective-permute-start(f32[384,256]{1,0:T(8,128)S(1)} %get-tuple-element.33), channel_id=1, source_target_pairs={{0,8},{8,0},{16,24},{24,16},{32,40},{40,32},{48,56},{56,48},{64,72... | collective-permute-start | bytes 1179656 | tf_op jit(solution)/shard_map/ppermute | solution.py:362
  130.7 1.3 %collective-permute-done.7.got = f32[384,256]{1,0:T(8,128)S(1)} collective-permute-done((f32[384,256]{1,0:T(8,128)S(1)}, f32[384,256]{1,0:T(8,128)S(1)}, u32[]{:S(2)}, u32[]{:S(2)}) %collective-permute-start.7) | collective-permute-done | bytes 393248 | tf_op jit(solution)/shard_map/ppermute | solution.py:362
  132.0 0.9 shard_map.69
  (25 shorter events, 0.3 us)
Async XLA Ops:
  0.6 0.7 copy-start.3
  1.3 1.0 copy-start
  2.4 1.9 %collective-permute-start = (f32[256,256]{1,0:T(8,128)S(1)}, f32[256,256]{1,0:T(8,128)S(1)}, u32[]{:S(2)}, u32[]{:S(2)}) collective-permute-start(f32[256,256]{1,0:T(8,128)S(1)} %get-tuple-element.20), channel_id=1, source_target_pairs={{0,8},{8,0},{16,24},{24,16},{32,40},{40,32},{48,56},{56,48},{64,72... | collective-permute-start | bytes 786440 | tf_op jit(solution)/shard_map/ppermute | solution.py:362
  4.4 12.7 %collective-permute-start.1 = (f32[512,256]{1,0:T(8,128)S(1)}, f32[512,256]{1,0:T(8,128)S(1)}, u32[]{:S(2)}, u32[]{:S(2)}) collective-permute-start(f32[512,256]{1,0:T(8,128)S(1)} %pad_maximum_fusion), channel_id=1, source_target_pairs={{0,7},{1,0},{2,1},{3,2},{4,3},{5,4},{6,5},{7,6},{8,9},{9,10},{10,1... | collective-permute-start | bytes 1572872 | tf_op jit(solution)/shard_map/ppermute | solution.py:372
  8.7 19.4 %all-to-all-start = ((f32[16,24,128]{2,1,0:T(8,128)}), f32[16,24,128]{2,1,0:T(8,128)S(1)}, u32[]{:S(2)}, u32[]{:S(2)}) async-start(f32[16,24,128]{2,1,0:T(8,128)} %bitcast.1), calls=%async_computation | async-start | bytes 393216 | tf_op jit(solution)/shard_map/all_to_all | solution.py:354
  29.0 3.7 %copy-start.4 = (f32[256,512]{1,0:T(8,128)S(1)}, f32[256,512]{1,0:T(8,128)}, u32[]{:S(2)}) copy-start(f32[256,512]{1,0:T(8,128)} %constant.68.clone) | copy-start | bytes 1572868
  29.0 18.6 %all-to-all-start.1 = ((f32[16,56,128]{2,1,0:T(8,128)}), f32[16,56,128]{2,1,0:T(8,128)S(1)}, u32[]{:S(2)}, u32[]{:S(2)}) async-start(f32[16,56,128]{2,1,0:T(8,128)} %shard_map.62), calls=%async_computation.1 | async-start | bytes 917504 | tf_op jit(solution)/shard_map/all_to_all | solution.py:354
  32.7 0.7 copy-start.7
  48.3 13.8 %all-to-all-start.2 = ((f32[16,32,128]{2,1,0:T(8,128)}), f32[16,32,128]{2,1,0:T(8,128)S(1)}, u32[]{:S(2)}, u32[]{:S(2)}) async-start(f32[16,32,128]{2,1,0:T(8,128)} %broadcast_in_dim.28), calls=%async_computation.2 | async-start | bytes 524288 | tf_op jit(solution)/shard_map/all_to_all | solution.py:354
  56.5 4.9 %collective-permute-start.2 = (f32[384,128]{1,0:T(8,128)S(1)}, f32[384,128]{1,0:T(8,128)S(1)}, u32[]{:S(2)}, u32[]{:S(2)}) collective-permute-start(f32[384,128]{1,0:T(8,128)S(1)} %get-tuple-element.22), channel_id=1, source_target_pairs={{0,7},{1,0},{2,1},{3,2},{4,3},{5,4},{6,5},{7,6},{8,9},{9,10},{10,1... | collective-permute-start | bytes 589832 | tf_op jit(solution)/shard_map/ppermute | solution.py:372
  58.0 0.6 copy-start.1
  62.1 0.8 copy-start.2
  68.0 8.9 %collective-permute-start.3 = (f32[512,128]{1,0:T(8,128)S(1)}, f32[512,128]{1,0:T(8,128)S(1)}, u32[]{:S(2)}, u32[]{:S(2)}) collective-permute-start(f32[512,128]{1,0:T(8,128)S(1)} %get-tuple-element.25.x0), channel_id=1, source_target_pairs={{0,1},{1,2},{2,3},{3,4},{4,5},{5,6},{6,7},{7,0},{8,15},{9,8},{10,9... | collective-permute-start | bytes 786440 | tf_op jit(solution)/shard_map/ppermute | solution.py:372
  68.1 10.2 %collective-permute-start.4 = (f32[512,128]{1,0:T(8,128)S(1)}, f32[512,128]{1,0:T(8,128)S(1)}, u32[]{:S(2)}, u32[]{:S(2)}) collective-permute-start(f32[512,128]{1,0:T(8,128)S(1)} %get-tuple-element.26.x1), channel_id=1, source_target_pairs={{0,7},{1,0},{2,1},{3,2},{4,3},{5,4},{6,5},{7,6},{8,9},{9,10},{10,1... | collective-permute-start | bytes 786440 | tf_op jit(solution)/shard_map/ppermute | solution.py:372
  95.3 14.6 %all-to-all-start.4 = ((f32[16,40,128]{2,1,0:T(8,128)}), f32[16,40,128]{2,1,0:T(8,128)S(1)}, u32[]{:S(2)}, u32[]{:S(2)}) async-start(f32[16,40,128]{2,1,0:T(8,128)} %broadcast_in_dim.31), calls=%async_computation.4 | async-start | bytes 655360 | tf_op jit(solution)/shard_map/all_to_all | solution.py:354
  100.3 9.6 %collective-permute-start.5 = (f32[384,128]{1,0:T(8,128)S(1)}, f32[384,128]{1,0:T(8,128)S(1)}, u32[]{:S(2)}, u32[]{:S(2)}) collective-permute-start(f32[384,128]{1,0:T(8,128)S(1)} %get-tuple-element.31.rest0), channel_id=1, source_target_pairs={{0,1},{1,2},{2,3},{3,4},{4,5},{5,6},{6,7},{7,0},{8,15},{9,8},{10,9... | collective-permute-start | bytes 589832 | tf_op jit(solution)/shard_map/ppermute | solution.py:372
  100.4 9.5 %collective-permute-start.6 = (f32[384,128]{1,0:T(8,128)S(1)}, f32[384,128]{1,0:T(8,128)S(1)}, u32[]{:S(2)}, u32[]{:S(2)}) collective-permute-start(f32[384,128]{1,0:T(8,128)S(1)} %get-tuple-element.32.rest1), channel_id=1, source_target_pairs={{0,7},{1,0},{2,1},{3,2},{4,3},{5,4},{6,5},{7,6},{8,9},{9,10},{10,1... | collective-permute-start | bytes 589832 | tf_op jit(solution)/shard_map/ppermute | solution.py:372
  107.1 0.7 copy-start.6
  107.8 0.7 copy-start.5
  119.7 12.3 %collective-permute-start.7 = (f32[384,256]{1,0:T(8,128)S(1)}, f32[384,256]{1,0:T(8,128)S(1)}, u32[]{:S(2)}, u32[]{:S(2)}) collective-permute-start(f32[384,256]{1,0:T(8,128)S(1)} %get-tuple-element.33), channel_id=1, source_target_pairs={{0,8},{8,0},{16,24},{24,16},{32,40},{40,32},{48,56},{56,48},{64,72... | collective-permute-start | bytes 1179656 | tf_op jit(solution)/shard_map/ppermute | solution.py:362

commit v5 on v4

--- a/solution.py
+++ b/solution.py
@@ -116,12 +116,14 @@
     return c, t * c
 
 
-def solves(grams, along, down, scratch):
+def solves(grams, step, along_ref, down_ref, scratch):
+    along = along_ref[2 * step : 2 * step + 1]
+    down = down_ref[:, 2 * step : 2 * step + 2]
     ga, gb, gc, gd, qa, qb, qc, qd = scratch
     count = len(grams)
     lane = lax.broadcasted_iota(jnp.int32, (N, N), 1).astype(jnp.float32)
     sub = lax.broadcasted_iota(jnp.int32, (N, N), 0).astype(jnp.float32)
-    take = jnp.where(sub == along[0:1, :], 1.0, 0.0).astype(jnp.bfloat16)
+    take = jnp.where(sub == along, 1.0, 0.0).astype(jnp.bfloat16)
     take_t = jnp.where(lane == down[:, 0:1], 1.0, 0.0)
     back_t = jnp.where(lane == down[:, 1:2], 1.0, 0.0).astype(jnp.bfloat16)
     i0 = lax.broadcasted_iota(jnp.int32, (BLOCK, BLOCK), 0)
@@ -199,14 +201,47 @@
     ]
 
 
-def start_kernel(sample, scale, swapped, own, send):
-    x = sample[...] * scale[...]
-    blocks = [x[:, k * BLOCK : (k + 1) * BLOCK] for k in range(4)]
+def start_kernel(sample, scale, swapped, own, send, rows_in, scale_in, sems):
+    steps = sems.shape[0] - 1
+    size = sample.shape[0] // steps
+    copies = [
+        pltpu.make_async_copy(
+            sample.at[pl.ds(k * size, size)], rows_in.at[pl.ds(k * size, size)], sems.at[k]
+        )
+        for k in range(steps)
+    ]
+    scale_copy = pltpu.make_async_copy(scale, scale_in, sems.at[steps])
+    scale_copy.start()
+    for copy in copies:
+        copy.start()
+    scale_copy.wait()
     swap = swapped[...] > 0.0
-    for k, far in ((0, 3), (1, 2)):
-        at = slice(k * BLOCK, (k + 1) * BLOCK)
-        own[:, at] = jnp.where(swap, blocks[far], blocks[k])
-        send[:, at] = jnp.where(swap, blocks[k], blocks[far])
+    for k in range(steps):
+        copies[k].wait()
+        part = pl.ds(k * size, size)
+        x = rows_in[part] * scale_in[...]
+        blocks = [x[:, b * BLOCK : (b + 1) * BLOCK] for b in range(4)]
+        for near, far in ((0, 3), (1, 2)):
+            at = slice(near * BLOCK, (near + 1) * BLOCK)
+            own[part, at] = jnp.where(swap, blocks[far], blocks[near])
+            send[part, at] = jnp.where(swap, blocks[near], blocks[far])
+
+
+def start(sample, scale, swapped):
+    rows, width = sample.shape
+    steps = 4
+    hbm = pl.BlockSpec(memory_space=pltpu.HBM)
+    return pl.pallas_call(
+        start_kernel,
+        out_shape=(shape(rows, N), shape(rows, N)),
+        in_specs=[hbm, hbm, VMEM],
+        out_specs=(VMEM, VMEM),
+        scratch_shapes=[
+            pltpu.VMEM((rows, width), jnp.float32),
+            pltpu.VMEM((1, width), jnp.float32),
+            pltpu.SemaphoreType.DMA((steps + 1,)),
+        ],
+    )(sample, scale, swapped)
 
 
 def gram_kernel(own, other, out):
@@ -238,28 +273,30 @@
 
 def first_kernel(landed, along, down, q_out, ship, *scratch):
     gram = first_gram(landed, 3 * BLOCK // landed.shape[0])
-    (q,) = solves([gram], along[...], down[...], scratch)
+    (q,) = solves([gram], 0, along, down, scratch)
     q_out[...] = q
     q1 = q[:, BLOCK:]
     ship[:N] = q1
     ship[N:] = dot_t(q1, dot(gram, q1))
 
 
-def keep_kernel(landed, q, own, other, unit, g00, kept, kept_basis):
+def keep_kernel(landed, q, own, other, unit, kept, kept_basis):
     q0 = q[:, :BLOCK]
-    kept[...] = dot(jnp.concatenate([own[...], other[...]], axis=0), q0)
+    rows = kept.shape[0] - BLOCK
+    kept[:rows] = dot(jnp.concatenate([own[...], other[...]], axis=0), q0)
+    kept[rows:] = dot_t(q0, dot(first_gram(landed, 3 * BLOCK // landed.shape[0]), q0))
     kept_basis[...] = dot(unit[...], q0)
-    g00[...] = dot_t(q0, dot(first_gram(landed, 3 * BLOCK // landed.shape[0]), q0))
-
-
-def second_kernel(mixed, q, ship, g00, kept, near, along, down, x0, x1, gram_out, q_out, *scratch):
+
+
+def second_kernel(mixed, q, ship, kept, near, along, down, x0, x1, gram_out, q_out, *scratch):
     q1 = ship[:N]
     cross = dot(q[:, :BLOCK].T, dot(beside(mixed[0], mixed[1]), q1))
-    gram = joined(g00[...], cross, ship[N:])
+    rows = near.shape[0]
+    gram = joined(kept[rows:], cross, ship[N:])
     gram_out[...] = gram
-    (turned,) = solves([gram], along[...], down[...], scratch)
+    (turned,) = solves([gram], 1, along, down, scratch)
     q_out[...] = turned
-    y = dot(beside(kept[...], dot(near[...], q1)), turned)
+    y = dot(beside(kept[:rows], dot(near[...], q1)), turned)
     x0[...] = y[:, :BLOCK]
     x1[...] = y[:, BLOCK:]
 
@@ -294,10 +331,8 @@
     rest0,
     rest1,
     near_rest,
-    along2,
-    down2,
-    along3,
-    down3,
+    along,
+    down,
     swapped,
     mine_data,
     mine_basis,
@@ -310,11 +345,11 @@
     mixed = jnp.concatenate(
         [beside(sums[2], sums[3]), beside(inner[...].T, sums[4].T)], axis=0
     )
-    qa, qb = solves([gram_a, gram_b], along2[...], down2[...], scratch)
+    qa, qb = solves([gram_a, gram_b], 2, along, down, scratch)
     qa, qb = qa[:, :BLOCK], qb[:, BLOCK:]
     left = dot(qa.T, beside(gram_a, mixed))
     gram = joined(dot(left[:, :N], qa), dot(left[:, N:], qb), dot(dot(qb.T, gram_b), qb))
-    (q,) = solves([gram], along3[...], down3[...], scratch)
+    (q,) = solves([gram], 3, along, down, scratch)
 
     def whole(data, rest):
         return jnp.concatenate([data[...], rest[:basis_rows]], axis=0)
@@ -379,14 +414,7 @@
     rows, width = sample.shape
     height = W // lax.axis_size("rows")
     swapped = jnp.full((1, BLOCK), core, jnp.float32)
-    own, send = call(
-        start_kernel,
-        (shape(rows, N), shape(rows, N)),
-        [],
-        sample,
-        column_scale.reshape(1, width),
-        swapped,
-    )
+    own, send = start(sample, column_scale.reshape(1, width), swapped)
     other = other_core(send)
     near = along_pairs(jnp.concatenate([own, other], axis=0), 1)
     near_col = (col + jnp.where(core == 0, 1, -1)) % n_pairs
@@ -398,11 +426,10 @@
     near_unit = jnp.where(row_ids == places + 2 * N * near_col, 1.0, 0.0).astype(jnp.float32)
 
     order = ((inner_order + core * BLOCK) % N).astype(jnp.float32)
-    table = np.concatenate([np.eye(N)[:, arrangement(0)], np.eye(N)[:, arrangement(ROUNDS)]], 1)
+    table = np.eye(N)[:, np.concatenate([arrangement(0), arrangement(ROUNDS)])]
     table = jnp.asarray(table.astype(np.float32))
-    along = dot(order, table).reshape(STEPS, 2, N)
-    down = dot_t(table, order.T).reshape(2, N, STEPS)
-    down = [down[:, :, s].T for s in range(STEPS)]
+    along = dot(order, table).reshape(2 * STEPS, N)
+    down = along.T
 
     chips = lax.axis_size("rows") // 2
     gram_rows, mixed_rows = 3 * BLOCK // chips, 2 * N // chips
@@ -425,14 +452,14 @@
         (shape(N, N), shape(N + BLOCK, BLOCK)),
         solve_scratch(1),
         landed,
-        along[0],
-        down[0],
+        along,
+        down,
     )
     ship = along_pairs(ship, 1)
     half, half_basis = shape(2 * rows, BLOCK), shape(2 * height, BLOCK)
-    g00, kept, kept_basis = call(
+    kept, kept_basis = call(
         keep_kernel,
-        (shape(BLOCK, BLOCK), half, half_basis),
+        (shape(2 * rows + BLOCK, BLOCK), half_basis),
         [],
         landed,
         q,
@@ -447,11 +474,10 @@
         mixed,
         q,
         ship,
-        g00,
         kept,
         near,
-        along[1],
-        down[1],
+        along,
+        down,
     )
 
     far0, near1 = along_pairs(x0, -1), along_pairs(x1, 1)
@@ -466,9 +492,11 @@
         q,
         gram,
     )
+    far0, near1, rest0, rest1 = lax.optimization_barrier((far0, near1, rest0, rest1))
+    far_rest, near_rest = along_pairs(rest0, -1), along_pairs(rest1, 1)
     cross = call(cross_kernel, shape(5, BLOCK, BLOCK), [], far0, x0, x1, near1)
     sums = trade(cross.reshape(chips, -1, BLOCK)).sum(0)
-    far_rest, near_rest = along_pairs(rest0, -1), along_pairs(rest1, 1)
+    sums, far_rest, near_rest = lax.optimization_barrier((sums, far_rest, near_rest))
     sums = all_slices(sums, chips).reshape(5, BLOCK, BLOCK)
     mine_data, mine_basis, theirs = call(
         last_kernel,
@@ -484,10 +512,8 @@
         rest0,
         rest1,
         near_rest,
-        along[2],
-        down[2],
-        along[3],
-        down[3],
+        along,
+        down,
         swapped,
     )
     return call(

time: 134 us -> 139 us (1.037)
  local copies, waits for them, and re-layouts: 7.74 us -> 2.8 us
  Pallas kernels: 26.1 us -> 30 us
  starting transfers between devices: 46.2 us -> 48.6 us
  waiting for transfers between devices: 36.2 us -> 38.1 us
    all_to_all x4, waiting for transfers between devices: 24.2 us -> 28.6 us  [trade(): return lax.all_to_all(parts, 'rows', 0, 0, axis_index_groups=groups)]
    unnamed x20 -> x8, local copies, waits for them, and re-layouts: 5.58 us -> 1.34 us
    ppermute x6, waiting for transfers between devices: 9.43 us -> 6.79 us  [along_pairs(): return lax.ppermute(x, ('rows', 'pairs'), route)]
    pallas_call x0 -> x1, Pallas kernels: none -> 2.62 us  [start(): pl.pallas_call(start_kernel, out_shape=(shape(rows, N), shape(rows, N)),...]
    all_to_all x4, starting transfers between devices: 19.7 us -> 21.1 us  [trade(): return lax.all_to_all(parts, 'rows', 0, 0, axis_index_groups=groups)]
    pallas_call x11 -> x10, Pallas kernels: 26.1 us -> 27.3 us  [call(): pl.pallas_call(kernel, out_shape=out_shape, in_specs=[VMEM] * len(operand...]
  transfers between devices with their start and end apart: 12 -> 12, of which waited for: 9 -> 9; matrix products, arithmetic and copies ran while one was open for 1% -> 0% of each run, Pallas kernels for 6% -> 7%
where the time goes in v5:
time: 139 us; the launch traced here: 138 us
  starting transfers between devices  48.6 us (35%)
  waiting for transfers between devices  38.1 us (27%)
  Pallas kernels  30 us (22%)
  blocking collectives  16.2 us (12%)
  local copies, waits for them, and re-layouts  2.8 us (2%)
    all_to_all x4, waiting for transfers between devices, trade(): return lax.all_to_all(parts, 'rows', 0, 0, axis_index_groups=groups)  28.6 us
    pallas_call x10, Pallas kernels, call(): pl.pallas_call(kernel, out_shape=out_shape, in_specs=[VMEM] * len(operand...  27.3 us
    all_to_all x4, starting transfers between devices, trade(): return lax.all_to_all(parts, 'rows', 0, 0, axis_index_groups=groups)  21.1 us
    all_to_all x1, blocking collectives, trade(): return lax.all_to_all(parts, 'rows', 0, 0, axis_index_groups=groups)  16.2 us
    ppermute x6, starting transfers between devices, along_pairs(): return lax.ppermute(x, ('rows', 'pairs'), route)  14.7 us
    ppermute x2, starting transfers between devices, other_core(): lax.ppermute(x, 'rows', [(i, i ^ 1) for i in range(lax.axis_size('rows'))])  12.8 us
    ppermute x6, waiting for transfers between devices, along_pairs(): return lax.ppermute(x, ('rows', 'pairs'), route)  6.79 us
  transfers between devices with their start and end apart: 12, of which 9 were waited for; matrix products, arithmetic and copies ran while one was open for 0% of the time, Pallas kernels for 7%

profile of v5, /device:TPU:7, one launch (start us, length us, event | category | flops | bytes accessed | tf_op | source)
XLA Modules:
  0.0 138.2 jit_solution(10599642634376583363)
XLA Ops:
  0.6 0.6 broadcast_in_dim.27.swapped
  1.2 2.6 %shard_map.59 = (f32[256,256]{1,0:T(8,128)}, f32[256,256]{1,0:T(8,128)}) custom-call(f32[256,512]{1,0:T(8,128)} %sample.1, f32[1,512]{1,0:T(1,128)} %bitcast.14, f32[1,128]{1,0:T(1,128)} %broadcast_in_dim.27.swapped), custom_call_target="tpu_custom_call" | custom-call | tf_op jit(solution)/shard_map/pallas_call | solution.py:234
  3.8 0.8 collective-permute-start
  4.6 1.4 collective-permute-done.other
  6.0 0.0 copy-start
  6.0 1.1 pad_maximum_fusion
  7.0 2.9 %collective-permute-start.1 = (f32[512,256]{1,0:T(8,128)S(1)}, f32[512,256]{1,0:T(8,128)S(1)}, u32[]{:S(2)}, u32[]{:S(2)}) collective-permute-start(f32[512,256]{1,0:T(8,128)S(1)} %pad_maximum_fusion), channel_id=1, source_target_pairs={{0,7},{1,0},{2,1},{3,2},{4,3},{5,4},{6,5},{7,6},{8,9},{9,10},{10,1... | collective-permute-start | bytes 1572872 | tf_op jit(solution)/shard_map/ppermute | solution.py:407
  9.9 0.0 copy-done
  10.0 1.4 %shard_map.60 = f32[3,128,128]{2,1,0:T(8,128)} custom-call(f32[256,256]{1,0:T(8,128)S(1)} %copy-done, f32[256,256]{1,0:T(8,128)S(1)} %collective-permute-done.other), custom_call_target="tpu_custom_call" | custom-call | tf_op jit(solution)/shard_map/pallas_call | solution.py:32
  11.4 8.4 %all-to-all-start = ((f32[16,24,128]{2,1,0:T(8,128)}), f32[16,24,128]{2,1,0:T(8,128)S(1)}, u32[]{:S(2)}, u32[]{:S(2)}) async-start(f32[16,24,128]{2,1,0:T(8,128)} %bitcast.1), calls=%async_computation | async-start | bytes 393216 | tf_op jit(solution)/shard_map/all_to_all | solution.py:389
  19.8 0.0 collective-permute-done.1.near
  19.8 0.7 shard_map.61
  20.5 10.3 %all-to-all-done.parts = f32[16,24,128]{2,1,0:T(8,128)S(1)} async-done(((f32[16,24,128]{2,1,0:T(8,128)}), f32[16,24,128]{2,1,0:T(8,128)S(1)}, u32[]{:S(2)}, u32[]{:S(2)}) %all-to-all-start) | async-done | bytes 196640 | tf_op jit(solution)/shard_map/all_to_all | solution.py:389
  30.8 0.8 shard_map.62
  31.6 3.7 %all-to-all-start.1 = ((f32[16,56,128]{2,1,0:T(8,128)}), f32[16,56,128]{2,1,0:T(8,128)S(1)}, u32[]{:S(2)}, u32[]{:S(2)}) async-start(f32[16,56,128]{2,1,0:T(8,128)} %shard_map.62), calls=%async_computation.1 | async-start | bytes 917504 | tf_op jit(solution)/shard_map/all_to_all | solution.py:389
  35.3 0.0 copy-start.3
  35.3 0.0 copy-done.2
  35.3 0.7 copy-done.3
  36.0 0.4 fusion.2
  36.4 13.9 %all-to-all-done.1.landed = f32[16,56,128]{2,1,0:T(8,128)S(1)} async-done(((f32[16,56,128]{2,1,0:T(8,128)}), f32[16,56,128]{2,1,0:T(8,128)S(1)}, u32[]{:S(2)}, u32[]{:S(2)}) %all-to-all-start.1) | async-done | bytes 458784 | tf_op jit(solution)/shard_map/all_to_all | solution.py:389
  50.3 0.7 broadcast_in_dim.28
  51.0 4.0 %all-to-all-start.2 = ((f32[16,32,128]{2,1,0:T(8,128)}), f32[16,32,128]{2,1,0:T(8,128)S(1)}, u32[]{:S(2)}, u32[]{:S(2)}) async-start(f32[16,32,128]{2,1,0:T(8,128)} %broadcast_in_dim.28), calls=%async_computation.2 | async-start | bytes 524288 | tf_op jit(solution)/shard_map/all_to_all | solution.py:389
  55.1 0.1 copy.9
  55.2 3.7 %shard_map.63 = (f32[256,256]{1,0:T(8,128)S(1)}, f32[384,128]{1,0:T(8,128)S(1)}) custom-call(f32[16,56,128]{2,1,0:T(8,128)S(1)} %all-to-all-done.1.landed, f32[8,256]{1,0:T(8,128)S(1)} %reshape.61.along, f32[256,8]{1,0:T(8,128)S(1)} %bitcast.8), custom_call_target="tpu_custom_call" | custom-call | tf_op jit(solution)/shard_map/pallas_call | solution.py:32
  59.0 0.1 collective-permute-start.2
  59.1 0.1 compare_select_fusion
  59.2 1.8 %shard_map.64 = (f32[640,128]{1,0:T(8,128)S(1)}, f32[256,128]{1,0:T(8,128)S(1)}) custom-call(f32[16,56,128]{2,1,0:T(8,128)S(1)} %all-to-all-done.1.landed, f32[256,256]{1,0:T(8,128)S(1)} %get-tuple-element.27.q, f32[256,256]{1,0:T(8,128)S(1)} %copy-done, f32[256,256]{1,0:T(8,128)S(1)} %collective-permute-done.other, f32[256,256]{1,0:T(8,128)S(1)} %get-tuple-element.49.unit), custom_call_target="tpu_custom_call" | custom-call | tf_op jit(solution)/shard_map/pallas_call | solution.py:32
  61.0 2.9 %collective-permute-done.2.ship = f32[384,128]{1,0:T(8,128)S(1)} collective-permute-done((f32[384,128]{1,0:T(8,128)S(1)}, f32[384,128]{1,0:T(8,128)S(1)}, u32[]{:S(2)}, u32[]{:S(2)}) %collective-permute-start.2) | collective-permute-done | bytes 196640 | tf_op jit(solution)/shard_map/ppermute | solution.py:407
  63.9 0.9 all-to-all-done.2
  64.8 5.1 %shard_map.65 = (f32[512,128]{1,0:T(8,128)S(1)}, f32[512,128]{1,0:T(8,128)S(1)}, f32[256,256]{1,0:T(8,128)S(1)}, f32[256,256]{1,0:T(8,128)S(1)}) custom-call(f32[2,256,128]{2,1,0:T(8,128)S(1)} %bitcast.13, f32[256,256]{1,0:T(8,128)S(1)} %get-tuple-element.27.q, f32[384,128]{1,0:T(8,128)S(1)} %collective-permute-done.2.ship, ...), custom_call_target="tpu_custom_call" | custom-call | tf_op jit(solution)/shard_map/pallas_call | solution.py:32
  69.9 0.1 collective-permute-start.3
  70.0 5.1 %collective-permute-start.4 = (f32[512,128]{1,0:T(8,128)S(1)}, f32[512,128]{1,0:T(8,128)S(1)}, u32[]{:S(2)}, u32[]{:S(2)}) collective-permute-start(f32[512,128]{1,0:T(8,128)S(1)} %get-tuple-element.31.x1), channel_id=1, source_target_pairs={{0,7},{1,0},{2,1},{3,2},{4,3},{5,4},{6,5},{7,6},{8,9},{9,10},{10,1... | collective-permute-start | bytes 786440 | tf_op jit(solution)/shard_map/ppermute | solution.py:407
  75.0 1.5 %shard_map.66 = (f32[384,128]{1,0:T(8,128)S(1)}, f32[384,128]{1,0:T(8,128)S(1)}, f32[128,128]{1,0:T(8,128)S(1)}) custom-call(f32[256,128]{1,0:T(8,128)S(1)} %get-tuple-element.32.kept, f32[256,256]{1,0:T(8,128)S(1)} %get-tuple-element.48.unit, f32[384,128]{1,0:T(8,128)S(1)} %collective-permute-done.2.ship, f32[256,256]{1,0:T(8,128)S(1)} %get-tuple-element.33.q, ...), custom_call_target="tpu_custom_call" | custom-call | tf_op jit(solution)/shard_map/pallas_call | solution.py:32
  76.5 2.3 %collective-permute-done.3.far0 = f32[512,128]{1,0:T(8,128)S(1)} collective-permute-done((f32[512,128]{1,0:T(8,128)S(1)}, f32[512,128]{1,0:T(8,128)S(1)}, u32[]{:S(2)}, u32[]{:S(2)}) %collective-permute-start.3) | collective-permute-done | bytes 262176 | tf_op jit(solution)/shard_map/ppermute | solution.py:407
  78.8 1.6 %collective-permute-done.4.near1 = f32[512,128]{1,0:T(8,128)S(1)} collective-permute-done((f32[512,128]{1,0:T(8,128)S(1)}, f32[512,128]{1,0:T(8,128)S(1)}, u32[]{:S(2)}, u32[]{:S(2)}) %collective-permute-start.4) | collective-permute-done | bytes 262176 | tf_op jit(solution)/shard_map/ppermute | solution.py:407
  80.4 1.6 %shard_map.67 = f32[5,128,128]{2,1,0:T(8,128)} custom-call(f32[512,128]{1,0:T(8,128)S(1)} %collective-permute-done.3.far0, f32[512,128]{1,0:T(8,128)S(1)} %get-tuple-element.30.x0, f32[512,128]{1,0:T(8,128)S(1)} %get-tuple-element.31.x1, f32[512,128]{1,0:T(8,128)S(1)} %collective-permute-done.4.near1), custom_call_target="tpu_custom_call" | custom-call | tf_op jit(solution)/shard_map/pallas_call | solution.py:32
  81.9 4.9 %all-to-all-start.3 = ((f32[16,40,128]{2,1,0:T(8,128)}), f32[16,40,128]{2,1,0:T(8,128)S(1)}, u32[]{:S(2)}, u32[]{:S(2)}) async-start(f32[16,40,128]{2,1,0:T(8,128)} %bitcast.5), calls=%async_computation.3 | async-start | bytes 655360 | tf_op jit(solution)/shard_map/all_to_all | solution.py:389
  86.9 0.1 collective-permute-start.5
  87.0 6.5 %collective-permute-start.6 = (f32[384,128]{1,0:T(8,128)S(1)}, f32[384,128]{1,0:T(8,128)S(1)}, u32[]{:S(2)}, u32[]{:S(2)}) collective-permute-start(f32[384,128]{1,0:T(8,128)S(1)} %get-tuple-element.40.rest1), channel_id=1, source_target_pairs={{0,7},{1,0},{2,1},{3,2},{4,3},{5,4},{6,5},{7,6},{8,9},{9,10},{10,1... | collective-permute-start | bytes 589832 | tf_op jit(solution)/shard_map/ppermute | solution.py:407
  93.5 3.6 %all-to-all-done.3 = f32[16,40,128]{2,1,0:T(8,128)S(1)} async-done(((f32[16,40,128]{2,1,0:T(8,128)}), f32[16,40,128]{2,1,0:T(8,128)S(1)}, u32[]{:S(2)}, u32[]{:S(2)}) %all-to-all-start.3) | async-done | bytes 327712 | tf_op jit(solution)/shard_map/all_to_all | solution.py:389
  97.1 0.0 collective-permute-done.5.far_rest
  97.1 0.0 collective-permute-done.6.near_rest
  97.2 16.2 %all_to_all.25 = f32[16,40,128]{2,1,0:T(8,128)S(1)} all-to-all(f32[16,40,128]{2,1,0:T(8,128)S(1)} %broadcast_in_dim.31), channel_id=1, replica_groups={{0,16,32,48,64,80,96,112,128,144,160,176,192,208,224,240},{8,24,40,56,7..., dimensions={0} | all-to-all | bytes 655360 | tf_op jit(solution)/shard_map/all_to_all | solution.py:389
  113.3 0.7 copy-done.1
  114.0 9.8 %shard_map.68 = (f32[256,256]{1,0:T(8,128)S(1)}, f32[128,256]{1,0:T(8,128)S(1)}, f32[384,256]{1,0:T(8,128)S(1)}) custom-call(f32[5,128,128]{2,1,0:T(8,128)S(1)} %bitcast.11, f32[128,128]{1,0:T(8,128)S(1)} %get-tuple-element.42.inner, f32[512,128]{1,0:T(8,128)S(1)} %collective-permute-done.3.far0, f32[512,128]{1,0:T(8,128)S(1)} %get-tuple-element.30.x0, ...), custom_call_target="tpu_custom_call" | custom-call | tf_op jit(solution)/shard_map/pallas_call | solution.py:32
  123.8 12.1 %collective-permute-start.7 = (f32[384,256]{1,0:T(8,128)S(1)}, f32[384,256]{1,0:T(8,128)S(1)}, u32[]{:S(2)}, u32[]{:S(2)}) collective-permute-start(f32[384,256]{1,0:T(8,128)S(1)} %get-tuple-element.45), channel_id=1, source_target_pairs={{0,8},{8,0},{16,24},{24,16},{32,40},{40,32},{48,56},{56,48},{64,72... | collective-permute-start | bytes 1179656 | tf_op jit(solution)/shard_map/ppermute | solution.py:397
  135.9 1.3 collective-permute-done.7.got
  137.2 0.9 shard_map.69
  (9 shorter events, 0.1 us)
Async XLA Ops:
  3.8 2.1 %collective-permute-start = (f32[256,256]{1,0:T(8,128)}, f32[256,256]{1,0:T(8,128)S(1)}, u32[]{:S(2)}, u32[]{:S(2)}) collective-permute-start(f32[256,256]{1,0:T(8,128)} %get-tuple-element.26), channel_id=1, source_target_pairs={{0,8},{8,0},{16,24},{24,16},{32,40},{40,32},{48,56},{56,48},{64,72... | collective-permute-start | bytes 786440 | tf_op jit(solution)/shard_map/ppermute | solution.py:397
  6.0 4.0 %copy-start = (f32[256,256]{1,0:T(8,128)S(1)}, f32[256,256]{1,0:T(8,128)}, u32[]{:S(2)}) copy-start(f32[256,256]{1,0:T(8,128)} %get-tuple-element.25.own) | copy-start | bytes 786436
  7.0 12.7 %collective-permute-start.1 = (f32[512,256]{1,0:T(8,128)S(1)}, f32[512,256]{1,0:T(8,128)S(1)}, u32[]{:S(2)}, u32[]{:S(2)}) collective-permute-start(f32[512,256]{1,0:T(8,128)S(1)} %pad_maximum_fusion), channel_id=1, source_target_pairs={{0,7},{1,0},{2,1},{3,2},{4,3},{5,4},{6,5},{7,6},{8,9},{9,10},{10,1... | collective-permute-start | bytes 1572872 | tf_op jit(solution)/shard_map/ppermute | solution.py:407
  11.4 19.4 %all-to-all-start = ((f32[16,24,128]{2,1,0:T(8,128)}), f32[16,24,128]{2,1,0:T(8,128)S(1)}, u32[]{:S(2)}, u32[]{:S(2)}) async-start(f32[16,24,128]{2,1,0:T(8,128)} %bitcast.1), calls=%async_computation | async-start | bytes 393216 | tf_op jit(solution)/shard_map/all_to_all | solution.py:389
  31.6 3.7 %copy-start.2 = (f32[256,512]{1,0:T(8,128)S(1)}, f32[256,512]{1,0:T(8,128)}, u32[]{:S(2)}) copy-start(f32[256,512]{1,0:T(8,128)} %constant.68.clone) | copy-start | bytes 1572868
  31.6 18.6 %all-to-all-start.1 = ((f32[16,56,128]{2,1,0:T(8,128)}), f32[16,56,128]{2,1,0:T(8,128)S(1)}, u32[]{:S(2)}, u32[]{:S(2)}) async-start(f32[16,56,128]{2,1,0:T(8,128)} %shard_map.62), calls=%async_computation.1 | async-start | bytes 917504 | tf_op jit(solution)/shard_map/all_to_all | solution.py:389
  35.3 0.7 copy-start.3
  51.0 13.8 %all-to-all-start.2 = ((f32[16,32,128]{2,1,0:T(8,128)}), f32[16,32,128]{2,1,0:T(8,128)S(1)}, u32[]{:S(2)}, u32[]{:S(2)}) async-start(f32[16,32,128]{2,1,0:T(8,128)} %broadcast_in_dim.28), calls=%async_computation.2 | async-start | bytes 524288 | tf_op jit(solution)/shard_map/all_to_all | solution.py:389
  59.0 4.9 %collective-permute-start.2 = (f32[384,128]{1,0:T(8,128)S(1)}, f32[384,128]{1,0:T(8,128)S(1)}, u32[]{:S(2)}, u32[]{:S(2)}) collective-permute-start(f32[384,128]{1,0:T(8,128)S(1)} %get-tuple-element.28), channel_id=1, source_target_pairs={{0,7},{1,0},{2,1},{3,2},{4,3},{5,4},{6,5},{7,6},{8,9},{9,10},{10,1... | collective-permute-start | bytes 589832 | tf_op jit(solution)/shard_map/ppermute | solution.py:407
  69.9 8.9 %collective-permute-start.3 = (f32[512,128]{1,0:T(8,128)S(1)}, f32[512,128]{1,0:T(8,128)S(1)}, u32[]{:S(2)}, u32[]{:S(2)}) collective-permute-start(f32[512,128]{1,0:T(8,128)S(1)} %get-tuple-element.30.x0), channel_id=1, source_target_pairs={{0,1},{1,2},{2,3},{3,4},{4,5},{5,6},{6,7},{7,0},{8,15},{9,8},{10,9... | collective-permute-start | bytes 786440 | tf_op jit(solution)/shard_map/ppermute | solution.py:407
  70.0 10.4 %collective-permute-start.4 = (f32[512,128]{1,0:T(8,128)S(1)}, f32[512,128]{1,0:T(8,128)S(1)}, u32[]{:S(2)}, u32[]{:S(2)}) collective-permute-start(f32[512,128]{1,0:T(8,128)S(1)} %get-tuple-element.31.x1), channel_id=1, source_target_pairs={{0,7},{1,0},{2,1},{3,2},{4,3},{5,4},{6,5},{7,6},{8,9},{9,10},{10,1... | collective-permute-start | bytes 786440 | tf_op jit(solution)/shard_map/ppermute | solution.py:407
  81.9 15.1 %all-to-all-start.3 = ((f32[16,40,128]{2,1,0:T(8,128)}), f32[16,40,128]{2,1,0:T(8,128)S(1)}, u32[]{:S(2)}, u32[]{:S(2)}) async-start(f32[16,40,128]{2,1,0:T(8,128)} %bitcast.5), calls=%async_computation.3 | async-start | bytes 655360 | tf_op jit(solution)/shard_map/all_to_all | solution.py:389
  86.9 10.2 %collective-permute-start.5 = (f32[384,128]{1,0:T(8,128)S(1)}, f32[384,128]{1,0:T(8,128)S(1)}, u32[]{:S(2)}, u32[]{:S(2)}) collective-permute-start(f32[384,128]{1,0:T(8,128)S(1)} %get-tuple-element.39.rest0), channel_id=1, source_target_pairs={{0,1},{1,2},{2,3},{3,4},{4,5},{5,6},{6,7},{7,0},{8,15},{9,8},{10,9... | collective-permute-start | bytes 589832 | tf_op jit(solution)/shard_map/ppermute | solution.py:407
  87.0 10.1 %collective-permute-start.6 = (f32[384,128]{1,0:T(8,128)S(1)}, f32[384,128]{1,0:T(8,128)S(1)}, u32[]{:S(2)}, u32[]{:S(2)}) collective-permute-start(f32[384,128]{1,0:T(8,128)S(1)} %get-tuple-element.40.rest1), channel_id=1, source_target_pairs={{0,7},{1,0},{2,1},{3,2},{4,3},{5,4},{6,5},{7,6},{8,9},{9,10},{10,1... | collective-permute-start | bytes 589832 | tf_op jit(solution)/shard_map/ppermute | solution.py:407
  113.3 0.7 copy-start.1
  123.8 13.4 %collective-permute-start.7 = (f32[384,256]{1,0:T(8,128)S(1)}, f32[384,256]{1,0:T(8,128)S(1)}, u32[]{:S(2)}, u32[]{:S(2)}) collective-permute-start(f32[384,256]{1,0:T(8,128)S(1)} %get-tuple-element.45), channel_id=1, source_target_pairs={{0,8},{8,0},{16,24},{24,16},{32,40},{40,32},{48,56},{56,48},{64,72... | collective-permute-start | bytes 1179656 | tf_op jit(solution)/shard_map/ppermute | solution.py:397

commit v6 on v5

--- a/solution.py
+++ b/solution.py
@@ -116,7 +116,7 @@
     return c, t * c
 
 
-def solves(grams, step, along_ref, down_ref, scratch):
+def solves(grams, step, along_ref, down_ref, scratch, beside_rounds=None):
     along = along_ref[2 * step : 2 * step + 1]
     down = down_ref[:, 2 * step : 2 * step + 2]
     ga, gb, gc, gd, qa, qb, qc, qd = scratch
@@ -186,7 +186,9 @@
             bottom[new, k, pl.ds(8, 1)] = up[1:2]
         return new_pp, new_cross, new_qq
 
-    def two_rounds(_, state):
+    def two_rounds(i, state):
+        if beside_rounds is not None:
+            beside_rounds(i)
         state = [one_round(0, 1, k, *state[k]) for k in range(count)]
         return [one_round(1, 0, k, *state[k]) for k in range(count)]
 
@@ -201,47 +203,18 @@
     ]
 
 
-def start_kernel(sample, scale, swapped, own, send, rows_in, scale_in, sems):
-    steps = sems.shape[0] - 1
-    size = sample.shape[0] // steps
-    copies = [
-        pltpu.make_async_copy(
-            sample.at[pl.ds(k * size, size)], rows_in.at[pl.ds(k * size, size)], sems.at[k]
-        )
-        for k in range(steps)
-    ]
-    scale_copy = pltpu.make_async_copy(scale, scale_in, sems.at[steps])
-    scale_copy.start()
-    for copy in copies:
-        copy.start()
-    scale_copy.wait()
-    swap = swapped[...] > 0.0
-    for k in range(steps):
-        copies[k].wait()
-        part = pl.ds(k * size, size)
-        x = rows_in[part] * scale_in[...]
-        blocks = [x[:, b * BLOCK : (b + 1) * BLOCK] for b in range(4)]
-        for near, far in ((0, 3), (1, 2)):
-            at = slice(near * BLOCK, (near + 1) * BLOCK)
-            own[part, at] = jnp.where(swap, blocks[far], blocks[near])
-            send[part, at] = jnp.where(swap, blocks[near], blocks[far])
-
-
-def start(sample, scale, swapped):
-    rows, width = sample.shape
-    steps = 4
-    hbm = pl.BlockSpec(memory_space=pltpu.HBM)
-    return pl.pallas_call(
-        start_kernel,
-        out_shape=(shape(rows, N), shape(rows, N)),
-        in_specs=[hbm, hbm, VMEM],
-        out_specs=(VMEM, VMEM),
-        scratch_shapes=[
-            pltpu.VMEM((rows, width), jnp.float32),
-            pltpu.VMEM((1, width), jnp.float32),
-            pltpu.SemaphoreType.DMA((steps + 1,)),
-        ],
-    )(sample, scale, swapped)
+def on_core_1():
+    return lax.axis_index("rows") % 2 == 1
+
+
+def start_kernel(sample, scale, own, send):
+    x = sample[...] * scale[...]
+    blocks = [x[:, k * BLOCK : (k + 1) * BLOCK] for k in range(4)]
+    swap = on_core_1()
+    for k, far in ((0, 3), (1, 2)):
+        at = slice(k * BLOCK, (k + 1) * BLOCK)
+        own[:, at] = jnp.where(swap, blocks[far], blocks[k])
+        send[:, at] = jnp.where(swap, blocks[k], blocks[far])
 
 
 def gram_kernel(own, other, out):
@@ -252,18 +225,32 @@
 
 def mixed_kernel(own, other, near, out):
     x = jnp.concatenate([own[...], other[...]], axis=0)
-    mixed = dot_t(x, near[...])
+    mixed = dot_t(near[...], x)
     out[0], out[1] = mixed[:, :BLOCK], mixed[:, BLOCK:]
 
 
 def spread_kernel(parts, mixed, out):
     n, m = parts.shape[0], parts.shape[1]
+    size = N // n
     total = parts[0]
     for k in range(1, n):
         total = total + parts[k]
     for k in range(n):
         out[k, :m] = total
-    out[:, m:] = mixed[...]
+        for half in range(2):
+            at = pl.ds(m + half * size, size)
+            out[k, at] = mixed[half, k * size : (k + 1) * size]
+
+
+def share_kernel(landed, q, out):
+    n, m = landed.shape[0], 3 * BLOCK // landed.shape[0]
+    size = N // n
+    total = landed[0, m:]
+    for k in range(1, n):
+        total = total + landed[k, m:]
+    mine = dot(beside(total[:size], total[size:]), q[:, :BLOCK])
+    for k in range(n):
+        out[k] = mine
 
 
 def first_gram(landed, m):
@@ -288,15 +275,21 @@
     kept_basis[...] = dot(unit[...], q0)
 
 
-def second_kernel(mixed, q, ship, kept, near, along, down, x0, x1, gram_out, q_out, *scratch):
+def second_kernel(mixed, ship, kept, near, along, down, x0, x1, gram_out, q_out, turned1, *scratch):
     q1 = ship[:N]
-    cross = dot(q[:, :BLOCK].T, dot(beside(mixed[0], mixed[1]), q1))
+    cross = dot_t(mixed[...], q1)
     rows = near.shape[0]
     gram = joined(kept[rows:], cross, ship[N:])
     gram_out[...] = gram
-    (turned,) = solves([gram], 1, along, down, scratch)
+    part = rows // (ROUNDS // 2)
+
+    def near_rows(k):
+        at = pl.ds(pl.multiple_of(k * part, part), part)
+        turned1[at] = dot(near[at], ship[:N])
+
+    (turned,) = solves([gram], 1, along, down, scratch, near_rows)
     q_out[...] = turned
-    y = dot(beside(kept[:rows], dot(near[...], q1)), turned)
+    y = dot(beside(kept[:rows], turned1[...]), turned)
     x0[...] = y[:, :BLOCK]
     x1[...] = y[:, BLOCK:]
 
@@ -333,10 +326,11 @@
     near_rest,
     along,
     down,
-    swapped,
     mine_data,
     mine_basis,
     theirs,
+    ya,
+    yb,
     *scratch,
 ):
     basis_rows = far_rest.shape[0] - BLOCK
@@ -349,15 +343,22 @@
     qa, qb = qa[:, :BLOCK], qb[:, BLOCK:]
     left = dot(qa.T, beside(gram_a, mixed))
     gram = joined(dot(left[:, :N], qa), dot(left[:, N:], qb), dot(dot(qb.T, gram_b), qb))
-    (q,) = solves([gram], 3, along, down, scratch)
-
-    def whole(data, rest):
-        return jnp.concatenate([data[...], rest[:basis_rows]], axis=0)
-
-    ya = dot_3(beside(whole(far0, far_rest), whole(x1, rest1)), qa)
-    yb = dot_3(beside(whole(x0, rest0), whole(near1, near_rest)), qb)
-    y = dot_3(beside(ya, yb), q)
-    swap = swapped[...] > 0.0
+    data_rows = far0.shape[0]
+
+    def quarter(k):
+        for first, count, pairs in (
+            (0, data_rows, ((far0, x1, qa, ya), (x0, near1, qb, yb))),
+            (data_rows, basis_rows, ((far_rest, rest1, qa, ya), (rest0, near_rest, qb, yb))),
+        ):
+            part = count // (ROUNDS // 2)
+            at = pl.ds(pl.multiple_of(k * part, part), part)
+            to = pl.ds(pl.multiple_of(first + k * part, part), part)
+            for left, right, q, out in pairs:
+                out[to] = dot_3(beside(left[at], right[at]), q)
+
+    (q,) = solves([gram], 3, along, down, scratch, quarter)
+    y = dot_3(beside(ya[...], yb[...]), q)
+    swap = on_core_1()
     y = beside(
         jnp.where(swap, y[:, BLOCK:], y[:, :BLOCK]), jnp.where(swap, y[:, :BLOCK], y[:, BLOCK:])
     )
@@ -368,9 +369,8 @@
     theirs[rows:] = y[2 * rows + height :]
 
 
-def place_kernel(got, mine_data, mine_basis, swapped, data, basis):
-    swap = swapped[...] > 0.0
-    swap = beside(swap, swap)
+def place_kernel(got, mine_data, mine_basis, data, basis):
+    swap = on_core_1()
     rows = mine_data.shape[0]
     for mine, theirs, out in (
         (mine_data[...], got[:rows], data),
@@ -413,8 +413,8 @@
     n_pairs = lax.axis_size("pairs")
     rows, width = sample.shape
     height = W // lax.axis_size("rows")
-    swapped = jnp.full((1, BLOCK), core, jnp.float32)
-    own, send = start(sample, column_scale.reshape(1, width), swapped)
+    pair = (shape(rows, N), shape(rows, N))
+    own, send = call(start_kernel, pair, [], sample, column_scale.reshape(1, width))
     other = other_core(send)
     near = along_pairs(jnp.concatenate([own, other], axis=0), 1)
     near_col = (col + jnp.where(core == 0, 1, -1)) % n_pairs
@@ -442,11 +442,9 @@
             shape(chips, gram_rows + mixed_rows, BLOCK),
             [],
             parts,
-            mixed.reshape(chips, -1, BLOCK),
+            mixed,
         )
     )
-    mixed = all_slices(landed[:, gram_rows:].sum(0), chips).reshape(2, N, BLOCK)
-
     q, ship = call(
         first_kernel,
         (shape(N, N), shape(N + BLOCK, BLOCK)),
@@ -456,6 +454,8 @@
         down,
     )
     ship = along_pairs(ship, 1)
+    mixed = trade(call(share_kernel, shape(chips, N // chips, BLOCK), [], landed, q))
+    mixed = mixed.reshape(N, BLOCK)
     half, half_basis = shape(2 * rows, BLOCK), shape(2 * height, BLOCK)
     kept, kept_basis = call(
         keep_kernel,
@@ -470,9 +470,8 @@
     x0, x1, gram, q = call(
         second_kernel,
         (half, half, shape(N, N), shape(N, N)),
-        solve_scratch(1),
+        [pltpu.VMEM(half.shape, jnp.float32)] + solve_scratch(1),
         mixed,
-        q,
         ship,
         kept,
         near,
@@ -501,7 +500,7 @@
     mine_data, mine_basis, theirs = call(
         last_kernel,
         (shape(rows, N), shape(height, N), shape(rows + height, N)),
-        solve_scratch(2),
+        [pltpu.VMEM((2 * (rows + height), BLOCK), jnp.float32)] * 2 + solve_scratch(2),
         sums,
         inner,
         far0,
@@ -514,7 +513,6 @@
         near_rest,
         along,
         down,
-        swapped,
     )
     return call(
         place_kernel,
@@ -523,7 +521,6 @@
         other_core(theirs),
         mine_data,
         mine_basis,
-        swapped,
     )
 
 

time: 139 us -> 133 us (0.957)
  Pallas kernels: 30 us -> 26.8 us
  starting transfers between devices: 48.6 us -> 46.4 us
    all_to_all x4, waiting for transfers between devices: 28.6 us -> 31.8 us  [trade(): return lax.all_to_all(parts, 'rows', 0, 0, axis_index_groups=groups)]
    pallas_call x1 -> x0, Pallas kernels: 2.62 us -> none  [start(): pl.pallas_call(start_kernel, out_shape=(shape(rows, N), shape(rows, N)),...]
    ppermute x6, waiting for transfers between devices: 6.79 us -> 5.04 us  [along_pairs(): return lax.ppermute(x, ('rows', 'pairs'), route)]
    pallas_call x10 -> x12, Pallas kernels: 27.3 us -> 26.8 us  [call(): pl.pallas_call(kernel, out_shape=out_shape, in_specs=[VMEM] * len(operand...]
  transfers between devices with their start and end apart: 12 -> 12, of which waited for: 9 -> 9; matrix products, arithmetic and copies ran while one was open for 0% -> 0% of each run, Pallas kernels for 7% -> 4%
where the time goes in v6:
time: 133 us
  starting transfers between devices  46.4 us (35%)
  waiting for transfers between devices  39.4 us (30%)
  Pallas kernels  26.8 us (20%)
  blocking collectives  16.2 us (12%)
  local copies, waits for them, and re-layouts  2.55 us (2%)
    all_to_all x4, waiting for transfers between devices, trade(): return lax.all_to_all(parts, 'rows', 0, 0, axis_index_groups=groups)  31.8 us
    pallas_call x12, Pallas kernels, call(): pl.pallas_call(kernel, out_shape=out_shape, in_specs=[VMEM] * len(operand...  26.8 us
    all_to_all x4, starting transfers between devices, trade(): return lax.all_to_all(parts, 'rows', 0, 0, axis_index_groups=groups)  20 us
    all_to_all x1, blocking collectives, trade(): return lax.all_to_all(parts, 'rows', 0, 0, axis_index_groups=groups)  16.2 us
    ppermute x6, starting transfers between devices, along_pairs(): return lax.ppermute(x, ('rows', 'pairs'), route)  14.7 us
    ppermute x2, starting transfers between devices, other_core(): lax.ppermute(x, 'rows', [(i, i ^ 1) for i in range(lax.axis_size('rows'))])  11.6 us
    ppermute x6, waiting for transfers between devices, along_pairs(): return lax.ppermute(x, ('rows', 'pairs'), route)  5.04 us
  transfers between devices with their start and end apart: 12, of which 9 were waited for; matrix products, arithmetic and copies ran while one was open for 0% of the time, Pallas kernels for 4%

profile of v6, /device:TPU:7, one launch (start us, length us, event | category | flops | bytes accessed | tf_op | source)
XLA Modules:
  0.0 132.7 jit_solution(12035316338296810252)
XLA Ops:
  0.6 0.0 copy-start
  0.6 1.0 copy-done
  1.7 0.0 copy-start.1
  1.7 0.7 copy-done.1
  2.4 0.1 shard_map.59
  2.4 0.8 collective-permute-start
  3.2 1.2 collective-permute-done.other
  4.4 2.9 %collective-permute-start.1 = (f32[512,256]{1,0:T(8,128)S(1)}, f32[512,256]{1,0:T(8,128)S(1)}, u32[]{:S(2)}, u32[]{:S(2)}) collective-permute-start(f32[512,256]{1,0:T(8,128)S(1)} %pad_maximum_fusion), channel_id=1, source_target_pairs={{0,7},{1,0},{2,1},{3,2},{4,3},{5,4},{6,5},{7,6},{8,9},{9,10},{10,1... | collective-permute-start | bytes 1572872 | tf_op jit(solution)/shard_map/ppermute | solution.py:407
  7.3 1.4 %shard_map.60 = f32[3,128,128]{2,1,0:T(8,128)} custom-call(f32[256,256]{1,0:T(8,128)S(1)} %get-tuple-element.25.own, f32[256,256]{1,0:T(8,128)S(1)} %collective-permute-done.other), custom_call_target="tpu_custom_call" | custom-call | tf_op jit(solution)/shard_map/pallas_call | solution.py:32
  8.7 8.4 %all-to-all-start = ((f32[16,24,128]{2,1,0:T(8,128)}), f32[16,24,128]{2,1,0:T(8,128)S(1)}, u32[]{:S(2)}, u32[]{:S(2)}) async-start(f32[16,24,128]{2,1,0:T(8,128)} %bitcast.1), calls=%async_computation | async-start | bytes 393216 | tf_op jit(solution)/shard_map/all_to_all | solution.py:389
  17.1 0.0 collective-permute-done.1.near
  17.1 0.7 shard_map.61.mixed
  17.8 10.3 %all-to-all-done.parts = f32[16,24,128]{2,1,0:T(8,128)S(1)} async-done(((f32[16,24,128]{2,1,0:T(8,128)}), f32[16,24,128]{2,1,0:T(8,128)S(1)}, u32[]{:S(2)}, u32[]{:S(2)}) %all-to-all-start) | async-done | bytes 196640 | tf_op jit(solution)/shard_map/all_to_all | solution.py:389
  28.1 0.8 shard_map.62
  29.0 0.0 copy-start.2
  29.0 3.7 %all-to-all-start.1 = ((f32[16,56,128]{2,1,0:T(8,128)}), f32[16,56,128]{2,1,0:T(8,128)S(1)}, u32[]{:S(2)}, u32[]{:S(2)}) async-start(f32[16,56,128]{2,1,0:T(8,128)} %shard_map.62), calls=%async_computation.1 | async-start | bytes 917504 | tf_op jit(solution)/shard_map/all_to_all | solution.py:389
  32.7 0.0 copy-start.3
  32.7 0.0 copy-done.2
  32.7 0.7 copy-done.3
  33.4 0.4 fusion.2
  33.8 0.1 copy.9
  33.9 13.6 %all-to-all-done.1.landed = f32[16,56,128]{2,1,0:T(8,128)S(1)} async-done(((f32[16,56,128]{2,1,0:T(8,128)}), f32[16,56,128]{2,1,0:T(8,128)S(1)}, u32[]{:S(2)}, u32[]{:S(2)}) %all-to-all-start.1) | async-done | bytes 458784 | tf_op jit(solution)/shard_map/all_to_all | solution.py:389
  47.6 3.7 %shard_map.63 = (f32[256,256]{1,0:T(8,128)S(1)}, f32[384,128]{1,0:T(8,128)S(1)}) custom-call(f32[16,56,128]{2,1,0:T(8,128)S(1)} %all-to-all-done.1.landed, f32[8,256]{1,0:T(8,128)S(1)} %reshape.55.along, f32[256,8]{1,0:T(8,128)S(1)} %bitcast.7), custom_call_target="tpu_custom_call" | custom-call | tf_op jit(solution)/shard_map/pallas_call | solution.py:32
  51.3 0.9 shard_map.64
  52.2 4.0 %all-to-all-start.2 = ((f32[16,16,128]{2,1,0:T(8,128)}), f32[16,16,128]{2,1,0:T(8,128)S(1)}, u32[]{:S(2)}, u32[]{:S(2)}) async-start(f32[16,16,128]{2,1,0:T(8,128)} %shard_map.64), calls=%async_computation.2 | async-start | bytes 262144 | tf_op jit(solution)/shard_map/all_to_all | solution.py:389
  56.2 0.1 collective-permute-start.2
  56.3 0.1 compare_select_fusion
  56.4 1.8 %shard_map.65 = (f32[640,128]{1,0:T(8,128)S(1)}, f32[256,128]{1,0:T(8,128)S(1)}) custom-call(f32[16,56,128]{2,1,0:T(8,128)S(1)} %all-to-all-done.1.landed, f32[256,256]{1,0:T(8,128)S(1)} %get-tuple-element.27.q, f32[256,256]{1,0:T(8,128)S(1)} %get-tuple-element.25.own, f32[256,256]{1,0:T(8,128)S(1)} %collective-permute-done.other, ...), custom_call_target="tpu_custom_call" | custom-call | tf_op jit(solution)/shard_map/pallas_call | solution.py:32
  58.2 2.6 %collective-permute-done.2.ship = f32[384,128]{1,0:T(8,128)S(1)} collective-permute-done((f32[384,128]{1,0:T(8,128)S(1)}, f32[384,128]{1,0:T(8,128)S(1)}, u32[]{:S(2)}, u32[]{:S(2)}) %collective-permute-start.2) | collective-permute-done | bytes 196640 | tf_op jit(solution)/shard_map/ppermute | solution.py:407
  60.8 4.3 %all-to-all-done.2 = f32[16,16,128]{2,1,0:T(8,128)S(1)} async-done(((f32[16,16,128]{2,1,0:T(8,128)}), f32[16,16,128]{2,1,0:T(8,128)S(1)}, u32[]{:S(2)}, u32[]{:S(2)}) %all-to-all-start.2) | async-done | bytes 131104 | tf_op jit(solution)/shard_map/all_to_all | solution.py:389
  65.1 4.1 %shard_map.66 = (f32[512,128]{1,0:T(8,128)S(1)}, f32[512,128]{1,0:T(8,128)S(1)}, f32[256,256]{1,0:T(8,128)S(1)}, f32[256,256]{1,0:T(8,128)S(1)}) custom-call(f32[256,128]{1,0:T(8,128)S(1)} %bitcast.11, f32[384,128]{1,0:T(8,128)S(1)} %collective-permute-done.2.ship, f32[640,128]{1,0:T(8,128)S(1)} %get-tuple-element.29.kept, ...), custom_call_target="tpu_custom_call" | custom-call | tf_op jit(solution)/shard_map/pallas_call | solution.py:32
  69.2 0.1 collective-permute-start.3
  69.3 5.1 %collective-permute-start.4 = (f32[512,128]{1,0:T(8,128)S(1)}, f32[512,128]{1,0:T(8,128)S(1)}, u32[]{:S(2)}, u32[]{:S(2)}) collective-permute-start(f32[512,128]{1,0:T(8,128)S(1)} %get-tuple-element.31.x1), channel_id=1, source_target_pairs={{0,7},{1,0},{2,1},{3,2},{4,3},{5,4},{6,5},{7,6},{8,9},{9,10},{10,1... | collective-permute-start | bytes 786440 | tf_op jit(solution)/shard_map/ppermute | solution.py:407
  74.4 1.5 %shard_map.67 = (f32[384,128]{1,0:T(8,128)S(1)}, f32[384,128]{1,0:T(8,128)S(1)}, f32[128,128]{1,0:T(8,128)S(1)}) custom-call(f32[256,128]{1,0:T(8,128)S(1)} %get-tuple-element.32.kept, f32[256,256]{1,0:T(8,128)S(1)} %get-tuple-element.48.unit, f32[384,128]{1,0:T(8,128)S(1)} %collective-permute-done.2.ship, f32[256,256]{1,0:T(8,128)S(1)} %get-tuple-element.33.q, ...), custom_call_target="tpu_custom_call" | custom-call | tf_op jit(solution)/shard_map/pallas_call | solution.py:32
  75.9 2.3 %collective-permute-done.3.far0 = f32[512,128]{1,0:T(8,128)S(1)} collective-permute-done((f32[512,128]{1,0:T(8,128)S(1)}, f32[512,128]{1,0:T(8,128)S(1)}, u32[]{:S(2)}, u32[]{:S(2)}) %collective-permute-start.3) | collective-permute-done | bytes 262176 | tf_op jit(solution)/shard_map/ppermute | solution.py:407
  78.1 0.2 collective-permute-done.4.near1
  78.3 1.6 %shard_map.68 = f32[5,128,128]{2,1,0:T(8,128)} custom-call(f32[512,128]{1,0:T(8,128)S(1)} %collective-permute-done.3.far0, f32[512,128]{1,0:T(8,128)S(1)} %get-tuple-element.30.x0, f32[512,128]{1,0:T(8,128)S(1)} %get-tuple-element.31.x1, f32[512,128]{1,0:T(8,128)S(1)} %collective-permute-done.4.near1), custom_call_target="tpu_custom_call" | custom-call | tf_op jit(solution)/shard_map/pallas_call | solution.py:32
  79.8 3.9 %all-to-all-start.3 = ((f32[16,40,128]{2,1,0:T(8,128)}), f32[16,40,128]{2,1,0:T(8,128)S(1)}, u32[]{:S(2)}, u32[]{:S(2)}) async-start(f32[16,40,128]{2,1,0:T(8,128)} %bitcast.4), calls=%async_computation.3 | async-start | bytes 655360 | tf_op jit(solution)/shard_map/all_to_all | solution.py:389
  83.7 0.1 collective-permute-start.5
  83.8 6.5 %collective-permute-start.6 = (f32[384,128]{1,0:T(8,128)S(1)}, f32[384,128]{1,0:T(8,128)S(1)}, u32[]{:S(2)}, u32[]{:S(2)}) collective-permute-start(f32[384,128]{1,0:T(8,128)S(1)} %get-tuple-element.40.rest1), channel_id=1, source_target_pairs={{0,7},{1,0},{2,1},{3,2},{4,3},{5,4},{6,5},{7,6},{8,9},{9,10},{10,1... | collective-permute-start | bytes 589832 | tf_op jit(solution)/shard_map/ppermute | solution.py:407
  90.3 3.6 %all-to-all-done.3 = f32[16,40,128]{2,1,0:T(8,128)S(1)} async-done(((f32[16,40,128]{2,1,0:T(8,128)}), f32[16,40,128]{2,1,0:T(8,128)S(1)}, u32[]{:S(2)}, u32[]{:S(2)}) %all-to-all-start.3) | async-done | bytes 327712 | tf_op jit(solution)/shard_map/all_to_all | solution.py:389
  93.9 0.0 collective-permute-done.5.far_rest
  94.0 0.0 collective-permute-done.6.near_rest
  94.0 16.2 %all_to_all.25 = f32[16,40,128]{2,1,0:T(8,128)S(1)} all-to-all(f32[16,40,128]{2,1,0:T(8,128)S(1)} %broadcast_in_dim.20), channel_id=1, replica_groups={{0,16,32,48,64,80,96,112,128,144,160,176,192,208,224,240},{8,24,40,56,7..., dimensions={0} | all-to-all | bytes 655360 | tf_op jit(solution)/shard_map/all_to_all | solution.py:389
  110.2 9.3 %shard_map.69 = (f32[256,256]{1,0:T(8,128)S(1)}, f32[128,256]{1,0:T(8,128)S(1)}, f32[384,256]{1,0:T(8,128)S(1)}) custom-call(f32[5,128,128]{2,1,0:T(8,128)S(1)} %bitcast.10, f32[128,128]{1,0:T(8,128)S(1)} %get-tuple-element.42.inner, f32[512,128]{1,0:T(8,128)S(1)} %collective-permute-done.3.far0, f32[512,128]{1,0:T(8,128)S(1)} %get-tuple-element.30.x0, ...), custom_call_target="tpu_custom_call" | custom-call | tf_op jit(solution)/shard_map/pallas_call | solution.py:32
  119.5 10.9 %collective-permute-start.7 = (f32[384,256]{1,0:T(8,128)S(1)}, f32[384,256]{1,0:T(8,128)S(1)}, u32[]{:S(2)}, u32[]{:S(2)}) collective-permute-start(f32[384,256]{1,0:T(8,128)S(1)} %get-tuple-element.45), channel_id=1, source_target_pairs={{0,8},{8,0},{16,24},{24,16},{32,40},{40,32},{48,56},{56,48},{64,72... | collective-permute-start | bytes 1179656 | tf_op jit(solution)/shard_map/ppermute | solution.py:397
  130.4 1.3 %collective-permute-done.7.got = f32[384,256]{1,0:T(8,128)S(1)} collective-permute-done((f32[384,256]{1,0:T(8,128)S(1)}, f32[384,256]{1,0:T(8,128)S(1)}, u32[]{:S(2)}, u32[]{:S(2)}) %collective-permute-start.7) | collective-permute-done | bytes 393248 | tf_op jit(solution)/shard_map/ppermute | solution.py:397
  131.7 1.0 shard_map.70
  (7 shorter events, 0.1 us)
Async XLA Ops:
  0.6 1.0 copy-start
  1.7 0.7 copy-start.1
  2.4 1.9 %collective-permute-start = (f32[256,256]{1,0:T(8,128)S(1)}, f32[256,256]{1,0:T(8,128)S(1)}, u32[]{:S(2)}, u32[]{:S(2)}) collective-permute-start(f32[256,256]{1,0:T(8,128)S(1)} %get-tuple-element.26), channel_id=1, source_target_pairs={{0,8},{8,0},{16,24},{24,16},{32,40},{40,32},{48,56},{56,48},{64,72... | collective-permute-start | bytes 786440 | tf_op jit(solution)/shard_map/ppermute | solution.py:397
  4.4 12.7 %collective-permute-start.1 = (f32[512,256]{1,0:T(8,128)S(1)}, f32[512,256]{1,0:T(8,128)S(1)}, u32[]{:S(2)}, u32[]{:S(2)}) collective-permute-start(f32[512,256]{1,0:T(8,128)S(1)} %pad_maximum_fusion), channel_id=1, source_target_pairs={{0,7},{1,0},{2,1},{3,2},{4,3},{5,4},{6,5},{7,6},{8,9},{9,10},{10,1... | collective-permute-start | bytes 1572872 | tf_op jit(solution)/shard_map/ppermute | solution.py:407
  8.7 19.4 %all-to-all-start = ((f32[16,24,128]{2,1,0:T(8,128)}), f32[16,24,128]{2,1,0:T(8,128)S(1)}, u32[]{:S(2)}, u32[]{:S(2)}) async-start(f32[16,24,128]{2,1,0:T(8,128)} %bitcast.1), calls=%async_computation | async-start | bytes 393216 | tf_op jit(solution)/shard_map/all_to_all | solution.py:389
  29.0 3.8 %copy-start.2 = (f32[256,512]{1,0:T(8,128)S(1)}, f32[256,512]{1,0:T(8,128)}, u32[]{:S(2)}) copy-start(f32[256,512]{1,0:T(8,128)} %constant.68.clone) | copy-start | bytes 1572868
  29.0 18.6 %all-to-all-start.1 = ((f32[16,56,128]{2,1,0:T(8,128)}), f32[16,56,128]{2,1,0:T(8,128)S(1)}, u32[]{:S(2)}, u32[]{:S(2)}) async-start(f32[16,56,128]{2,1,0:T(8,128)} %shard_map.62), calls=%async_computation.1 | async-start | bytes 917504 | tf_op jit(solution)/shard_map/all_to_all | solution.py:389
  32.7 0.7 copy-start.3
  52.2 12.9 %all-to-all-start.2 = ((f32[16,16,128]{2,1,0:T(8,128)}), f32[16,16,128]{2,1,0:T(8,128)S(1)}, u32[]{:S(2)}, u32[]{:S(2)}) async-start(f32[16,16,128]{2,1,0:T(8,128)} %shard_map.64), calls=%async_computation.2 | async-start | bytes 262144 | tf_op jit(solution)/shard_map/all_to_all | solution.py:389
  56.2 4.6 %collective-permute-start.2 = (f32[384,128]{1,0:T(8,128)S(1)}, f32[384,128]{1,0:T(8,128)S(1)}, u32[]{:S(2)}, u32[]{:S(2)}) collective-permute-start(f32[384,128]{1,0:T(8,128)S(1)} %get-tuple-element.28), channel_id=1, source_target_pairs={{0,7},{1,0},{2,1},{3,2},{4,3},{5,4},{6,5},{7,6},{8,9},{9,10},{10,1... | collective-permute-start | bytes 589832 | tf_op jit(solution)/shard_map/ppermute | solution.py:407
  69.2 8.9 %collective-permute-start.3 = (f32[512,128]{1,0:T(8,128)S(1)}, f32[512,128]{1,0:T(8,128)S(1)}, u32[]{:S(2)}, u32[]{:S(2)}) collective-permute-start(f32[512,128]{1,0:T(8,128)S(1)} %get-tuple-element.30.x0), channel_id=1, source_target_pairs={{0,1},{1,2},{2,3},{3,4},{4,5},{5,6},{6,7},{7,0},{8,15},{9,8},{10,9... | collective-permute-start | bytes 786440 | tf_op jit(solution)/shard_map/ppermute | solution.py:407
  69.3 9.0 %collective-permute-start.4 = (f32[512,128]{1,0:T(8,128)S(1)}, f32[512,128]{1,0:T(8,128)S(1)}, u32[]{:S(2)}, u32[]{:S(2)}) collective-permute-start(f32[512,128]{1,0:T(8,128)S(1)} %get-tuple-element.31.x1), channel_id=1, source_target_pairs={{0,7},{1,0},{2,1},{3,2},{4,3},{5,4},{6,5},{7,6},{8,9},{9,10},{10,1... | collective-permute-start | bytes 786440 | tf_op jit(solution)/shard_map/ppermute | solution.py:407
  79.8 14.1 %all-to-all-start.3 = ((f32[16,40,128]{2,1,0:T(8,128)}), f32[16,40,128]{2,1,0:T(8,128)S(1)}, u32[]{:S(2)}, u32[]{:S(2)}) async-start(f32[16,40,128]{2,1,0:T(8,128)} %bitcast.4), calls=%async_computation.3 | async-start | bytes 655360 | tf_op jit(solution)/shard_map/all_to_all | solution.py:389
  83.7 10.2 %collective-permute-start.5 = (f32[384,128]{1,0:T(8,128)S(1)}, f32[384,128]{1,0:T(8,128)S(1)}, u32[]{:S(2)}, u32[]{:S(2)}) collective-permute-start(f32[384,128]{1,0:T(8,128)S(1)} %get-tuple-element.39.rest0), channel_id=1, source_target_pairs={{0,1},{1,2},{2,3},{3,4},{4,5},{5,6},{6,7},{7,0},{8,15},{9,8},{10,9... | collective-permute-start | bytes 589832 | tf_op jit(solution)/shard_map/ppermute | solution.py:407
  83.8 10.1 %collective-permute-start.6 = (f32[384,128]{1,0:T(8,128)S(1)}, f32[384,128]{1,0:T(8,128)S(1)}, u32[]{:S(2)}, u32[]{:S(2)}) collective-permute-start(f32[384,128]{1,0:T(8,128)S(1)} %get-tuple-element.40.rest1), channel_id=1, source_target_pairs={{0,7},{1,0},{2,1},{3,2},{4,3},{5,4},{6,5},{7,6},{8,9},{9,10},{10,1... | collective-permute-start | bytes 589832 | tf_op jit(solution)/shard_map/ppermute | solution.py:407
  119.5 12.2 %collective-permute-start.7 = (f32[384,256]{1,0:T(8,128)S(1)}, f32[384,256]{1,0:T(8,128)S(1)}, u32[]{:S(2)}, u32[]{:S(2)}) collective-permute-start(f32[384,256]{1,0:T(8,128)S(1)} %get-tuple-element.45), channel_id=1, source_target_pairs={{0,8},{8,0},{16,24},{24,16},{32,40},{40,32},{48,56},{56,48},{64,72... | collective-permute-start | bytes 1179656 | tf_op jit(solution)/shard_map/ppermute | solution.py:397

commit v7 on v6

--- a/solution.py
+++ b/solution.py
@@ -223,32 +223,40 @@
     out[0], out[1], out[2] = gram[:BLOCK, :BLOCK], gram[:BLOCK, BLOCK:], gram[BLOCK:, BLOCK:]
 
 
-def mixed_kernel(own, other, near, out):
+def mixed_kernel(own, other, near, keep, give):
     x = jnp.concatenate([own[...], other[...]], axis=0)
     mixed = dot_t(near[...], x)
-    out[0], out[1] = mixed[:, :BLOCK], mixed[:, BLOCK:]
-
-
-def spread_kernel(parts, mixed, out):
+    upper = lax.axis_index("rows") // 2 % 2 == 1
+    for half in range(2):
+        at = slice(half * BLOCK, (half + 1) * BLOCK)
+        top, bottom = mixed[:BLOCK, at], mixed[BLOCK:, at]
+        keep[half] = jnp.where(upper, bottom, top)
+        give[half] = jnp.where(upper, top, bottom)
+
+
+def spread_kernel(parts, keep, got, out):
     n, m = parts.shape[0], parts.shape[1]
-    size = N // n
+    size = BLOCK // n
     total = parts[0]
     for k in range(1, n):
         total = total + parts[k]
+    mixed = [keep[half] + got[half] for half in range(2)]
     for k in range(n):
         out[k, :m] = total
         for half in range(2):
-            at = pl.ds(m + half * size, size)
-            out[k, at] = mixed[half, k * size : (k + 1) * size]
+            out[k, pl.ds(m + half * size, size)] = mixed[half][k * size : (k + 1) * size]
 
 
 def share_kernel(landed, q, out):
     n, m = landed.shape[0], 3 * BLOCK // landed.shape[0]
-    size = N // n
-    total = landed[0, m:]
-    for k in range(1, n):
-        total = total + landed[k, m:]
-    mine = dot(beside(total[:size], total[size:]), q[:, :BLOCK])
+    size = BLOCK // n
+    rows = []
+    for upper in range(2):
+        total = landed[upper, m:]
+        for k in range(upper + 2, n, 2):
+            total = total + landed[k, m:]
+        rows.append(beside(total[:size], total[size:]))
+    mine = dot(jnp.concatenate(rows, axis=0), q[:, :BLOCK])
     for k in range(n):
         out[k] = mine
 
@@ -277,7 +285,10 @@
 
 def second_kernel(mixed, ship, kept, near, along, down, x0, x1, gram_out, q_out, turned1, *scratch):
     q1 = ship[:N]
-    cross = dot_t(mixed[...], q1)
+    size = mixed.shape[1] // 2
+    cross = dot_t(mixed[:, :size].reshape(BLOCK, BLOCK), q1[:BLOCK]) + dot_t(
+        mixed[:, size:].reshape(BLOCK, BLOCK), q1[BLOCK:]
+    )
     rows = near.shape[0]
     gram = joined(kept[rows:], cross, ship[N:])
     gram_out[...] = gram
@@ -326,11 +337,10 @@
     near_rest,
     along,
     down,
-    mine_data,
-    mine_basis,
     theirs,
     ya,
     yb,
+    q_out,
     *scratch,
 ):
     basis_rows = far_rest.shape[0] - BLOCK
@@ -357,16 +367,25 @@
                 out[to] = dot_3(beside(left[at], right[at]), q)
 
     (q,) = solves([gram], 3, along, down, scratch, quarter)
-    y = dot_3(beside(ya[...], yb[...]), q)
+    q_out[...] = q
+    half = data_rows // 2
+    theirs[:half] = turned_rows(ya, yb, q, half, half)
+    theirs[half:] = turned_rows(ya, yb, q, data_rows + basis_rows // 2, basis_rows // 2)
+
+
+def turned_rows(ya, yb, q, first, count):
+    at = pl.ds(first, count)
+    y = dot_3(beside(ya[at], yb[at]), q)
     swap = on_core_1()
-    y = beside(
+    return beside(
         jnp.where(swap, y[:, BLOCK:], y[:, :BLOCK]), jnp.where(swap, y[:, :BLOCK], y[:, BLOCK:])
     )
-    rows, height = mine_data.shape[0], mine_basis.shape[0]
-    mine_data[...] = y[:rows]
-    theirs[:rows] = y[rows : 2 * rows]
-    mine_basis[...] = y[2 * rows : 2 * rows + height]
-    theirs[rows:] = y[2 * rows + height :]
+
+
+def mine_kernel(ya, yb, q, data, basis):
+    rows, height = data.shape[0], basis.shape[0]
+    data[...] = turned_rows(ya, yb, q[...], 0, rows)
+    basis[...] = turned_rows(ya, yb, q[...], 2 * rows, height)
 
 
 def place_kernel(got, mine_data, mine_basis, data, basis):
@@ -393,8 +412,8 @@
     return trade(jnp.broadcast_to(mine[None], (n,) + mine.shape))
 
 
-def other_core(x):
-    return lax.ppermute(x, "rows", [(i, i ^ 1) for i in range(lax.axis_size("rows"))])
+def across(x, bit):
+    return lax.ppermute(x, "rows", [(i, i ^ bit) for i in range(lax.axis_size("rows"))])
 
 
 def along_pairs(x, sign):
@@ -415,7 +434,7 @@
     height = W // lax.axis_size("rows")
     pair = (shape(rows, N), shape(rows, N))
     own, send = call(start_kernel, pair, [], sample, column_scale.reshape(1, width))
-    other = other_core(send)
+    other = across(send, 1)
     near = along_pairs(jnp.concatenate([own, other], axis=0), 1)
     near_col = (col + jnp.where(core == 0, 1, -1)) % n_pairs
 
@@ -432,17 +451,20 @@
     down = along.T
 
     chips = lax.axis_size("rows") // 2
-    gram_rows, mixed_rows = 3 * BLOCK // chips, 2 * N // chips
+    gram_rows, mixed_rows = 3 * BLOCK // chips, N // chips
     gram = call(gram_kernel, shape(3, BLOCK, BLOCK), [], own, other)
     parts = trade(gram.reshape(chips, -1, BLOCK))
-    mixed = call(mixed_kernel, shape(2, N, BLOCK), [], own, other, near)
+    blocks = shape(2, BLOCK, BLOCK)
+    keep, give = call(mixed_kernel, (blocks, blocks), [], own, other, near)
+    got = across(give, 2)
     landed = trade(
         call(
             spread_kernel,
             shape(chips, gram_rows + mixed_rows, BLOCK),
             [],
             parts,
-            mixed,
+            keep,
+            got,
         )
     )
     q, ship = call(
@@ -455,7 +477,6 @@
     )
     ship = along_pairs(ship, 1)
     mixed = trade(call(share_kernel, shape(chips, N // chips, BLOCK), [], landed, q))
-    mixed = mixed.reshape(N, BLOCK)
     half, half_basis = shape(2 * rows, BLOCK), shape(2 * height, BLOCK)
     kept, kept_basis = call(
         keep_kernel,
@@ -497,10 +518,11 @@
     sums = trade(cross.reshape(chips, -1, BLOCK)).sum(0)
     sums, far_rest, near_rest = lax.optimization_barrier((sums, far_rest, near_rest))
     sums = all_slices(sums, chips).reshape(5, BLOCK, BLOCK)
-    mine_data, mine_basis, theirs = call(
+    tall = shape(2 * (rows + height), BLOCK)
+    theirs, ya, yb, q = call(
         last_kernel,
-        (shape(rows, N), shape(height, N), shape(rows + height, N)),
-        [pltpu.VMEM((2 * (rows + height), BLOCK), jnp.float32)] * 2 + solve_scratch(2),
+        (shape(rows + height, N), tall, tall, shape(N, N)),
+        solve_scratch(2),
         sums,
         inner,
         far0,
@@ -514,11 +536,15 @@
         along,
         down,
     )
+    got = across(theirs, 1)
+    mine_data, mine_basis = call(
+        mine_kernel, (shape(rows, N), shape(height, N)), [], ya, yb, q
+    )
     return call(
         place_kernel,
         (shape(rows, width), shape(height, width)),
         [],
-        other_core(theirs),
+        got,
         mine_data,
         mine_basis,
     )

time: 133 us -> 129 us (0.970)
  waiting for transfers between devices: 39.4 us -> 31.4 us
  starting transfers between devices: 46.4 us -> 50.4 us
    all_to_all x4, waiting for transfers between devices: 31.8 us -> 25.8 us  [trade(): return lax.all_to_all(parts, 'rows', 0, 0, axis_index_groups=groups)]
    ppermute x6, starting transfers between devices: 14.7 us -> 16.8 us  [along_pairs(): return lax.ppermute(x, ('rows', 'pairs'), route)]
    ppermute x2 -> x3, starting transfers between devices: 11.6 us -> 13.6 us  [across(): lax.ppermute(x, 'rows', [(i, i ^ bit) for i in range(lax.axis_size('rows'...]
    ppermute x6, waiting for transfers between devices: 5.04 us -> 3.5 us  [along_pairs(): return lax.ppermute(x, ('rows', 'pairs'), route)]
    pallas_call x12 -> x13, Pallas kernels: 26.8 us -> 26.9 us  [call(): pl.pallas_call(kernel, out_shape=out_shape, in_specs=[VMEM] * len(operand...]
  transfers between devices with their start and end apart: 12 -> 13, of which waited for: 9 -> 9; matrix products, arithmetic and copies ran while one was open for 0% -> 1% of each run, Pallas kernels for 4% -> 4%
where the time goes in v7:
time: 129 us
  starting transfers between devices  50.4 us (39%)
  waiting for transfers between devices  31.4 us (24%)
  Pallas kernels  26.9 us (21%)
  blocking collectives  16.2 us (13%)
  local copies, waits for them, and re-layouts  2.55 us (2%)
    pallas_call x13, Pallas kernels, call(): pl.pallas_call(kernel, out_shape=out_shape, in_specs=[VMEM] * len(operand...  26.9 us
    all_to_all x4, waiting for transfers between devices, trade(): return lax.all_to_all(parts, 'rows', 0, 0, axis_index_groups=groups)  25.8 us
    all_to_all x4, starting transfers between devices, trade(): return lax.all_to_all(parts, 'rows', 0, 0, axis_index_groups=groups)  20 us
    ppermute x6, starting transfers between devices, along_pairs(): return lax.ppermute(x, ('rows', 'pairs'), route)  16.8 us
    all_to_all x1, blocking collectives, trade(): return lax.all_to_all(parts, 'rows', 0, 0, axis_index_groups=groups)  16.2 us
    ppermute x3, starting transfers between devices, across(): lax.ppermute(x, 'rows', [(i, i ^ bit) for i in range(lax.axis_size('rows'...  13.6 us
    ppermute x6, waiting for transfers between devices, along_pairs(): return lax.ppermute(x, ('rows', 'pairs'), route)  3.5 us
  transfers between devices with their start and end apart: 13, of which 9 were waited for; matrix products, arithmetic and copies ran while one was open for 1% of the time, Pallas kernels for 4%

profile of v7, /device:TPU:7, one launch (start us, length us, event | category | flops | bytes accessed | tf_op | source)
XLA Modules:
  0.0 128.9 jit_solution(12060036051815716419)
XLA Ops:
  0.6 1.0 copy-done
  1.7 0.7 copy-done.1
  2.4 0.1 shard_map.59
  2.4 0.8 collective-permute-start
  3.2 1.2 collective-permute-done.other
  4.4 2.9 %collective-permute-start.1 = (f32[512,256]{1,0:T(8,128)S(1)}, f32[512,256]{1,0:T(8,128)S(1)}, u32[]{:S(2)}, u32[]{:S(2)}) collective-permute-start(f32[512,256]{1,0:T(8,128)S(1)} %pad_maximum_fusion), channel_id=1, source_target_pairs={{0,7},{1,0},{2,1},{3,2},{4,3},{5,4},{6,5},{7,6},{8,9},{9,10},{10,1... | collective-permute-start | bytes 1572872 | tf_op jit(solution)/shard_map/ppermute | solution.py:426
  7.3 1.4 %shard_map.60 = f32[3,128,128]{2,1,0:T(8,128)} custom-call(f32[256,256]{1,0:T(8,128)S(1)} %get-tuple-element.30.own, f32[256,256]{1,0:T(8,128)S(1)} %collective-permute-done.other), custom_call_target="tpu_custom_call" | custom-call | tf_op jit(solution)/shard_map/pallas_call | solution.py:32
  8.7 8.4 %all-to-all-start = ((f32[16,24,128]{2,1,0:T(8,128)}), f32[16,24,128]{2,1,0:T(8,128)S(1)}, u32[]{:S(2)}, u32[]{:S(2)}) async-start(f32[16,24,128]{2,1,0:T(8,128)} %bitcast.1), calls=%async_computation | async-start | bytes 393216 | tf_op jit(solution)/shard_map/all_to_all | solution.py:408
  17.1 0.0 collective-permute-done.1.near
  17.1 0.7 shard_map.61
  17.8 1.4 %collective-permute-start.2 = (f32[2,128,128]{2,1,0:T(8,128)S(1)}, f32[2,128,128]{2,1,0:T(8,128)S(1)}, u32[]{:S(2)}, u32[]{:S(2)}) collective-permute-start(f32[2,128,128]{2,1,0:T(8,128)S(1)} %get-tuple-element.33), channel_id=1, source_target_pairs={{0,16},{8,24},{16,0},{24,8},{32,48},{40,56},{48,32},{56,40},{64,80... | collective-permute-start | bytes 393224 | tf_op jit(solution)/shard_map/ppermute | solution.py:416
  19.3 8.9 %all-to-all-done.parts = f32[16,24,128]{2,1,0:T(8,128)S(1)} async-done(((f32[16,24,128]{2,1,0:T(8,128)}), f32[16,24,128]{2,1,0:T(8,128)S(1)}, u32[]{:S(2)}, u32[]{:S(2)}) %all-to-all-start) | async-done | bytes 196640 | tf_op jit(solution)/shard_map/all_to_all | solution.py:408
  28.1 0.0 collective-permute-done.2.got
  28.2 0.8 shard_map.62
  28.9 3.7 %all-to-all-start.1 = ((f32[16,40,128]{2,1,0:T(8,128)}), f32[16,40,128]{2,1,0:T(8,128)S(1)}, u32[]{:S(2)}, u32[]{:S(2)}) async-start(f32[16,40,128]{2,1,0:T(8,128)} %shard_map.62), calls=%async_computation.1 | async-start | bytes 655360 | tf_op jit(solution)/shard_map/all_to_all | solution.py:408
  32.6 0.0 copy-start.3
  32.6 0.0 copy-done.2
  32.7 0.7 copy-done.3
  33.3 0.4 fusion.2
  33.7 0.1 copy.9
  33.9 9.6 %all-to-all-done.1.landed = f32[16,40,128]{2,1,0:T(8,128)S(1)} async-done(((f32[16,40,128]{2,1,0:T(8,128)}), f32[16,40,128]{2,1,0:T(8,128)S(1)}, u32[]{:S(2)}, u32[]{:S(2)}) %all-to-all-start.1) | async-done | bytes 327712 | tf_op jit(solution)/shard_map/all_to_all | solution.py:408
  43.4 3.7 %shard_map.63 = (f32[256,256]{1,0:T(8,128)S(1)}, f32[384,128]{1,0:T(8,128)S(1)}) custom-call(f32[16,40,128]{2,1,0:T(8,128)S(1)} %all-to-all-done.1.landed, f32[8,256]{1,0:T(8,128)S(1)} %reshape.52.along, f32[256,8]{1,0:T(8,128)S(1)} %bitcast.6), custom_call_target="tpu_custom_call" | custom-call | tf_op jit(solution)/shard_map/pallas_call | solution.py:32
  47.2 0.9 shard_map.64
  48.0 4.1 %all-to-all-start.2 = ((f32[16,16,128]{2,1,0:T(8,128)}), f32[16,16,128]{2,1,0:T(8,128)S(1)}, u32[]{:S(2)}, u32[]{:S(2)}) async-start(f32[16,16,128]{2,1,0:T(8,128)} %shard_map.64), calls=%async_computation.2 | async-start | bytes 262144 | tf_op jit(solution)/shard_map/all_to_all | solution.py:408
  52.2 2.2 %collective-permute-start.3 = (f32[384,128]{1,0:T(8,128)S(1)}, f32[384,128]{1,0:T(8,128)S(1)}, u32[]{:S(2)}, u32[]{:S(2)}) collective-permute-start(f32[384,128]{1,0:T(8,128)S(1)} %get-tuple-element.35), channel_id=1, source_target_pairs={{0,7},{1,0},{2,1},{3,2},{4,3},{5,4},{6,5},{7,6},{8,9},{9,10},{10,1... | collective-permute-start | bytes 589832 | tf_op jit(solution)/shard_map/ppermute | solution.py:426
  54.4 0.1 compare_select_fusion
  54.5 1.8 %shard_map.65 = (f32[640,128]{1,0:T(8,128)S(1)}, f32[256,128]{1,0:T(8,128)S(1)}) custom-call(f32[16,40,128]{2,1,0:T(8,128)S(1)} %all-to-all-done.1.landed, f32[256,256]{1,0:T(8,128)S(1)} %get-tuple-element.34.q, f32[256,256]{1,0:T(8,128)S(1)} %get-tuple-element.30.own, f32[256,256]{1,0:T(8,128)S(1)} %collective-permute-done.other, ...), custom_call_target="tpu_custom_call" | custom-call | tf_op jit(solution)/shard_map/pallas_call | solution.py:32
  56.3 0.7 collective-permute-done.3.ship
  57.0 3.8 %all-to-all-done.2.mixed = f32[16,16,128]{2,1,0:T(8,128)S(1)} async-done(((f32[16,16,128]{2,1,0:T(8,128)}), f32[16,16,128]{2,1,0:T(8,128)S(1)}, u32[]{:S(2)}, u32[]{:S(2)}) %all-to-all-start.2) | async-done | bytes 131104 | tf_op jit(solution)/shard_map/all_to_all | solution.py:408
  60.7 4.1 %shard_map.66 = (f32[512,128]{1,0:T(8,128)S(1)}, f32[512,128]{1,0:T(8,128)S(1)}, f32[256,256]{1,0:T(8,128)S(1)}, f32[256,256]{1,0:T(8,128)S(1)}) custom-call(f32[16,16,128]{2,1,0:T(8,128)S(1)} %all-to-all-done.2.mixed, f32[384,128]{1,0:T(8,128)S(1)} %collective-permute-done.3.ship, f32[640,128]{1,0:T(8,128)S(1)} %get-tuple-element.36.kept, ...), custom_call_target="tpu_custom_call" | custom-call | tf_op jit(solution)/shard_map/pallas_call | solution.py:32
  64.9 0.1 collective-permute-start.4
  65.0 5.1 %collective-permute-start.5 = (f32[512,128]{1,0:T(8,128)S(1)}, f32[512,128]{1,0:T(8,128)S(1)}, u32[]{:S(2)}, u32[]{:S(2)}) collective-permute-start(f32[512,128]{1,0:T(8,128)S(1)} %get-tuple-element.38.x1), channel_id=1, source_target_pairs={{0,7},{1,0},{2,1},{3,2},{4,3},{5,4},{6,5},{7,6},{8,9},{9,10},{10,1... | collective-permute-start | bytes 786440 | tf_op jit(solution)/shard_map/ppermute | solution.py:426
  70.1 1.5 %shard_map.67 = (f32[384,128]{1,0:T(8,128)S(1)}, f32[384,128]{1,0:T(8,128)S(1)}, f32[128,128]{1,0:T(8,128)S(1)}) custom-call(f32[256,128]{1,0:T(8,128)S(1)} %get-tuple-element.39.kept, f32[256,256]{1,0:T(8,128)S(1)} %get-tuple-element.58.unit, f32[384,128]{1,0:T(8,128)S(1)} %collective-permute-done.3.ship, f32[256,256]{1,0:T(8,128)S(1)} %get-tuple-element.40.q, ...), custom_call_target="tpu_custom_call" | custom-call | tf_op jit(solution)/shard_map/pallas_call | solution.py:32
  71.5 2.3 %collective-permute-done.4.far0 = f32[512,128]{1,0:T(8,128)S(1)} collective-permute-done((f32[512,128]{1,0:T(8,128)S(1)}, f32[512,128]{1,0:T(8,128)S(1)}, u32[]{:S(2)}, u32[]{:S(2)}) %collective-permute-start.4) | collective-permute-done | bytes 262176 | tf_op jit(solution)/shard_map/ppermute | solution.py:426
  73.8 0.5 collective-permute-done.5.near1
  74.3 1.6 %shard_map.68 = f32[5,128,128]{2,1,0:T(8,128)} custom-call(f32[512,128]{1,0:T(8,128)S(1)} %collective-permute-done.4.far0, f32[512,128]{1,0:T(8,128)S(1)} %get-tuple-element.37.x0, f32[512,128]{1,0:T(8,128)S(1)} %get-tuple-element.38.x1, f32[512,128]{1,0:T(8,128)S(1)} %collective-permute-done.5.near1), custom_call_target="tpu_custom_call" | custom-call | tf_op jit(solution)/shard_map/pallas_call | solution.py:32
  75.9 3.8 %all-to-all-start.3 = ((f32[16,40,128]{2,1,0:T(8,128)}), f32[16,40,128]{2,1,0:T(8,128)S(1)}, u32[]{:S(2)}, u32[]{:S(2)}) async-start(f32[16,40,128]{2,1,0:T(8,128)} %bitcast.3), calls=%async_computation.3 | async-start | bytes 655360 | tf_op jit(solution)/shard_map/all_to_all | solution.py:408
  79.6 0.1 collective-permute-start.6
  79.7 6.5 %collective-permute-start.7 = (f32[384,128]{1,0:T(8,128)S(1)}, f32[384,128]{1,0:T(8,128)S(1)}, u32[]{:S(2)}, u32[]{:S(2)}) collective-permute-start(f32[384,128]{1,0:T(8,128)S(1)} %get-tuple-element.47.rest1), channel_id=1, source_target_pairs={{0,7},{1,0},{2,1},{3,2},{4,3},{5,4},{6,5},{7,6},{8,9},{9,10},{10,1... | collective-permute-start | bytes 589832 | tf_op jit(solution)/shard_map/ppermute | solution.py:426
  86.2 3.6 %all-to-all-done.3 = f32[16,40,128]{2,1,0:T(8,128)S(1)} async-done(((f32[16,40,128]{2,1,0:T(8,128)}), f32[16,40,128]{2,1,0:T(8,128)S(1)}, u32[]{:S(2)}, u32[]{:S(2)}) %all-to-all-start.3) | async-done | bytes 327712 | tf_op jit(solution)/shard_map/all_to_all | solution.py:408
  89.9 0.0 collective-permute-done.6.far_rest
  89.9 0.0 collective-permute-done.7.near_rest
  89.9 16.2 %all_to_all.25 = f32[16,40,128]{2,1,0:T(8,128)S(1)} all-to-all(f32[16,40,128]{2,1,0:T(8,128)S(1)} %broadcast_in_dim.20), channel_id=1, replica_groups={{0,16,32,48,64,80,96,112,128,144,160,176,192,208,224,240},{8,24,40,56,7..., dimensions={0} | all-to-all | bytes 655360 | tf_op jit(solution)/shard_map/all_to_all | solution.py:408
  106.1 9.1 %shard_map.69 = (f32[384,256]{1,0:T(8,128)S(1)}, f32[768,128]{1,0:T(8,128)S(1)}, f32[768,128]{1,0:T(8,128)S(1)}, f32[256,256]{1,0:T(8,128)S(1)}) custom-call(f32[5,128,128]{2,1,0:T(8,128)S(1)} %bitcast.9, f32[128,128]{1,0:T(8,128)S(1)} %get-tuple-element.49.inner, f32[512,128]{1,0:T(8,128)S(1)} %collective-permute-done.4.far0, ...), custom_call_target="tpu_custom_call" | custom-call | tf_op jit(solution)/shard_map/pallas_call | solution.py:32
  115.2 11.4 %collective-permute-start.8 = (f32[384,256]{1,0:T(8,128)S(1)}, f32[384,256]{1,0:T(8,128)S(1)}, u32[]{:S(2)}, u32[]{:S(2)}) collective-permute-start(f32[384,256]{1,0:T(8,128)S(1)} %get-tuple-element.52), channel_id=1, source_target_pairs={{0,8},{8,0},{16,24},{24,16},{32,40},{40,32},{48,56},{56,48},{64,72... | collective-permute-start | bytes 1179656 | tf_op jit(solution)/shard_map/ppermute | solution.py:416
  126.6 0.3 shard_map.70
  127.0 1.0 collective-permute-done.8.got
  128.0 0.9 shard_map.71
  (10 shorter events, 0.1 us)
Async XLA Ops:
  0.6 1.0 copy-start
  1.7 0.7 copy-start.1
  2.4 1.9 %collective-permute-start = (f32[256,256]{1,0:T(8,128)S(1)}, f32[256,256]{1,0:T(8,128)S(1)}, u32[]{:S(2)}, u32[]{:S(2)}) collective-permute-start(f32[256,256]{1,0:T(8,128)S(1)} %get-tuple-element.31), channel_id=1, source_target_pairs={{0,8},{8,0},{16,24},{24,16},{32,40},{40,32},{48,56},{56,48},{64,72... | collective-permute-start | bytes 786440 | tf_op jit(solution)/shard_map/ppermute | solution.py:416
  4.4 12.7 %collective-permute-start.1 = (f32[512,256]{1,0:T(8,128)S(1)}, f32[512,256]{1,0:T(8,128)S(1)}, u32[]{:S(2)}, u32[]{:S(2)}) collective-permute-start(f32[512,256]{1,0:T(8,128)S(1)} %pad_maximum_fusion), channel_id=1, source_target_pairs={{0,7},{1,0},{2,1},{3,2},{4,3},{5,4},{6,5},{7,6},{8,9},{9,10},{10,1... | collective-permute-start | bytes 1572872 | tf_op jit(solution)/shard_map/ppermute | solution.py:426
  8.7 19.4 %all-to-all-start = ((f32[16,24,128]{2,1,0:T(8,128)}), f32[16,24,128]{2,1,0:T(8,128)S(1)}, u32[]{:S(2)}, u32[]{:S(2)}) async-start(f32[16,24,128]{2,1,0:T(8,128)} %bitcast.1), calls=%async_computation | async-start | bytes 393216 | tf_op jit(solution)/shard_map/all_to_all | solution.py:408
  17.8 10.3 %collective-permute-start.2 = (f32[2,128,128]{2,1,0:T(8,128)S(1)}, f32[2,128,128]{2,1,0:T(8,128)S(1)}, u32[]{:S(2)}, u32[]{:S(2)}) collective-permute-start(f32[2,128,128]{2,1,0:T(8,128)S(1)} %get-tuple-element.33), channel_id=1, source_target_pairs={{0,16},{8,24},{16,0},{24,8},{32,48},{40,56},{48,32},{56,40},{64,80... | collective-permute-start | bytes 393224 | tf_op jit(solution)/shard_map/ppermute | solution.py:416
  28.9 3.7 %copy-start.2 = (f32[256,512]{1,0:T(8,128)S(1)}, f32[256,512]{1,0:T(8,128)}, u32[]{:S(2)}) copy-start(f32[256,512]{1,0:T(8,128)} %constant.68.clone) | copy-start | bytes 1572868
  28.9 14.5 %all-to-all-start.1 = ((f32[16,40,128]{2,1,0:T(8,128)}), f32[16,40,128]{2,1,0:T(8,128)S(1)}, u32[]{:S(2)}, u32[]{:S(2)}) async-start(f32[16,40,128]{2,1,0:T(8,128)} %shard_map.62), calls=%async_computation.1 | async-start | bytes 655360 | tf_op jit(solution)/shard_map/all_to_all | solution.py:408
  32.6 0.7 copy-start.3
  48.0 12.7 %all-to-all-start.2 = ((f32[16,16,128]{2,1,0:T(8,128)}), f32[16,16,128]{2,1,0:T(8,128)S(1)}, u32[]{:S(2)}, u32[]{:S(2)}) async-start(f32[16,16,128]{2,1,0:T(8,128)} %shard_map.64), calls=%async_computation.2 | async-start | bytes 262144 | tf_op jit(solution)/shard_map/all_to_all | solution.py:408
  52.2 4.8 %collective-permute-start.3 = (f32[384,128]{1,0:T(8,128)S(1)}, f32[384,128]{1,0:T(8,128)S(1)}, u32[]{:S(2)}, u32[]{:S(2)}) collective-permute-start(f32[384,128]{1,0:T(8,128)S(1)} %get-tuple-element.35), channel_id=1, source_target_pairs={{0,7},{1,0},{2,1},{3,2},{4,3},{5,4},{6,5},{7,6},{8,9},{9,10},{10,1... | collective-permute-start | bytes 589832 | tf_op jit(solution)/shard_map/ppermute | solution.py:426
  64.9 8.9 %collective-permute-start.4 = (f32[512,128]{1,0:T(8,128)S(1)}, f32[512,128]{1,0:T(8,128)S(1)}, u32[]{:S(2)}, u32[]{:S(2)}) collective-permute-start(f32[512,128]{1,0:T(8,128)S(1)} %get-tuple-element.37.x0), channel_id=1, source_target_pairs={{0,1},{1,2},{2,3},{3,4},{4,5},{5,6},{6,7},{7,0},{8,15},{9,8},{10,9... | collective-permute-start | bytes 786440 | tf_op jit(solution)/shard_map/ppermute | solution.py:426
  65.0 9.3 %collective-permute-start.5 = (f32[512,128]{1,0:T(8,128)S(1)}, f32[512,128]{1,0:T(8,128)S(1)}, u32[]{:S(2)}, u32[]{:S(2)}) collective-permute-start(f32[512,128]{1,0:T(8,128)S(1)} %get-tuple-element.38.x1), channel_id=1, source_target_pairs={{0,7},{1,0},{2,1},{3,2},{4,3},{5,4},{6,5},{7,6},{8,9},{9,10},{10,1... | collective-permute-start | bytes 786440 | tf_op jit(solution)/shard_map/ppermute | solution.py:426
  75.9 14.0 %all-to-all-start.3 = ((f32[16,40,128]{2,1,0:T(8,128)}), f32[16,40,128]{2,1,0:T(8,128)S(1)}, u32[]{:S(2)}, u32[]{:S(2)}) async-start(f32[16,40,128]{2,1,0:T(8,128)} %bitcast.3), calls=%async_computation.3 | async-start | bytes 655360 | tf_op jit(solution)/shard_map/all_to_all | solution.py:408
  79.6 10.2 %collective-permute-start.6 = (f32[384,128]{1,0:T(8,128)S(1)}, f32[384,128]{1,0:T(8,128)S(1)}, u32[]{:S(2)}, u32[]{:S(2)}) collective-permute-start(f32[384,128]{1,0:T(8,128)S(1)} %get-tuple-element.46.rest0), channel_id=1, source_target_pairs={{0,1},{1,2},{2,3},{3,4},{4,5},{5,6},{6,7},{7,0},{8,15},{9,8},{10,9... | collective-permute-start | bytes 589832 | tf_op jit(solution)/shard_map/ppermute | solution.py:426
  79.7 10.1 %collective-permute-start.7 = (f32[384,128]{1,0:T(8,128)S(1)}, f32[384,128]{1,0:T(8,128)S(1)}, u32[]{:S(2)}, u32[]{:S(2)}) collective-permute-start(f32[384,128]{1,0:T(8,128)S(1)} %get-tuple-element.47.rest1), channel_id=1, source_target_pairs={{0,7},{1,0},{2,1},{3,2},{4,3},{5,4},{6,5},{7,6},{8,9},{9,10},{10,1... | collective-permute-start | bytes 589832 | tf_op jit(solution)/shard_map/ppermute | solution.py:426
  115.2 12.8 %collective-permute-start.8 = (f32[384,256]{1,0:T(8,128)S(1)}, f32[384,256]{1,0:T(8,128)S(1)}, u32[]{:S(2)}, u32[]{:S(2)}) collective-permute-start(f32[384,256]{1,0:T(8,128)S(1)} %get-tuple-element.52), channel_id=1, source_target_pairs={{0,8},{8,0},{16,24},{24,16},{32,40},{40,32},{48,56},{56,48},{64,72... | collective-permute-start | bytes 1179656 | tf_op jit(solution)/shard_map/ppermute | solution.py:416

commit v8 on v7

--- a/solution.py
+++ b/solution.py
@@ -149,8 +149,12 @@
         c, s = angles(gpp, cross, gqq)
         a, b, c_, d_ = ga[old, k, body], gb[old, k, body], gc[old, k, body], gd[old, k, body]
         on = i0 == i1
-        c_col = jnp.sum(jnp.where(on, c, 0.0), axis=1, keepdims=True)
-        s_col = jnp.sum(jnp.where(on, s, 0.0), axis=1, keepdims=True)
+        if count == 1:
+            c_col = jnp.sum(jnp.where(on, c, 0.0), axis=1, keepdims=True)
+            s_col = jnp.sum(jnp.where(on, s, 0.0), axis=1, keepdims=True)
+        else:
+            c_col = jnp.broadcast_to(c, (BLOCK, BLOCK)).T
+            s_col = jnp.broadcast_to(s, (BLOCK, BLOCK)).T
         low = c * gpp - s * cross
         new_pp = c * low - s * (c * cross - s * gqq)
         new_qq = s * (s * gpp + c * cross) + c * (s * cross + c * gqq)
@@ -192,7 +196,11 @@
         state = [one_round(0, 1, k, *state[k]) for k in range(count)]
         return [one_round(1, 0, k, *state[k]) for k in range(count)]
 
-    lax.fori_loop(0, ROUNDS // 2, two_rounds, state)
+    if count == 1:
+        lax.fori_loop(0, ROUNDS // 2, two_rounds, state)
+    else:
+        for pair in range(ROUNDS // 2):
+            state = two_rounds(pair, state)
     turned = [
         [jnp.concatenate([top[0, k, body], bottom[0, k, body]], axis=0).T for k in range(count)]
         for top, bottom in ((qa, qc), (qb, qd))
@@ -207,9 +215,8 @@
     return lax.axis_index("rows") % 2 == 1
 
 
-def start_kernel(sample, scale, own, send):
-    x = sample[...] * scale[...]
-    blocks = [x[:, k * BLOCK : (k + 1) * BLOCK] for k in range(4)]
+def start_kernel(sample, own, send):
+    blocks = [sample[:, k * BLOCK : (k + 1) * BLOCK] for k in range(4)]
     swap = on_core_1()
     for k, far in ((0, 3), (1, 2)):
         at = slice(k * BLOCK, (k + 1) * BLOCK)
@@ -217,15 +224,22 @@
         send[:, at] = jnp.where(swap, blocks[k], blocks[far])
 
 
-def gram_kernel(own, other, out):
-    x = jnp.concatenate([own[...], other[...]], axis=0)
-    gram = dot_t(x, x)
+def gram_kernel(x, out):
+    high, middle, low = thirds(x[...])
+
+    def dot_16_t(left, right):
+        return lax.dot_general(
+            left, right, (((0,), (0,)), ((), ())), preferred_element_type=jnp.float32
+        )
+
+    wide = dot_16_t(high, beside(high, middle, low))
+    mixed = wide[:, N : 2 * N] + wide[:, 2 * N :]
+    gram = wide[:, :N] + ((mixed + mixed.T) + dot_16_t(middle, middle))
     out[0], out[1], out[2] = gram[:BLOCK, :BLOCK], gram[:BLOCK, BLOCK:], gram[BLOCK:, BLOCK:]
 
 
-def mixed_kernel(own, other, near, keep, give):
-    x = jnp.concatenate([own[...], other[...]], axis=0)
-    mixed = dot_t(near[...], x)
+def mixed_kernel(x, near, keep, give):
+    mixed = dot_t(near[...], x[...])
     upper = lax.axis_index("rows") // 2 % 2 == 1
     for half in range(2):
         at = slice(half * BLOCK, (half + 1) * BLOCK)
@@ -266,19 +280,22 @@
     return joined(sums[0], sums[1], sums[2])
 
 
-def first_kernel(landed, along, down, q_out, ship, *scratch):
+def first_kernel(landed, along, down, q_out, *scratch):
     gram = first_gram(landed, 3 * BLOCK // landed.shape[0])
     (q,) = solves([gram], 0, along, down, scratch)
     q_out[...] = q
+
+
+def ship_kernel(landed, q, ship):
     q1 = q[:, BLOCK:]
     ship[:N] = q1
-    ship[N:] = dot_t(q1, dot(gram, q1))
-
-
-def keep_kernel(landed, q, own, other, unit, kept, kept_basis):
+    ship[N:] = dot_t(q1, dot(first_gram(landed, 3 * BLOCK // landed.shape[0]), q1))
+
+
+def keep_kernel(landed, q, x, unit, kept, kept_basis):
     q0 = q[:, :BLOCK]
     rows = kept.shape[0] - BLOCK
-    kept[:rows] = dot(jnp.concatenate([own[...], other[...]], axis=0), q0)
+    kept[:rows] = dot(x[...], q0)
     kept[rows:] = dot_t(q0, dot(first_gram(landed, 3 * BLOCK // landed.shape[0]), q0))
     kept_basis[...] = dot(unit[...], q0)
 
@@ -322,6 +339,19 @@
     out[2] = both[:BLOCK, BLOCK:]
     out[3] = dot_t(f0, n1)
     out[4] = both[BLOCK:, :BLOCK]
+
+
+def last_grams(sums, inner, far_rest, rest0, rest1, near_rest):
+    basis_rows = far_rest.shape[0] - BLOCK
+    gram_a = joined(far_rest[basis_rows:], sums[0], rest1[basis_rows:])
+    gram_b = joined(rest0[basis_rows:], sums[1].T, near_rest[basis_rows:])
+    return gram_a, gram_b
+
+
+def third_kernel(sums, far_rest, rest0, rest1, near_rest, along, down, out, *scratch):
+    grams = last_grams(sums, None, far_rest, rest0, rest1, near_rest)
+    qa, qb = solves(grams, 2, along, down, scratch)
+    out[0], out[1] = qa[:, :BLOCK], qb[:, BLOCK:]
 
 
 def last_kernel(
@@ -337,6 +367,7 @@
     near_rest,
     along,
     down,
+    q_in,
     theirs,
     ya,
     yb,
@@ -344,13 +375,11 @@
     *scratch,
 ):
     basis_rows = far_rest.shape[0] - BLOCK
-    gram_a = joined(far_rest[basis_rows:], sums[0], rest1[basis_rows:])
-    gram_b = joined(rest0[basis_rows:], sums[1].T, near_rest[basis_rows:])
+    gram_a, gram_b = last_grams(sums, inner, far_rest, rest0, rest1, near_rest)
     mixed = jnp.concatenate(
         [beside(sums[2], sums[3]), beside(inner[...].T, sums[4].T)], axis=0
     )
-    qa, qb = solves([gram_a, gram_b], 2, along, down, scratch)
-    qa, qb = qa[:, :BLOCK], qb[:, BLOCK:]
+    qa, qb = q_in[0], q_in[1]
     left = dot(qa.T, beside(gram_a, mixed))
     gram = joined(dot(left[:, :N], qa), dot(left[:, N:], qb), dot(dot(qb.T, gram_b), qb))
     data_rows = far0.shape[0]
@@ -433,9 +462,11 @@
     rows, width = sample.shape
     height = W // lax.axis_size("rows")
     pair = (shape(rows, N), shape(rows, N))
-    own, send = call(start_kernel, pair, [], sample, column_scale.reshape(1, width))
-    other = across(send, 1)
-    near = along_pairs(jnp.concatenate([own, other], axis=0), 1)
+    own, send = call(start_kernel, pair, [], sample)
+    scale = column_scale.reshape(4, BLOCK)
+    scale = jnp.where(core == 0, scale[:2], scale[:1:-1]).reshape(1, N)
+    x = jnp.concatenate([own, across(send, 1)], axis=0) * scale
+    near = along_pairs(x, 1)
     near_col = (col + jnp.where(core == 0, 1, -1)) % n_pairs
 
     ids = jnp.arange(height, dtype=jnp.int32)
@@ -452,10 +483,10 @@
 
     chips = lax.axis_size("rows") // 2
     gram_rows, mixed_rows = 3 * BLOCK // chips, N // chips
-    gram = call(gram_kernel, shape(3, BLOCK, BLOCK), [], own, other)
+    gram = call(gram_kernel, shape(3, BLOCK, BLOCK), [], x)
     parts = trade(gram.reshape(chips, -1, BLOCK))
     blocks = shape(2, BLOCK, BLOCK)
-    keep, give = call(mixed_kernel, (blocks, blocks), [], own, other, near)
+    keep, give = call(mixed_kernel, (blocks, blocks), [], x, near)
     got = across(give, 2)
     landed = trade(
         call(
@@ -467,14 +498,8 @@
             got,
         )
     )
-    q, ship = call(
-        first_kernel,
-        (shape(N, N), shape(N + BLOCK, BLOCK)),
-        solve_scratch(1),
-        landed,
-        along,
-        down,
-    )
+    q = call(first_kernel, shape(N, N), solve_scratch(1), landed, along, down)
+    ship = call(ship_kernel, shape(N + BLOCK, BLOCK), [], landed, q)
     ship = along_pairs(ship, 1)
     mixed = trade(call(share_kernel, shape(chips, N // chips, BLOCK), [], landed, q))
     half, half_basis = shape(2 * rows, BLOCK), shape(2 * height, BLOCK)
@@ -484,8 +509,7 @@
         [],
         landed,
         q,
-        own,
-        other,
+        x,
         unit,
     )
     x0, x1, gram, q = call(
@@ -518,11 +542,23 @@
     sums = trade(cross.reshape(chips, -1, BLOCK)).sum(0)
     sums, far_rest, near_rest = lax.optimization_barrier((sums, far_rest, near_rest))
     sums = all_slices(sums, chips).reshape(5, BLOCK, BLOCK)
+    q = call(
+        third_kernel,
+        shape(2, N, BLOCK),
+        solve_scratch(2),
+        sums,
+        far_rest,
+        rest0,
+        rest1,
+        near_rest,
+        along,
+        down,
+    )
     tall = shape(2 * (rows + height), BLOCK)
     theirs, ya, yb, q = call(
         last_kernel,
         (shape(rows + height, N), tall, tall, shape(N, N)),
-        solve_scratch(2),
+        solve_scratch(1),
         sums,
         inner,
         far0,
@@ -535,6 +571,7 @@
         near_rest,
         along,
         down,
+        q,
     )
     got = across(theirs, 1)
     mine_data, mine_basis = call(

time: 129 us -> 128 us (level)
    pallas_call x13 -> x15, Pallas kernels: 26.9 us -> 26.1 us  [call(): pl.pallas_call(kernel, out_shape=out_shape, in_specs=[VMEM] * len(operand...]
  transfers between devices with their start and end apart: 13 -> 13, of which waited for: 9 -> 9; matrix products, arithmetic and copies ran while one was open for 1% -> 1% of each run, Pallas kernels for 4% -> 5%
where the time goes in v8:
time: 128 us; the launch traced here: 127 us
  starting transfers between devices  51.6 us (40%)
  waiting for transfers between devices  30.5 us (24%)
  Pallas kernels  26.1 us (20%)
  blocking collectives  15.9 us (12%)
  local copies, waits for them, and re-layouts  1.91 us (1%)
    pallas_call x15, Pallas kernels, call(): pl.pallas_call(kernel, out_shape=out_shape, in_specs=[VMEM] * len(operand...  26.1 us
    all_to_all x4, waiting for transfers between devices, trade(): return lax.all_to_all(parts, 'rows', 0, 0, axis_index_groups=groups)  25.1 us
    all_to_all x4, starting transfers between devices, trade(): return lax.all_to_all(parts, 'rows', 0, 0, axis_index_groups=groups)  20.9 us
    ppermute x6, starting transfers between devices, along_pairs(): return lax.ppermute(x, ('rows', 'pairs'), route)  16.7 us
    all_to_all x1, blocking collectives, trade(): return lax.all_to_all(parts, 'rows', 0, 0, axis_index_groups=groups)  15.9 us
    ppermute x3, starting transfers between devices, across(): lax.ppermute(x, 'rows', [(i, i ^ bit) for i in range(lax.axis_size('rows'...  14 us
    ppermute x6, waiting for transfers between devices, along_pairs(): return lax.ppermute(x, ('rows', 'pairs'), route)  3.3 us
  transfers between devices with their start and end apart: 13, of which 9 were waited for; matrix products, arithmetic and copies ran while one was open for 1% of the time, Pallas kernels for 5%

profile of v8, /device:TPU:7, one launch (start us, length us, event | category | flops | bytes accessed | tf_op | source)
XLA Modules:
  0.0 127.4 jit_solution(3247848329341429730)
XLA Ops:
  0.6 1.0 copy-done
  1.7 0.1 shard_map.59
  1.7 0.8 collective-permute-start
  2.5 1.1 collective-permute-done
  3.7 2.9 %collective-permute-start.1 = (f32[512,256]{1,0:T(8,128)S(1)}, f32[512,256]{1,0:T(8,128)S(1)}, u32[]{:S(2)}, u32[]{:S(2)}) collective-permute-start(f32[512,256]{1,0:T(8,128)S(1)} %maximum_multiply_fusion.x), channel_id=1, source_target_pairs={{0,7},{1,0},{2,1},{3,2},{4,3},{5,4},{6,5},{7,6},{8,9},{9,10},{10,1... | collective-permute-start | bytes 1572872 | tf_op jit(solution)/shard_map/ppermute | solution.py:455
  6.6 1.2 shard_map.60
  7.8 8.4 %all-to-all-start = ((f32[16,24,128]{2,1,0:T(8,128)}), f32[16,24,128]{2,1,0:T(8,128)S(1)}, u32[]{:S(2)}, u32[]{:S(2)}) async-start(f32[16,24,128]{2,1,0:T(8,128)} %bitcast.3), calls=%async_computation | async-start | bytes 393216 | tf_op jit(solution)/shard_map/all_to_all | solution.py:437
  16.2 0.0 collective-permute-done.1.near
  16.3 0.7 shard_map.61
  17.0 1.4 %collective-permute-start.2 = (f32[2,128,128]{2,1,0:T(8,128)S(1)}, f32[2,128,128]{2,1,0:T(8,128)S(1)}, u32[]{:S(2)}, u32[]{:S(2)}) collective-permute-start(f32[2,128,128]{2,1,0:T(8,128)S(1)} %get-tuple-element.31), channel_id=1, source_target_pairs={{0,16},{8,24},{16,0},{24,8},{32,48},{40,56},{48,32},{56,40},{64,80... | collective-permute-start | bytes 393224 | tf_op jit(solution)/shard_map/ppermute | solution.py:445
  18.4 8.9 %all-to-all-done.parts = f32[16,24,128]{2,1,0:T(8,128)S(1)} async-done(((f32[16,24,128]{2,1,0:T(8,128)}), f32[16,24,128]{2,1,0:T(8,128)S(1)}, u32[]{:S(2)}, u32[]{:S(2)}) %all-to-all-start) | async-done | bytes 196640 | tf_op jit(solution)/shard_map/all_to_all | solution.py:437
  27.3 0.0 collective-permute-done.2.got
  27.3 0.8 shard_map.62
  28.0 3.7 %all-to-all-start.1 = ((f32[16,40,128]{2,1,0:T(8,128)}), f32[16,40,128]{2,1,0:T(8,128)S(1)}, u32[]{:S(2)}, u32[]{:S(2)}) async-start(f32[16,40,128]{2,1,0:T(8,128)} %shard_map.62), calls=%async_computation.1 | async-start | bytes 655360 | tf_op jit(solution)/shard_map/all_to_all | solution.py:437
  31.8 0.0 copy-start.2
  31.8 0.7 copy-done.2
  32.4 0.4 fusion.2
  32.8 0.1 copy.10
  33.0 9.5 %all-to-all-done.1.landed = f32[16,40,128]{2,1,0:T(8,128)S(1)} async-done(((f32[16,40,128]{2,1,0:T(8,128)}), f32[16,40,128]{2,1,0:T(8,128)S(1)}, u32[]{:S(2)}, u32[]{:S(2)}) %all-to-all-start.1) | async-done | bytes 327712 | tf_op jit(solution)/shard_map/all_to_all | solution.py:437
  42.5 2.8 %shard_map.63.q = f32[256,256]{1,0:T(8,128)S(1)} custom-call(f32[16,40,128]{2,1,0:T(8,128)S(1)} %all-to-all-done.1.landed, f32[8,256]{1,0:T(8,128)S(1)} %reshape.69.along, f32[256,8]{1,0:T(8,128)S(1)} %bitcast.13), custom_call_target="tpu_custom_call" | custom-call | tf_op jit(solution)/shard_map/pallas_call | solution.py:32
  45.4 0.9 shard_map.64
  46.2 4.1 %all-to-all-start.2 = ((f32[16,16,128]{2,1,0:T(8,128)}), f32[16,16,128]{2,1,0:T(8,128)S(1)}, u32[]{:S(2)}, u32[]{:S(2)}) async-start(f32[16,16,128]{2,1,0:T(8,128)} %shard_map.64), calls=%async_computation.2 | async-start | bytes 262144 | tf_op jit(solution)/shard_map/all_to_all | solution.py:437
  50.4 0.8 shard_map.65
  51.2 2.4 %collective-permute-start.3 = (f32[384,128]{1,0:T(8,128)S(1)}, f32[384,128]{1,0:T(8,128)S(1)}, u32[]{:S(2)}, u32[]{:S(2)}) collective-permute-start(f32[384,128]{1,0:T(8,128)S(1)} %shard_map.65), channel_id=1, source_target_pairs={{0,7},{1,0},{2,1},{3,2},{4,3},{5,4},{6,5},{7,6},{8,9},{9,10},{10,1... | collective-permute-start | bytes 589832 | tf_op jit(solution)/shard_map/ppermute | solution.py:455
  53.6 0.1 compare_select_fusion
  53.7 1.8 %shard_map.66 = (f32[640,128]{1,0:T(8,128)S(1)}, f32[256,128]{1,0:T(8,128)S(1)}) custom-call(f32[16,40,128]{2,1,0:T(8,128)S(1)} %all-to-all-done.1.landed, f32[256,256]{1,0:T(8,128)S(1)} %shard_map.63.q, f32[512,256]{1,0:T(8,128)S(1)} %maximum_multiply_fusion.x, f32[256,256]{1,0:T(8,128)S(1)} %get-tuple-element.55.unit), custom_call_target="tpu_custom_call" | custom-call | tf_op jit(solution)/shard_map/pallas_call | solution.py:32
  55.5 0.7 collective-permute-done.3.ship
  56.2 2.7 %all-to-all-done.2.mixed = f32[16,16,128]{2,1,0:T(8,128)S(1)} async-done(((f32[16,16,128]{2,1,0:T(8,128)}), f32[16,16,128]{2,1,0:T(8,128)S(1)}, u32[]{:S(2)}, u32[]{:S(2)}) %all-to-all-start.2) | async-done | bytes 131104 | tf_op jit(solution)/shard_map/all_to_all | solution.py:437
  58.9 4.1 %shard_map.67 = (f32[512,128]{1,0:T(8,128)S(1)}, f32[512,128]{1,0:T(8,128)S(1)}, f32[256,256]{1,0:T(8,128)S(1)}, f32[256,256]{1,0:T(8,128)S(1)}) custom-call(f32[16,16,128]{2,1,0:T(8,128)S(1)} %all-to-all-done.2.mixed, f32[384,128]{1,0:T(8,128)S(1)} %collective-permute-done.3.ship, f32[640,128]{1,0:T(8,128)S(1)} %get-tuple-element.32.kept, ...), custom_call_target="tpu_custom_call" | custom-call | tf_op jit(solution)/shard_map/pallas_call | solution.py:32
  63.1 0.1 collective-permute-start.4
  63.2 5.1 %collective-permute-start.5 = (f32[512,128]{1,0:T(8,128)S(1)}, f32[512,128]{1,0:T(8,128)S(1)}, u32[]{:S(2)}, u32[]{:S(2)}) collective-permute-start(f32[512,128]{1,0:T(8,128)S(1)} %get-tuple-element.34.x1), channel_id=1, source_target_pairs={{0,7},{1,0},{2,1},{3,2},{4,3},{5,4},{6,5},{7,6},{8,9},{9,10},{10,1... | collective-permute-start | bytes 786440 | tf_op jit(solution)/shard_map/ppermute | solution.py:455
  68.2 1.5 %shard_map.68 = (f32[384,128]{1,0:T(8,128)S(1)}, f32[384,128]{1,0:T(8,128)S(1)}, f32[128,128]{1,0:T(8,128)S(1)}) custom-call(f32[256,128]{1,0:T(8,128)S(1)} %get-tuple-element.35.kept, f32[256,256]{1,0:T(8,128)S(1)} %get-tuple-element.54.unit, f32[384,128]{1,0:T(8,128)S(1)} %collective-permute-done.3.ship, f32[256,256]{1,0:T(8,128)S(1)} %get-tuple-element.36.q, ...), custom_call_target="tpu_custom_call" | custom-call | tf_op jit(solution)/shard_map/pallas_call | solution.py:32
  69.7 2.3 %collective-permute-done.4.far0 = f32[512,128]{1,0:T(8,128)S(1)} collective-permute-done((f32[512,128]{1,0:T(8,128)S(1)}, f32[512,128]{1,0:T(8,128)S(1)}, u32[]{:S(2)}, u32[]{:S(2)}) %collective-permute-start.4) | collective-permute-done | bytes 262176 | tf_op jit(solution)/shard_map/ppermute | solution.py:455
  72.0 0.3 collective-permute-done.5.near1
  72.3 1.6 %shard_map.69 = f32[5,128,128]{2,1,0:T(8,128)} custom-call(f32[512,128]{1,0:T(8,128)S(1)} %collective-permute-done.4.far0, f32[512,128]{1,0:T(8,128)S(1)} %get-tuple-element.33.x0, f32[512,128]{1,0:T(8,128)S(1)} %get-tuple-element.34.x1, f32[512,128]{1,0:T(8,128)S(1)} %collective-permute-done.5.near1), custom_call_target="tpu_custom_call" | custom-call | tf_op jit(solution)/shard_map/pallas_call | solution.py:32
  73.8 4.6 %all-to-all-start.3 = ((f32[16,40,128]{2,1,0:T(8,128)}), f32[16,40,128]{2,1,0:T(8,128)S(1)}, u32[]{:S(2)}, u32[]{:S(2)}) async-start(f32[16,40,128]{2,1,0:T(8,128)} %bitcast.5), calls=%async_computation.3 | async-start | bytes 655360 | tf_op jit(solution)/shard_map/all_to_all | solution.py:437
  78.5 0.1 collective-permute-start.6
  78.6 6.2 %collective-permute-start.7 = (f32[384,128]{1,0:T(8,128)S(1)}, f32[384,128]{1,0:T(8,128)S(1)}, u32[]{:S(2)}, u32[]{:S(2)}) collective-permute-start(f32[384,128]{1,0:T(8,128)S(1)} %get-tuple-element.43.rest1), channel_id=1, source_target_pairs={{0,7},{1,0},{2,1},{3,2},{4,3},{5,4},{6,5},{7,6},{8,9},{9,10},{10,1... | collective-permute-start | bytes 589832 | tf_op jit(solution)/shard_map/ppermute | solution.py:455
  84.8 3.9 %all-to-all-done.3 = f32[16,40,128]{2,1,0:T(8,128)S(1)} async-done(((f32[16,40,128]{2,1,0:T(8,128)}), f32[16,40,128]{2,1,0:T(8,128)S(1)}, u32[]{:S(2)}, u32[]{:S(2)}) %all-to-all-start.3) | async-done | bytes 327712 | tf_op jit(solution)/shard_map/all_to_all | solution.py:437
  88.7 0.0 collective-permute-done.6.far_rest
  88.7 0.0 collective-permute-done.7.near_rest
  88.8 15.9 %all_to_all.25 = f32[16,40,128]{2,1,0:T(8,128)S(1)} all-to-all(f32[16,40,128]{2,1,0:T(8,128)S(1)} %broadcast_in_dim.20), channel_id=1, replica_groups={{0,16,32,48,64,80,96,112,128,144,160,176,192,208,224,240},{8,24,40,56,7..., dimensions={0} | all-to-all | bytes 655360 | tf_op jit(solution)/shard_map/all_to_all | solution.py:437
  104.6 4.0 %shard_map.70.q_in = f32[2,256,128]{2,1,0:T(8,128)S(1)} custom-call(f32[5,128,128]{2,1,0:T(8,128)S(1)} %bitcast.17, f32[384,128]{1,0:T(8,128)S(1)} %collective-permute-done.6.far_rest, f32[384,128]{1,0:T(8,128)S(1)} %get-tuple-element.42.rest0, f32[384,128]{1,0:T(8,128)S(1)} %get-tuple-element.43.rest1, f32[384,128]{1,0:T(8,128)S(1)} %collective-permute-done.7.near_rest, ...), custom_call_target="tpu_custom_call" | custom-call | tf_op jit(solution)/shard_map/pallas_call | solution.py:32
  108.6 4.7 %shard_map.71 = (f32[384,256]{1,0:T(8,128)S(1)}, f32[768,128]{1,0:T(8,128)S(1)}, f32[768,128]{1,0:T(8,128)S(1)}, f32[256,256]{1,0:T(8,128)S(1)}) custom-call(f32[5,128,128]{2,1,0:T(8,128)S(1)} %bitcast.18, f32[128,128]{1,0:T(8,128)S(1)} %get-tuple-element.45.inner, f32[512,128]{1,0:T(8,128)S(1)} %collective-permute-done.4.far0, ...), custom_call_target="tpu_custom_call" | custom-call | tf_op jit(solution)/shard_map/pallas_call | solution.py:32
  113.3 11.8 %collective-permute-start.8 = (f32[384,256]{1,0:T(8,128)S(1)}, f32[384,256]{1,0:T(8,128)S(1)}, u32[]{:S(2)}, u32[]{:S(2)}) collective-permute-start(f32[384,256]{1,0:T(8,128)S(1)} %get-tuple-element.48), channel_id=1, source_target_pairs={{0,8},{8,0},{16,24},{24,16},{32,40},{40,32},{48,56},{56,48},{64,72... | collective-permute-start | bytes 1179656 | tf_op jit(solution)/shard_map/ppermute | solution.py:445
  125.1 0.3 shard_map.72
  125.5 1.0 collective-permute-done.8.got
  126.5 0.9 shard_map.73
  (15 shorter events, 0.2 us)
Async XLA Ops:
  0.6 1.0 copy-start
  1.7 0.8 copy-start.3
  1.7 1.9 %collective-permute-start = (f32[256,256]{1,0:T(8,128)S(1)}, f32[256,256]{1,0:T(8,128)S(1)}, u32[]{:S(2)}, u32[]{:S(2)}) collective-permute-start(f32[256,256]{1,0:T(8,128)S(1)} %get-tuple-element.29), channel_id=1, source_target_pairs={{0,8},{8,0},{16,24},{24,16},{32,40},{40,32},{48,56},{56,48},{64,72... | collective-permute-start | bytes 786440 | tf_op jit(solution)/shard_map/ppermute | solution.py:445
  3.7 12.5 %collective-permute-start.1 = (f32[512,256]{1,0:T(8,128)S(1)}, f32[512,256]{1,0:T(8,128)S(1)}, u32[]{:S(2)}, u32[]{:S(2)}) collective-permute-start(f32[512,256]{1,0:T(8,128)S(1)} %maximum_multiply_fusion.x), channel_id=1, source_target_pairs={{0,7},{1,0},{2,1},{3,2},{4,3},{5,4},{6,5},{7,6},{8,9},{9,10},{10,1... | collective-permute-start | bytes 1572872 | tf_op jit(solution)/shard_map/ppermute | solution.py:455
  7.8 19.5 %all-to-all-start = ((f32[16,24,128]{2,1,0:T(8,128)}), f32[16,24,128]{2,1,0:T(8,128)S(1)}, u32[]{:S(2)}, u32[]{:S(2)}) async-start(f32[16,24,128]{2,1,0:T(8,128)} %bitcast.3), calls=%async_computation | async-start | bytes 393216 | tf_op jit(solution)/shard_map/all_to_all | solution.py:437
  17.0 10.3 %collective-permute-start.2 = (f32[2,128,128]{2,1,0:T(8,128)S(1)}, f32[2,128,128]{2,1,0:T(8,128)S(1)}, u32[]{:S(2)}, u32[]{:S(2)}) collective-permute-start(f32[2,128,128]{2,1,0:T(8,128)S(1)} %get-tuple-element.31), channel_id=1, source_target_pairs={{0,16},{8,24},{16,0},{24,8},{32,48},{40,56},{48,32},{56,40},{64,80... | collective-permute-start | bytes 393224 | tf_op jit(solution)/shard_map/ppermute | solution.py:445
  28.0 3.7 %copy-start.1 = (f32[256,512]{1,0:T(8,128)S(1)}, f32[256,512]{1,0:T(8,128)}, u32[]{:S(2)}) copy-start(f32[256,512]{1,0:T(8,128)} %constant.68.clone) | copy-start | bytes 1572868
  28.0 14.5 %all-to-all-start.1 = ((f32[16,40,128]{2,1,0:T(8,128)}), f32[16,40,128]{2,1,0:T(8,128)S(1)}, u32[]{:S(2)}, u32[]{:S(2)}) async-start(f32[16,40,128]{2,1,0:T(8,128)} %shard_map.62), calls=%async_computation.1 | async-start | bytes 655360 | tf_op jit(solution)/shard_map/all_to_all | solution.py:437
  31.8 0.7 copy-start.2
  46.2 12.7 %all-to-all-start.2 = ((f32[16,16,128]{2,1,0:T(8,128)}), f32[16,16,128]{2,1,0:T(8,128)S(1)}, u32[]{:S(2)}, u32[]{:S(2)}) async-start(f32[16,16,128]{2,1,0:T(8,128)} %shard_map.64), calls=%async_computation.2 | async-start | bytes 262144 | tf_op jit(solution)/shard_map/all_to_all | solution.py:437
  51.2 5.0 %collective-permute-start.3 = (f32[384,128]{1,0:T(8,128)S(1)}, f32[384,128]{1,0:T(8,128)S(1)}, u32[]{:S(2)}, u32[]{:S(2)}) collective-permute-start(f32[384,128]{1,0:T(8,128)S(1)} %shard_map.65), channel_id=1, source_target_pairs={{0,7},{1,0},{2,1},{3,2},{4,3},{5,4},{6,5},{7,6},{8,9},{9,10},{10,1... | collective-permute-start | bytes 589832 | tf_op jit(solution)/shard_map/ppermute | solution.py:455
  63.1 8.9 %collective-permute-start.4 = (f32[512,128]{1,0:T(8,128)S(1)}, f32[512,128]{1,0:T(8,128)S(1)}, u32[]{:S(2)}, u32[]{:S(2)}) collective-permute-start(f32[512,128]{1,0:T(8,128)S(1)} %get-tuple-element.33.x0), channel_id=1, source_target_pairs={{0,1},{1,2},{2,3},{3,4},{4,5},{5,6},{6,7},{7,0},{8,15},{9,8},{10,9... | collective-permute-start | bytes 786440 | tf_op jit(solution)/shard_map/ppermute | solution.py:455
  63.2 9.1 %collective-permute-start.5 = (f32[512,128]{1,0:T(8,128)S(1)}, f32[512,128]{1,0:T(8,128)S(1)}, u32[]{:S(2)}, u32[]{:S(2)}) collective-permute-start(f32[512,128]{1,0:T(8,128)S(1)} %get-tuple-element.34.x1), channel_id=1, source_target_pairs={{0,7},{1,0},{2,1},{3,2},{4,3},{5,4},{6,5},{7,6},{8,9},{9,10},{10,1... | collective-permute-start | bytes 786440 | tf_op jit(solution)/shard_map/ppermute | solution.py:455
  73.8 14.8 %all-to-all-start.3 = ((f32[16,40,128]{2,1,0:T(8,128)}), f32[16,40,128]{2,1,0:T(8,128)S(1)}, u32[]{:S(2)}, u32[]{:S(2)}) async-start(f32[16,40,128]{2,1,0:T(8,128)} %bitcast.5), calls=%async_computation.3 | async-start | bytes 655360 | tf_op jit(solution)/shard_map/all_to_all | solution.py:437
  78.5 10.2 %collective-permute-start.6 = (f32[384,128]{1,0:T(8,128)S(1)}, f32[384,128]{1,0:T(8,128)S(1)}, u32[]{:S(2)}, u32[]{:S(2)}) collective-permute-start(f32[384,128]{1,0:T(8,128)S(1)} %get-tuple-element.42.rest0), channel_id=1, source_target_pairs={{0,1},{1,2},{2,3},{3,4},{4,5},{5,6},{6,7},{7,0},{8,15},{9,8},{10,9... | collective-permute-start | bytes 589832 | tf_op jit(solution)/shard_map/ppermute | solution.py:455
  78.6 10.1 %collective-permute-start.7 = (f32[384,128]{1,0:T(8,128)S(1)}, f32[384,128]{1,0:T(8,128)S(1)}, u32[]{:S(2)}, u32[]{:S(2)}) collective-permute-start(f32[384,128]{1,0:T(8,128)S(1)} %get-tuple-element.43.rest1), channel_id=1, source_target_pairs={{0,7},{1,0},{2,1},{3,2},{4,3},{5,4},{6,5},{7,6},{8,9},{9,10},{10,1... | collective-permute-start | bytes 589832 | tf_op jit(solution)/shard_map/ppermute | solution.py:455
  113.3 13.1 %collective-permute-start.8 = (f32[384,256]{1,0:T(8,128)S(1)}, f32[384,256]{1,0:T(8,128)S(1)}, u32[]{:S(2)}, u32[]{:S(2)}) collective-permute-start(f32[384,256]{1,0:T(8,128)S(1)} %get-tuple-element.48), channel_id=1, source_target_pairs={{0,8},{8,0},{16,24},{24,16},{32,40},{40,32},{48,56},{56,48},{64,72... | collective-permute-start | bytes 1179656 | tf_op jit(solution)/shard_map/ppermute | solution.py:445

commit v9 on v8

--- a/solution.py
+++ b/solution.py
@@ -475,6 +475,7 @@
     unit = jnp.where(row_ids == places + 2 * N * col, 1.0, 0.0).astype(jnp.float32)
     near_unit = jnp.where(row_ids == places + 2 * N * near_col, 1.0, 0.0).astype(jnp.float32)
 
+    near, inner_order = lax.optimization_barrier((near, inner_order))
     order = ((inner_order + core * BLOCK) % N).astype(jnp.float32)
     table = np.eye(N)[:, np.concatenate([arrangement(0), arrangement(ROUNDS)])]
     table = jnp.asarray(table.astype(np.float32))
@@ -488,6 +489,9 @@
     blocks = shape(2, BLOCK, BLOCK)
     keep, give = call(mixed_kernel, (blocks, blocks), [], x, near)
     got = across(give, 2)
+    keep, got, along, down, unit, near_unit = lax.optimization_barrier(
+        (keep, got, along, down, unit, near_unit)
+    )
     landed = trade(
         call(
             spread_kernel,
@@ -537,10 +541,10 @@
         gram,
     )
     far0, near1, rest0, rest1 = lax.optimization_barrier((far0, near1, rest0, rest1))
-    far_rest, near_rest = along_pairs(rest0, -1), along_pairs(rest1, 1)
     cross = call(cross_kernel, shape(5, BLOCK, BLOCK), [], far0, x0, x1, near1)
     sums = trade(cross.reshape(chips, -1, BLOCK)).sum(0)
-    sums, far_rest, near_rest = lax.optimization_barrier((sums, far_rest, near_rest))
+    sums, rest0, rest1, inner = lax.optimization_barrier((sums, rest0, rest1, inner))
+    far_rest, near_rest = along_pairs(rest0, -1), along_pairs(rest1, 1)
     sums = all_slices(sums, chips).reshape(5, BLOCK, BLOCK)
     q = call(
         third_kernel,

time: 128 us -> 124 us (0.969)
  blocking collectives: 15.9 us -> 30.1 us
  waiting for transfers between devices: 30.5 us -> 18.2 us
  starting transfers between devices: 51.6 us -> 46.6 us
  Pallas kernels: 26.1 us -> 24.7 us
    all_to_all x4 -> x3, waiting for transfers between devices: 25.1 us -> 7.14 us  [trade(): return lax.all_to_all(parts, 'rows', 0, 0, axis_index_groups=groups)]
    all_to_all x1 -> x2, blocking collectives: 15.9 us -> 30.1 us  [trade(): return lax.all_to_all(parts, 'rows', 0, 0, axis_index_groups=groups)]
    all_to_all x4 -> x3, starting transfers between devices: 20.9 us -> 15.9 us  [trade(): return lax.all_to_all(parts, 'rows', 0, 0, axis_index_groups=groups)]
    ppermute x6, waiting for transfers between devices: 3.3 us -> 6.29 us  [along_pairs(): return lax.ppermute(x, ('rows', 'pairs'), route)]
    ppermute x3, waiting for transfers between devices: 2.13 us -> 4.8 us  [across(): lax.ppermute(x, 'rows', [(i, i ^ bit) for i in range(lax.axis_size('rows'...]
    ppermute x3, starting transfers between devices: 14 us -> 12.3 us  [across(): lax.ppermute(x, 'rows', [(i, i ^ bit) for i in range(lax.axis_size('rows'...]
    ppermute x6, starting transfers between devices: 16.7 us -> 18.4 us  [along_pairs(): return lax.ppermute(x, ('rows', 'pairs'), route)]
    pallas_call x15, Pallas kernels: 26.1 us -> 24.7 us  [call(): pl.pallas_call(kernel, out_shape=out_shape, in_specs=[VMEM] * len(operand...]
  transfers between devices with their start and end apart: 13 -> 12, of which waited for: 9 -> 9; matrix products, arithmetic and copies ran while one was open for 1% -> 1% of each run, Pallas kernels for 5% -> 5%
where the time goes in v9:
time: 124 us; the launch traced here: 123 us
  starting transfers between devices  46.6 us (38%)
  blocking collectives  30.1 us (24%)
  Pallas kernels  24.7 us (20%)
  waiting for transfers between devices  18.2 us (15%)
  local copies, waits for them, and re-layouts  1.98 us (2%)
    all_to_all x2, blocking collectives, trade(): return lax.all_to_all(parts, 'rows', 0, 0, axis_index_groups=groups)  30.1 us
    pallas_call x15, Pallas kernels, call(): pl.pallas_call(kernel, out_shape=out_shape, in_specs=[VMEM] * len(operand...  24.7 us
    ppermute x6, starting transfers between devices, along_pairs(): return lax.ppermute(x, ('rows', 'pairs'), route)  18.4 us
    all_to_all x3, starting transfers between devices, trade(): return lax.all_to_all(parts, 'rows', 0, 0, axis_index_groups=groups)  15.9 us
    ppermute x3, starting transfers between devices, across(): lax.ppermute(x, 'rows', [(i, i ^ bit) for i in range(lax.axis_size('rows'...  12.3 us
    all_to_all x3, waiting for transfers between devices, trade(): return lax.all_to_all(parts, 'rows', 0, 0, axis_index_groups=groups)  7.14 us
    ppermute x6, waiting for transfers between devices, along_pairs(): return lax.ppermute(x, ('rows', 'pairs'), route)  6.29 us
    ppermute x3, waiting for transfers between devices, across(): lax.ppermute(x, 'rows', [(i, i ^ bit) for i in range(lax.axis_size('rows'...  4.8 us
  transfers between devices with their start and end apart: 12, of which 9 were waited for; matrix products, arithmetic and copies ran while one was open for 1% of the time, Pallas kernels for 5%

profile of v9, /device:TPU:7, one launch (start us, length us, event | category | flops | bytes accessed | tf_op | source)
XLA Modules:
  0.0 123.0 jit_solution(15132806606145840524)
XLA Ops:
  0.6 0.0 copy-start
  0.6 1.0 copy-done
  1.7 0.1 shard_map.59
  1.7 0.8 collective-permute-start
  2.5 1.1 collective-permute-done
  3.7 2.9 %collective-permute-start.1 = (f32[512,256]{1,0:T(8,128)S(1)}, f32[512,256]{1,0:T(8,128)S(1)}, u32[]{:S(2)}, u32[]{:S(2)}) collective-permute-start(f32[512,256]{1,0:T(8,128)S(1)} %maximum_multiply_fusion.x), channel_id=1, source_target_pairs={{0,7},{1,0},{2,1},{3,2},{4,3},{5,4},{6,5},{7,6},{8,9},{9,10},{10,1... | collective-permute-start | bytes 1572872 | tf_op jit(solution)/shard_map/ppermute | solution.py:455
  6.6 1.2 shard_map.60
  7.9 8.4 %all-to-all-start = ((f32[16,24,128]{2,1,0:T(8,128)}), f32[16,24,128]{2,1,0:T(8,128)S(1)}, u32[]{:S(2)}, u32[]{:S(2)}) async-start(f32[16,24,128]{2,1,0:T(8,128)} %bitcast.3), calls=%async_computation | async-start | bytes 393216 | tf_op jit(solution)/shard_map/all_to_all | solution.py:437
  16.3 0.1 compare_select_fusion
  16.4 0.0 copy-start.1
  16.4 0.0 collective-permute-done.1.near
  16.4 0.0 copy-start.2
  16.4 0.7 shard_map.61
  17.1 1.5 %collective-permute-start.2 = (f32[2,128,128]{2,1,0:T(8,128)S(1)}, f32[2,128,128]{2,1,0:T(8,128)S(1)}, u32[]{:S(2)}, u32[]{:S(2)}) collective-permute-start(f32[2,128,128]{2,1,0:T(8,128)S(1)} %get-tuple-element.41), channel_id=1, source_target_pairs={{0,16},{8,24},{16,0},{24,8},{32,48},{40,56},{48,32},{56,40},{64,80... | collective-permute-start | bytes 393224 | tf_op jit(solution)/shard_map/ppermute | solution.py:445
  18.6 0.4 fusion.2
  19.0 0.1 copy.10
  19.1 2.7 %collective-permute-done.2.got = f32[2,128,128]{2,1,0:T(8,128)S(1)} collective-permute-done((f32[2,128,128]{2,1,0:T(8,128)S(1)}, f32[2,128,128]{2,1,0:T(8,128)S(1)}, u32[]{:S(2)}, u32[]{:S(2)}) %collective-permute-start.2) | collective-permute-done | bytes 131104 | tf_op jit(solution)/shard_map/ppermute | solution.py:445
  21.8 5.5 %all-to-all-done.parts = f32[16,24,128]{2,1,0:T(8,128)S(1)} async-done(((f32[16,24,128]{2,1,0:T(8,128)}), f32[16,24,128]{2,1,0:T(8,128)S(1)}, u32[]{:S(2)}, u32[]{:S(2)}) %all-to-all-start) | async-done | bytes 196640 | tf_op jit(solution)/shard_map/all_to_all | solution.py:437
  27.3 13.0 %all_to_all.25.landed = f32[16,40,128]{2,1,0:T(8,128)S(1)} all-to-all(f32[16,40,128]{2,1,0:T(8,128)S(1)} %shard_map.62), channel_id=1, replica_groups={{0,16,32,48,64,80,96,112,128,144,160,176,192,208,224,240},{8,24,40,56,7..., dimensions={0} | all-to-all | bytes 655360 | tf_op jit(solution)/shard_map/all_to_all | solution.py:437
  40.4 2.8 %shard_map.63.q = f32[256,256]{1,0:T(8,128)S(1)} custom-call(f32[16,40,128]{2,1,0:T(8,128)S(1)} %all_to_all.25.landed, f32[8,256]{1,0:T(8,128)S(1)} %reshape.69.along, f32[256,8]{1,0:T(8,128)S(1)} %bitcast.13), custom_call_target="tpu_custom_call" | custom-call | tf_op jit(solution)/shard_map/pallas_call | solution.py:32
  43.2 0.9 shard_map.64
  44.1 3.9 %all-to-all-start.2 = ((f32[16,16,128]{2,1,0:T(8,128)}), f32[16,16,128]{2,1,0:T(8,128)S(1)}, u32[]{:S(2)}, u32[]{:S(2)}) async-start(f32[16,16,128]{2,1,0:T(8,128)} %shard_map.64), calls=%async_computation.2 | async-start | bytes 262144 | tf_op jit(solution)/shard_map/all_to_all | solution.py:437
  48.0 0.8 shard_map.65
  48.8 3.7 %collective-permute-start.3 = (f32[384,128]{1,0:T(8,128)S(1)}, f32[384,128]{1,0:T(8,128)S(1)}, u32[]{:S(2)}, u32[]{:S(2)}) collective-permute-start(f32[384,128]{1,0:T(8,128)S(1)} %shard_map.65), channel_id=1, source_target_pairs={{0,7},{1,0},{2,1},{3,2},{4,3},{5,4},{6,5},{7,6},{8,9},{9,10},{10,1... | collective-permute-start | bytes 589832 | tf_op jit(solution)/shard_map/ppermute | solution.py:455
  52.4 1.8 %shard_map.66 = (f32[640,128]{1,0:T(8,128)S(1)}, f32[256,128]{1,0:T(8,128)S(1)}) custom-call(f32[16,40,128]{2,1,0:T(8,128)S(1)} %all_to_all.25.landed, f32[256,256]{1,0:T(8,128)S(1)} %shard_map.63.q, f32[512,256]{1,0:T(8,128)S(1)} %maximum_multiply_fusion.x, f32[256,256]{1,0:T(8,128)S(1)} %get-tuple-element.47.unit), custom_call_target="tpu_custom_call" | custom-call | tf_op jit(solution)/shard_map/pallas_call | solution.py:32
  54.2 0.8 collective-permute-done.3.ship
  55.1 1.4 %all-to-all-done.2.mixed = f32[16,16,128]{2,1,0:T(8,128)S(1)} async-done(((f32[16,16,128]{2,1,0:T(8,128)}), f32[16,16,128]{2,1,0:T(8,128)S(1)}, u32[]{:S(2)}, u32[]{:S(2)}) %all-to-all-start.2) | async-done | bytes 131104 | tf_op jit(solution)/shard_map/all_to_all | solution.py:437
  56.4 4.1 %shard_map.67 = (f32[512,128]{1,0:T(8,128)S(1)}, f32[512,128]{1,0:T(8,128)S(1)}, f32[256,256]{1,0:T(8,128)S(1)}, f32[256,256]{1,0:T(8,128)S(1)}) custom-call(f32[16,16,128]{2,1,0:T(8,128)S(1)} %all-to-all-done.2.mixed, f32[384,128]{1,0:T(8,128)S(1)} %collective-permute-done.3.ship, f32[640,128]{1,0:T(8,128)S(1)} %get-tuple-element.48.kept, ...), custom_call_target="tpu_custom_call" | custom-call | tf_op jit(solution)/shard_map/pallas_call | solution.py:32
  60.6 1.8 %collective-permute-start.4 = (f32[512,128]{1,0:T(8,128)S(1)}, f32[512,128]{1,0:T(8,128)S(1)}, u32[]{:S(2)}, u32[]{:S(2)}) collective-permute-start(f32[512,128]{1,0:T(8,128)S(1)} %get-tuple-element.49.x0), channel_id=1, source_target_pairs={{0,1},{1,2},{2,3},{3,4},{4,5},{5,6},{6,7},{7,0},{8,15},{9,8},{10,9... | collective-permute-start | bytes 786440 | tf_op jit(solution)/shard_map/ppermute | solution.py:455
  62.4 3.4 %collective-permute-start.5 = (f32[512,128]{1,0:T(8,128)S(1)}, f32[512,128]{1,0:T(8,128)S(1)}, u32[]{:S(2)}, u32[]{:S(2)}) collective-permute-start(f32[512,128]{1,0:T(8,128)S(1)} %get-tuple-element.50.x1), channel_id=1, source_target_pairs={{0,7},{1,0},{2,1},{3,2},{4,3},{5,4},{6,5},{7,6},{8,9},{9,10},{10,1... | collective-permute-start | bytes 786440 | tf_op jit(solution)/shard_map/ppermute | solution.py:455
  65.7 1.5 %shard_map.68 = (f32[384,128]{1,0:T(8,128)S(1)}, f32[384,128]{1,0:T(8,128)S(1)}, f32[128,128]{1,0:T(8,128)S(1)}) custom-call(f32[256,128]{1,0:T(8,128)S(1)} %get-tuple-element.51.kept, f32[256,256]{1,0:T(8,128)S(1)} %get-tuple-element.52.unit, f32[384,128]{1,0:T(8,128)S(1)} %collective-permute-done.3.ship, f32[256,256]{1,0:T(8,128)S(1)} %get-tuple-element.53.q, ...), custom_call_target="tpu_custom_call" | custom-call | tf_op jit(solution)/shard_map/pallas_call | solution.py:32
  67.2 2.3 %collective-permute-done.4.far0 = f32[512,128]{1,0:T(8,128)S(1)} collective-permute-done((f32[512,128]{1,0:T(8,128)S(1)}, f32[512,128]{1,0:T(8,128)S(1)}, u32[]{:S(2)}, u32[]{:S(2)}) %collective-permute-start.4) | collective-permute-done | bytes 262176 | tf_op jit(solution)/shard_map/ppermute | solution.py:455
  69.5 0.0 collective-permute-done.5.near1
  69.5 0.8 shard_map.69
  70.3 17.1 %all_to_all.26 = f32[16,40,128]{2,1,0:T(8,128)S(1)} all-to-all(f32[16,40,128]{2,1,0:T(8,128)S(1)} %bitcast.19), channel_id=1, replica_groups={{0,16,32,48,64,80,96,112,128,144,160,176,192,208,224,240},{8,24,40,56,7..., dimensions={0} | all-to-all | bytes 655360 | tf_op jit(solution)/shard_map/all_to_all | solution.py:437
  87.5 0.7 broadcast_in_dim.20
  88.2 3.5 %all-to-all-start.4 = ((f32[16,40,128]{2,1,0:T(8,128)}), f32[16,40,128]{2,1,0:T(8,128)S(1)}, u32[]{:S(2)}, u32[]{:S(2)}) async-start(f32[16,40,128]{2,1,0:T(8,128)} %broadcast_in_dim.20), calls=%async_computation.4 | async-start | bytes 655360 | tf_op jit(solution)/shard_map/all_to_all | solution.py:437
  91.8 0.1 collective-permute-start.6
  91.8 6.6 %collective-permute-start.7 = (f32[384,128]{1,0:T(8,128)S(1)}, f32[384,128]{1,0:T(8,128)S(1)}, u32[]{:S(2)}, u32[]{:S(2)}) collective-permute-start(f32[384,128]{1,0:T(8,128)S(1)} %get-tuple-element.65.rest1), channel_id=1, source_target_pairs={{0,7},{1,0},{2,1},{3,2},{4,3},{5,4},{6,5},{7,6},{8,9},{9,10},{10,1... | collective-permute-start | bytes 589832 | tf_op jit(solution)/shard_map/ppermute | solution.py:455
  98.4 3.2 %collective-permute-done.6.far_rest = f32[384,128]{1,0:T(8,128)S(1)} collective-permute-done((f32[384,128]{1,0:T(8,128)S(1)}, f32[384,128]{1,0:T(8,128)S(1)}, u32[]{:S(2)}, u32[]{:S(2)}) %collective-permute-start.6) | collective-permute-done | bytes 196640 | tf_op jit(solution)/shard_map/ppermute | solution.py:455
  101.6 0.0 collective-permute-done.7.near_rest
  101.6 0.2 all-to-all-done.4
  101.9 4.0 %shard_map.70.q_in = f32[2,256,128]{2,1,0:T(8,128)S(1)} custom-call(f32[5,128,128]{2,1,0:T(8,128)S(1)} %bitcast.17, f32[384,128]{1,0:T(8,128)S(1)} %collective-permute-done.6.far_rest, f32[384,128]{1,0:T(8,128)S(1)} %get-tuple-element.64.rest0, f32[384,128]{1,0:T(8,128)S(1)} %get-tuple-element.65.rest1, f32[384,128]{1,0:T(8,128)S(1)} %collective-permute-done.7.near_rest, ...), custom_call_target="tpu_custom_call" | custom-call | tf_op jit(solution)/shard_map/pallas_call | solution.py:32
  105.9 4.7 %shard_map.71 = (f32[384,256]{1,0:T(8,128)S(1)}, f32[768,128]{1,0:T(8,128)S(1)}, f32[768,128]{1,0:T(8,128)S(1)}, f32[256,256]{1,0:T(8,128)S(1)}) custom-call(f32[5,128,128]{2,1,0:T(8,128)S(1)} %bitcast.18, f32[128,128]{1,0:T(8,128)S(1)} %get-tuple-element.63.inner, f32[512,128]{1,0:T(8,128)S(1)} %collective-permute-done.4.far0, ...), custom_call_target="tpu_custom_call" | custom-call | tf_op jit(solution)/shard_map/pallas_call | solution.py:32
  110.6 10.1 %collective-permute-start.8 = (f32[384,256]{1,0:T(8,128)S(1)}, f32[384,256]{1,0:T(8,128)S(1)}, u32[]{:S(2)}, u32[]{:S(2)}) collective-permute-start(f32[384,256]{1,0:T(8,128)S(1)} %get-tuple-element.66), channel_id=1, source_target_pairs={{0,8},{8,0},{16,24},{24,16},{32,40},{40,32},{48,56},{56,48},{64,72... | collective-permute-start | bytes 1179656 | tf_op jit(solution)/shard_map/ppermute | solution.py:445
  120.7 0.3 shard_map.72
  121.0 1.0 collective-permute-done.8.got
  122.0 0.9 shard_map.73
  (14 shorter events, 0.2 us)
Async XLA Ops:
  0.6 1.0 copy-start
  1.7 0.8 copy-start.3
  1.7 1.9 %collective-permute-start = (f32[256,256]{1,0:T(8,128)S(1)}, f32[256,256]{1,0:T(8,128)S(1)}, u32[]{:S(2)}, u32[]{:S(2)}) collective-permute-start(f32[256,256]{1,0:T(8,128)S(1)} %get-tuple-element.38), channel_id=1, source_target_pairs={{0,8},{8,0},{16,24},{24,16},{32,40},{40,32},{48,56},{56,48},{64,72... | collective-permute-start | bytes 786440 | tf_op jit(solution)/shard_map/ppermute | solution.py:445
  3.7 12.7 %collective-permute-start.1 = (f32[512,256]{1,0:T(8,128)S(1)}, f32[512,256]{1,0:T(8,128)S(1)}, u32[]{:S(2)}, u32[]{:S(2)}) collective-permute-start(f32[512,256]{1,0:T(8,128)S(1)} %maximum_multiply_fusion.x), channel_id=1, source_target_pairs={{0,7},{1,0},{2,1},{3,2},{4,3},{5,4},{6,5},{7,6},{8,9},{9,10},{10,1... | collective-permute-start | bytes 1572872 | tf_op jit(solution)/shard_map/ppermute | solution.py:455
  7.9 19.5 %all-to-all-start = ((f32[16,24,128]{2,1,0:T(8,128)}), f32[16,24,128]{2,1,0:T(8,128)S(1)}, u32[]{:S(2)}, u32[]{:S(2)}) async-start(f32[16,24,128]{2,1,0:T(8,128)} %bitcast.3), calls=%async_computation | async-start | bytes 393216 | tf_op jit(solution)/shard_map/all_to_all | solution.py:437
  16.4 2.2 %copy-start.1 = (f32[256,512]{1,0:T(8,128)S(1)}, f32[256,512]{1,0:T(8,128)}, u32[]{:S(2)}) copy-start(f32[256,512]{1,0:T(8,128)} %constant.68.clone) | copy-start | bytes 1572868
  16.4 2.2 %copy-start.2 = (s32[4,256]{1,0:T(4,128)S(1)}, s32[4,256]{1,0:T(4,128)}, u32[]{:S(2)}) copy-start(s32[4,256]{1,0:T(4,128)} %param.6) | copy-start | bytes 12292
  17.1 4.7 %collective-permute-start.2 = (f32[2,128,128]{2,1,0:T(8,128)S(1)}, f32[2,128,128]{2,1,0:T(8,128)S(1)}, u32[]{:S(2)}, u32[]{:S(2)}) collective-permute-start(f32[2,128,128]{2,1,0:T(8,128)S(1)} %get-tuple-element.41), channel_id=1, source_target_pairs={{0,16},{8,24},{16,0},{24,8},{32,48},{40,56},{48,32},{56,40},{64,80... | collective-permute-start | bytes 393224 | tf_op jit(solution)/shard_map/ppermute | solution.py:445
  44.1 12.4 %all-to-all-start.2 = ((f32[16,16,128]{2,1,0:T(8,128)}), f32[16,16,128]{2,1,0:T(8,128)S(1)}, u32[]{:S(2)}, u32[]{:S(2)}) async-start(f32[16,16,128]{2,1,0:T(8,128)} %shard_map.64), calls=%async_computation.2 | async-start | bytes 262144 | tf_op jit(solution)/shard_map/all_to_all | solution.py:437
  48.8 6.3 %collective-permute-start.3 = (f32[384,128]{1,0:T(8,128)S(1)}, f32[384,128]{1,0:T(8,128)S(1)}, u32[]{:S(2)}, u32[]{:S(2)}) collective-permute-start(f32[384,128]{1,0:T(8,128)S(1)} %shard_map.65), channel_id=1, source_target_pairs={{0,7},{1,0},{2,1},{3,2},{4,3},{5,4},{6,5},{7,6},{8,9},{9,10},{10,1... | collective-permute-start | bytes 589832 | tf_op jit(solution)/shard_map/ppermute | solution.py:455
  60.6 8.9 %collective-permute-start.4 = (f32[512,128]{1,0:T(8,128)S(1)}, f32[512,128]{1,0:T(8,128)S(1)}, u32[]{:S(2)}, u32[]{:S(2)}) collective-permute-start(f32[512,128]{1,0:T(8,128)S(1)} %get-tuple-element.49.x0), channel_id=1, source_target_pairs={{0,1},{1,2},{2,3},{3,4},{4,5},{5,6},{6,7},{7,0},{8,15},{9,8},{10,9... | collective-permute-start | bytes 786440 | tf_op jit(solution)/shard_map/ppermute | solution.py:455
  62.4 7.1 %collective-permute-start.5 = (f32[512,128]{1,0:T(8,128)S(1)}, f32[512,128]{1,0:T(8,128)S(1)}, u32[]{:S(2)}, u32[]{:S(2)}) collective-permute-start(f32[512,128]{1,0:T(8,128)S(1)} %get-tuple-element.50.x1), channel_id=1, source_target_pairs={{0,7},{1,0},{2,1},{3,2},{4,3},{5,4},{6,5},{7,6},{8,9},{9,10},{10,1... | collective-permute-start | bytes 786440 | tf_op jit(solution)/shard_map/ppermute | solution.py:455
  88.2 13.7 %all-to-all-start.4 = ((f32[16,40,128]{2,1,0:T(8,128)}), f32[16,40,128]{2,1,0:T(8,128)S(1)}, u32[]{:S(2)}, u32[]{:S(2)}) async-start(f32[16,40,128]{2,1,0:T(8,128)} %broadcast_in_dim.20), calls=%async_computation.4 | async-start | bytes 655360 | tf_op jit(solution)/shard_map/all_to_all | solution.py:437
  91.8 9.9 %collective-permute-start.6 = (f32[384,128]{1,0:T(8,128)S(1)}, f32[384,128]{1,0:T(8,128)S(1)}, u32[]{:S(2)}, u32[]{:S(2)}) collective-permute-start(f32[384,128]{1,0:T(8,128)S(1)} %get-tuple-element.64.rest0), channel_id=1, source_target_pairs={{0,1},{1,2},{2,3},{3,4},{4,5},{5,6},{6,7},{7,0},{8,15},{9,8},{10,9... | collective-permute-start | bytes 589832 | tf_op jit(solution)/shard_map/ppermute | solution.py:455
  91.8 9.8 %collective-permute-start.7 = (f32[384,128]{1,0:T(8,128)S(1)}, f32[384,128]{1,0:T(8,128)S(1)}, u32[]{:S(2)}, u32[]{:S(2)}) collective-permute-start(f32[384,128]{1,0:T(8,128)S(1)} %get-tuple-element.65.rest1), channel_id=1, source_target_pairs={{0,7},{1,0},{2,1},{3,2},{4,3},{5,4},{6,5},{7,6},{8,9},{9,10},{10,1... | collective-permute-start | bytes 589832 | tf_op jit(solution)/shard_map/ppermute | solution.py:455
  110.6 11.5 %collective-permute-start.8 = (f32[384,256]{1,0:T(8,128)S(1)}, f32[384,256]{1,0:T(8,128)S(1)}, u32[]{:S(2)}, u32[]{:S(2)}) collective-permute-start(f32[384,256]{1,0:T(8,128)S(1)} %get-tuple-element.66), channel_id=1, source_target_pairs={{0,8},{8,0},{16,24},{24,16},{32,40},{40,32},{48,56},{56,48},{64,72... | collective-permute-start | bytes 1179656 | tf_op jit(solution)/shard_map/ppermute | solution.py:445

commit v10 on v9

--- a/solution.py
+++ b/solution.py
@@ -197,7 +197,10 @@
         return [one_round(1, 0, k, *state[k]) for k in range(count)]
 
     if count == 1:
-        lax.fori_loop(0, ROUNDS // 2, two_rounds, state)
+        def four_rounds(i, held):
+            return two_rounds(2 * i + 1, two_rounds(2 * i, held))
+
+        lax.fori_loop(0, ROUNDS // 4, four_rounds, state)
     else:
         for pair in range(ROUNDS // 2):
             state = two_rounds(pair, state)
@@ -289,7 +292,7 @@
 def ship_kernel(landed, q, ship):
     q1 = q[:, BLOCK:]
     ship[:N] = q1
-    ship[N:] = dot_t(q1, dot(first_gram(landed, 3 * BLOCK // landed.shape[0]), q1))
+    ship[N:] = dot(dot(q1.T, first_gram(landed, 3 * BLOCK // landed.shape[0])), q1)
 
 
 def keep_kernel(landed, q, x, unit, kept, kept_basis):
@@ -303,9 +306,8 @@
 def second_kernel(mixed, ship, kept, near, along, down, x0, x1, gram_out, q_out, turned1, *scratch):
     q1 = ship[:N]
     size = mixed.shape[1] // 2
-    cross = dot_t(mixed[:, :size].reshape(BLOCK, BLOCK), q1[:BLOCK]) + dot_t(
-        mixed[:, size:].reshape(BLOCK, BLOCK), q1[BLOCK:]
-    )
+    halves = [mixed[:, :size].reshape(BLOCK, BLOCK), mixed[:, size:].reshape(BLOCK, BLOCK)]
+    cross = dot(jnp.concatenate(halves, axis=0).T, q1)
     rows = near.shape[0]
     gram = joined(kept[rows:], cross, ship[N:])
     gram_out[...] = gram
@@ -528,7 +530,8 @@
         down,
     )
 
-    far0, near1 = along_pairs(x0, -1), along_pairs(x1, 1)
+    near1 = along_pairs(x1, 1)
+    far0 = along_pairs(x0, -1)
     rest = shape(2 * height + BLOCK, BLOCK)
     rest0, rest1, inner = call(
         basis_kernel,

time: 124 us -> 123 us (level)
  no operation moved by 1% of the time
where the time goes in v10:
time: 123 us
  starting transfers between devices  46.5 us (38%)
  blocking collectives  30 us (24%)
  Pallas kernels  24.3 us (20%)
  waiting for transfers between devices  18.3 us (15%)
  local copies, waits for them, and re-layouts  1.98 us (2%)
    all_to_all x2, blocking collectives, trade(): return lax.all_to_all(parts, 'rows', 0, 0, axis_index_groups=groups)  30 us
    pallas_call x15, Pallas kernels, call(): pl.pallas_call(kernel, out_shape=out_shape, in_specs=[VMEM] * len(operand...  24.3 us
    ppermute x6, starting transfers between devices, along_pairs(): return lax.ppermute(x, ('rows', 'pairs'), route)  18.4 us
    all_to_all x3, starting transfers between devices, trade(): return lax.all_to_all(parts, 'rows', 0, 0, axis_index_groups=groups)  15.9 us
    ppermute x3, starting transfers between devices, across(): lax.ppermute(x, 'rows', [(i, i ^ bit) for i in range(lax.axis_size('rows'...  12.3 us
    all_to_all x3, waiting for transfers between devices, trade(): return lax.all_to_all(parts, 'rows', 0, 0, axis_index_groups=groups)  7.25 us
    ppermute x6, waiting for transfers between devices, along_pairs(): return lax.ppermute(x, ('rows', 'pairs'), route)  6.29 us
    ppermute x3, waiting for transfers between devices, across(): lax.ppermute(x, 'rows', [(i, i ^ bit) for i in range(lax.axis_size('rows'...  4.8 us
  transfers between devices with their start and end apart: 12, of which 9 were waited for; matrix products, arithmetic and copies ran while one was open for 1% of the time, Pallas kernels for 5%

profile of v10, /device:TPU:7, one launch (start us, length us, event | category | flops | bytes accessed | tf_op | source)
XLA Modules:
  0.0 122.6 jit_solution(16944446116909255081)
XLA Ops:
  0.6 0.0 copy-start
  0.6 1.0 copy-done
  1.7 0.1 shard_map.59
  1.7 0.8 collective-permute-start
  2.5 1.1 collective-permute-done
  3.7 2.9 %collective-permute-start.1 = (f32[512,256]{1,0:T(8,128)S(1)}, f32[512,256]{1,0:T(8,128)S(1)}, u32[]{:S(2)}, u32[]{:S(2)}) collective-permute-start(f32[512,256]{1,0:T(8,128)S(1)} %maximum_multiply_fusion.x), channel_id=1, source_target_pairs={{0,7},{1,0},{2,1},{3,2},{4,3},{5,4},{6,5},{7,6},{8,9},{9,10},{10,1... | collective-permute-start | bytes 1572872 | tf_op jit(solution)/shard_map/ppermute | solution.py:457
  6.6 1.2 shard_map.60
  7.9 8.4 %all-to-all-start = ((f32[16,24,128]{2,1,0:T(8,128)}), f32[16,24,128]{2,1,0:T(8,128)S(1)}, u32[]{:S(2)}, u32[]{:S(2)}) async-start(f32[16,24,128]{2,1,0:T(8,128)} %bitcast.3), calls=%async_computation | async-start | bytes 393216 | tf_op jit(solution)/shard_map/all_to_all | solution.py:439
  16.3 0.1 compare_select_fusion
  16.4 0.0 copy-start.1
  16.4 0.0 collective-permute-done.1.near
  16.4 0.0 copy-start.2
  16.4 0.7 shard_map.61
  17.1 1.5 %collective-permute-start.2 = (f32[2,128,128]{2,1,0:T(8,128)S(1)}, f32[2,128,128]{2,1,0:T(8,128)S(1)}, u32[]{:S(2)}, u32[]{:S(2)}) collective-permute-start(f32[2,128,128]{2,1,0:T(8,128)S(1)} %get-tuple-element.41), channel_id=1, source_target_pairs={{0,16},{8,24},{16,0},{24,8},{32,48},{40,56},{48,32},{56,40},{64,80... | collective-permute-start | bytes 393224 | tf_op jit(solution)/shard_map/ppermute | solution.py:447
  18.6 0.4 fusion.2
  19.0 0.1 copy.10
  19.1 2.7 %collective-permute-done.2.got = f32[2,128,128]{2,1,0:T(8,128)S(1)} collective-permute-done((f32[2,128,128]{2,1,0:T(8,128)S(1)}, f32[2,128,128]{2,1,0:T(8,128)S(1)}, u32[]{:S(2)}, u32[]{:S(2)}) %collective-permute-start.2) | collective-permute-done | bytes 131104 | tf_op jit(solution)/shard_map/ppermute | solution.py:447
  21.8 5.5 %all-to-all-done.parts = f32[16,24,128]{2,1,0:T(8,128)S(1)} async-done(((f32[16,24,128]{2,1,0:T(8,128)}), f32[16,24,128]{2,1,0:T(8,128)S(1)}, u32[]{:S(2)}, u32[]{:S(2)}) %all-to-all-start) | async-done | bytes 196640 | tf_op jit(solution)/shard_map/all_to_all | solution.py:439
  27.3 13.0 %all_to_all.25.landed = f32[16,40,128]{2,1,0:T(8,128)S(1)} all-to-all(f32[16,40,128]{2,1,0:T(8,128)S(1)} %shard_map.62), channel_id=1, replica_groups={{0,16,32,48,64,80,96,112,128,144,160,176,192,208,224,240},{8,24,40,56,7..., dimensions={0} | all-to-all | bytes 655360 | tf_op jit(solution)/shard_map/all_to_all | solution.py:439
  40.4 2.7 %shard_map.63.q = f32[256,256]{1,0:T(8,128)S(1)} custom-call(f32[16,40,128]{2,1,0:T(8,128)S(1)} %all_to_all.25.landed, f32[8,256]{1,0:T(8,128)S(1)} %reshape.69.along, f32[256,8]{1,0:T(8,128)S(1)} %bitcast.13), custom_call_target="tpu_custom_call" | custom-call | tf_op jit(solution)/shard_map/pallas_call | solution.py:32
  43.1 0.9 shard_map.64
  44.0 3.9 %all-to-all-start.2 = ((f32[16,16,128]{2,1,0:T(8,128)}), f32[16,16,128]{2,1,0:T(8,128)S(1)}, u32[]{:S(2)}, u32[]{:S(2)}) async-start(f32[16,16,128]{2,1,0:T(8,128)} %shard_map.64), calls=%async_computation.2 | async-start | bytes 262144 | tf_op jit(solution)/shard_map/all_to_all | solution.py:439
  47.9 0.7 shard_map.65
  48.6 3.7 %collective-permute-start.3 = (f32[384,128]{1,0:T(8,128)S(1)}, f32[384,128]{1,0:T(8,128)S(1)}, u32[]{:S(2)}, u32[]{:S(2)}) collective-permute-start(f32[384,128]{1,0:T(8,128)S(1)} %shard_map.65), channel_id=1, source_target_pairs={{0,7},{1,0},{2,1},{3,2},{4,3},{5,4},{6,5},{7,6},{8,9},{9,10},{10,1... | collective-permute-start | bytes 589832 | tf_op jit(solution)/shard_map/ppermute | solution.py:457
  52.3 1.8 %shard_map.66 = (f32[640,128]{1,0:T(8,128)S(1)}, f32[256,128]{1,0:T(8,128)S(1)}) custom-call(f32[16,40,128]{2,1,0:T(8,128)S(1)} %all_to_all.25.landed, f32[256,256]{1,0:T(8,128)S(1)} %shard_map.63.q, f32[512,256]{1,0:T(8,128)S(1)} %maximum_multiply_fusion.x, f32[256,256]{1,0:T(8,128)S(1)} %get-tuple-element.47.unit), custom_call_target="tpu_custom_call" | custom-call | tf_op jit(solution)/shard_map/pallas_call | solution.py:32
  54.1 0.8 collective-permute-done.3.ship
  54.9 1.5 %all-to-all-done.2.mixed = f32[16,16,128]{2,1,0:T(8,128)S(1)} async-done(((f32[16,16,128]{2,1,0:T(8,128)}), f32[16,16,128]{2,1,0:T(8,128)S(1)}, u32[]{:S(2)}, u32[]{:S(2)}) %all-to-all-start.2) | async-done | bytes 131104 | tf_op jit(solution)/shard_map/all_to_all | solution.py:439
  56.4 4.0 %shard_map.67 = (f32[512,128]{1,0:T(8,128)S(1)}, f32[512,128]{1,0:T(8,128)S(1)}, f32[256,256]{1,0:T(8,128)S(1)}, f32[256,256]{1,0:T(8,128)S(1)}) custom-call(f32[16,16,128]{2,1,0:T(8,128)S(1)} %all-to-all-done.2.mixed, f32[384,128]{1,0:T(8,128)S(1)} %collective-permute-done.3.ship, f32[640,128]{1,0:T(8,128)S(1)} %get-tuple-element.48.kept, ...), custom_call_target="tpu_custom_call" | custom-call | tf_op jit(solution)/shard_map/pallas_call | solution.py:32
  60.4 1.8 %collective-permute-start.4 = (f32[512,128]{1,0:T(8,128)S(1)}, f32[512,128]{1,0:T(8,128)S(1)}, u32[]{:S(2)}, u32[]{:S(2)}) collective-permute-start(f32[512,128]{1,0:T(8,128)S(1)} %get-tuple-element.49.x0), channel_id=1, source_target_pairs={{0,1},{1,2},{2,3},{3,4},{4,5},{5,6},{6,7},{7,0},{8,15},{9,8},{10,9... | collective-permute-start | bytes 786440 | tf_op jit(solution)/shard_map/ppermute | solution.py:457
  62.1 3.4 %collective-permute-start.5 = (f32[512,128]{1,0:T(8,128)S(1)}, f32[512,128]{1,0:T(8,128)S(1)}, u32[]{:S(2)}, u32[]{:S(2)}) collective-permute-start(f32[512,128]{1,0:T(8,128)S(1)} %get-tuple-element.50.x1), channel_id=1, source_target_pairs={{0,7},{1,0},{2,1},{3,2},{4,3},{5,4},{6,5},{7,6},{8,9},{9,10},{10,1... | collective-permute-start | bytes 786440 | tf_op jit(solution)/shard_map/ppermute | solution.py:457
  65.5 1.5 %shard_map.68 = (f32[384,128]{1,0:T(8,128)S(1)}, f32[384,128]{1,0:T(8,128)S(1)}, f32[128,128]{1,0:T(8,128)S(1)}) custom-call(f32[256,128]{1,0:T(8,128)S(1)} %get-tuple-element.51.kept, f32[256,256]{1,0:T(8,128)S(1)} %get-tuple-element.52.unit, f32[384,128]{1,0:T(8,128)S(1)} %collective-permute-done.3.ship, f32[256,256]{1,0:T(8,128)S(1)} %get-tuple-element.53.q, ...), custom_call_target="tpu_custom_call" | custom-call | tf_op jit(solution)/shard_map/pallas_call | solution.py:32
  67.0 2.3 %collective-permute-done.4.far0 = f32[512,128]{1,0:T(8,128)S(1)} collective-permute-done((f32[512,128]{1,0:T(8,128)S(1)}, f32[512,128]{1,0:T(8,128)S(1)}, u32[]{:S(2)}, u32[]{:S(2)}) %collective-permute-start.4) | collective-permute-done | bytes 262176 | tf_op jit(solution)/shard_map/ppermute | solution.py:457
  69.3 0.0 collective-permute-done.5.near1
  69.3 0.8 shard_map.69
  70.1 17.0 %all_to_all.26 = f32[16,40,128]{2,1,0:T(8,128)S(1)} all-to-all(f32[16,40,128]{2,1,0:T(8,128)S(1)} %bitcast.19), channel_id=1, replica_groups={{0,16,32,48,64,80,96,112,128,144,160,176,192,208,224,240},{8,24,40,56,7..., dimensions={0} | all-to-all | bytes 655360 | tf_op jit(solution)/shard_map/all_to_all | solution.py:439
  87.1 0.7 broadcast_in_dim.20
  87.9 3.5 %all-to-all-start.4 = ((f32[16,40,128]{2,1,0:T(8,128)}), f32[16,40,128]{2,1,0:T(8,128)S(1)}, u32[]{:S(2)}, u32[]{:S(2)}) async-start(f32[16,40,128]{2,1,0:T(8,128)} %broadcast_in_dim.20), calls=%async_computation.4 | async-start | bytes 655360 | tf_op jit(solution)/shard_map/all_to_all | solution.py:439
  91.4 0.1 collective-permute-start.6
  91.5 6.6 %collective-permute-start.7 = (f32[384,128]{1,0:T(8,128)S(1)}, f32[384,128]{1,0:T(8,128)S(1)}, u32[]{:S(2)}, u32[]{:S(2)}) collective-permute-start(f32[384,128]{1,0:T(8,128)S(1)} %get-tuple-element.65.rest1), channel_id=1, source_target_pairs={{0,7},{1,0},{2,1},{3,2},{4,3},{5,4},{6,5},{7,6},{8,9},{9,10},{10,1... | collective-permute-start | bytes 589832 | tf_op jit(solution)/shard_map/ppermute | solution.py:457
  98.1 3.2 %collective-permute-done.6.far_rest = f32[384,128]{1,0:T(8,128)S(1)} collective-permute-done((f32[384,128]{1,0:T(8,128)S(1)}, f32[384,128]{1,0:T(8,128)S(1)}, u32[]{:S(2)}, u32[]{:S(2)}) %collective-permute-start.6) | collective-permute-done | bytes 196640 | tf_op jit(solution)/shard_map/ppermute | solution.py:457
  101.3 0.0 collective-permute-done.7.near_rest
  101.3 0.3 all-to-all-done.4
  101.6 4.0 %shard_map.70.q_in = f32[2,256,128]{2,1,0:T(8,128)S(1)} custom-call(f32[5,128,128]{2,1,0:T(8,128)S(1)} %bitcast.17, f32[384,128]{1,0:T(8,128)S(1)} %collective-permute-done.6.far_rest, f32[384,128]{1,0:T(8,128)S(1)} %get-tuple-element.64.rest0, f32[384,128]{1,0:T(8,128)S(1)} %get-tuple-element.65.rest1, f32[384,128]{1,0:T(8,128)S(1)} %collective-permute-done.7.near_rest, ...), custom_call_target="tpu_custom_call" | custom-call | tf_op jit(solution)/shard_map/pallas_call | solution.py:32
  105.6 4.6 %shard_map.71 = (f32[384,256]{1,0:T(8,128)S(1)}, f32[768,128]{1,0:T(8,128)S(1)}, f32[768,128]{1,0:T(8,128)S(1)}, f32[256,256]{1,0:T(8,128)S(1)}) custom-call(f32[5,128,128]{2,1,0:T(8,128)S(1)} %bitcast.18, f32[128,128]{1,0:T(8,128)S(1)} %get-tuple-element.63.inner, f32[512,128]{1,0:T(8,128)S(1)} %collective-permute-done.4.far0, ...), custom_call_target="tpu_custom_call" | custom-call | tf_op jit(solution)/shard_map/pallas_call | solution.py:32
  110.2 10.1 %collective-permute-start.8 = (f32[384,256]{1,0:T(8,128)S(1)}, f32[384,256]{1,0:T(8,128)S(1)}, u32[]{:S(2)}, u32[]{:S(2)}) collective-permute-start(f32[384,256]{1,0:T(8,128)S(1)} %get-tuple-element.66), channel_id=1, source_target_pairs={{0,8},{8,0},{16,24},{24,16},{32,40},{40,32},{48,56},{56,48},{64,72... | collective-permute-start | bytes 1179656 | tf_op jit(solution)/shard_map/ppermute | solution.py:447
  120.3 0.3 shard_map.72
  120.6 1.0 collective-permute-done.8.got
  121.6 0.9 shard_map.73
  (14 shorter events, 0.2 us)
Async XLA Ops:
  0.6 1.0 copy-start
  1.7 0.8 copy-start.3
  1.7 1.9 %collective-permute-start = (f32[256,256]{1,0:T(8,128)S(1)}, f32[256,256]{1,0:T(8,128)S(1)}, u32[]{:S(2)}, u32[]{:S(2)}) collective-permute-start(f32[256,256]{1,0:T(8,128)S(1)} %get-tuple-element.38), channel_id=1, source_target_pairs={{0,8},{8,0},{16,24},{24,16},{32,40},{40,32},{48,56},{56,48},{64,72... | collective-permute-start | bytes 786440 | tf_op jit(solution)/shard_map/ppermute | solution.py:447
  3.7 12.7 %collective-permute-start.1 = (f32[512,256]{1,0:T(8,128)S(1)}, f32[512,256]{1,0:T(8,128)S(1)}, u32[]{:S(2)}, u32[]{:S(2)}) collective-permute-start(f32[512,256]{1,0:T(8,128)S(1)} %maximum_multiply_fusion.x), channel_id=1, source_target_pairs={{0,7},{1,0},{2,1},{3,2},{4,3},{5,4},{6,5},{7,6},{8,9},{9,10},{10,1... | collective-permute-start | bytes 1572872 | tf_op jit(solution)/shard_map/ppermute | solution.py:457
  7.9 19.5 %all-to-all-start = ((f32[16,24,128]{2,1,0:T(8,128)}), f32[16,24,128]{2,1,0:T(8,128)S(1)}, u32[]{:S(2)}, u32[]{:S(2)}) async-start(f32[16,24,128]{2,1,0:T(8,128)} %bitcast.3), calls=%async_computation | async-start | bytes 393216 | tf_op jit(solution)/shard_map/all_to_all | solution.py:439
  16.4 2.2 %copy-start.1 = (f32[256,512]{1,0:T(8,128)S(1)}, f32[256,512]{1,0:T(8,128)}, u32[]{:S(2)}) copy-start(f32[256,512]{1,0:T(8,128)} %constant.68.clone) | copy-start | bytes 1572868
  16.4 2.2 %copy-start.2 = (s32[4,256]{1,0:T(4,128)S(1)}, s32[4,256]{1,0:T(4,128)}, u32[]{:S(2)}) copy-start(s32[4,256]{1,0:T(4,128)} %param.6) | copy-start | bytes 12292
  17.1 4.7 %collective-permute-start.2 = (f32[2,128,128]{2,1,0:T(8,128)S(1)}, f32[2,128,128]{2,1,0:T(8,128)S(1)}, u32[]{:S(2)}, u32[]{:S(2)}) collective-permute-start(f32[2,128,128]{2,1,0:T(8,128)S(1)} %get-tuple-element.41), channel_id=1, source_target_pairs={{0,16},{8,24},{16,0},{24,8},{32,48},{40,56},{48,32},{56,40},{64,80... | collective-permute-start | bytes 393224 | tf_op jit(solution)/shard_map/ppermute | solution.py:447
  44.0 12.4 %all-to-all-start.2 = ((f32[16,16,128]{2,1,0:T(8,128)}), f32[16,16,128]{2,1,0:T(8,128)S(1)}, u32[]{:S(2)}, u32[]{:S(2)}) async-start(f32[16,16,128]{2,1,0:T(8,128)} %shard_map.64), calls=%async_computation.2 | async-start | bytes 262144 | tf_op jit(solution)/shard_map/all_to_all | solution.py:439
  48.6 6.3 %collective-permute-start.3 = (f32[384,128]{1,0:T(8,128)S(1)}, f32[384,128]{1,0:T(8,128)S(1)}, u32[]{:S(2)}, u32[]{:S(2)}) collective-permute-start(f32[384,128]{1,0:T(8,128)S(1)} %shard_map.65), channel_id=1, source_target_pairs={{0,7},{1,0},{2,1},{3,2},{4,3},{5,4},{6,5},{7,6},{8,9},{9,10},{10,1... | collective-permute-start | bytes 589832 | tf_op jit(solution)/shard_map/ppermute | solution.py:457
  60.4 8.9 %collective-permute-start.4 = (f32[512,128]{1,0:T(8,128)S(1)}, f32[512,128]{1,0:T(8,128)S(1)}, u32[]{:S(2)}, u32[]{:S(2)}) collective-permute-start(f32[512,128]{1,0:T(8,128)S(1)} %get-tuple-element.49.x0), channel_id=1, source_target_pairs={{0,1},{1,2},{2,3},{3,4},{4,5},{5,6},{6,7},{7,0},{8,15},{9,8},{10,9... | collective-permute-start | bytes 786440 | tf_op jit(solution)/shard_map/ppermute | solution.py:457
  62.1 7.1 %collective-permute-start.5 = (f32[512,128]{1,0:T(8,128)S(1)}, f32[512,128]{1,0:T(8,128)S(1)}, u32[]{:S(2)}, u32[]{:S(2)}) collective-permute-start(f32[512,128]{1,0:T(8,128)S(1)} %get-tuple-element.50.x1), channel_id=1, source_target_pairs={{0,7},{1,0},{2,1},{3,2},{4,3},{5,4},{6,5},{7,6},{8,9},{9,10},{10,1... | collective-permute-start | bytes 786440 | tf_op jit(solution)/shard_map/ppermute | solution.py:457
  87.9 13.7 %all-to-all-start.4 = ((f32[16,40,128]{2,1,0:T(8,128)}), f32[16,40,128]{2,1,0:T(8,128)S(1)}, u32[]{:S(2)}, u32[]{:S(2)}) async-start(f32[16,40,128]{2,1,0:T(8,128)} %broadcast_in_dim.20), calls=%async_computation.4 | async-start | bytes 655360 | tf_op jit(solution)/shard_map/all_to_all | solution.py:439
  91.4 9.8 %collective-permute-start.6 = (f32[384,128]{1,0:T(8,128)S(1)}, f32[384,128]{1,0:T(8,128)S(1)}, u32[]{:S(2)}, u32[]{:S(2)}) collective-permute-start(f32[384,128]{1,0:T(8,128)S(1)} %get-tuple-element.64.rest0), channel_id=1, source_target_pairs={{0,1},{1,2},{2,3},{3,4},{4,5},{5,6},{6,7},{7,0},{8,15},{9,8},{10,9... | collective-permute-start | bytes 589832 | tf_op jit(solution)/shard_map/ppermute | solution.py:457
  91.5 9.8 %collective-permute-start.7 = (f32[384,128]{1,0:T(8,128)S(1)}, f32[384,128]{1,0:T(8,128)S(1)}, u32[]{:S(2)}, u32[]{:S(2)}) collective-permute-start(f32[384,128]{1,0:T(8,128)S(1)} %get-tuple-element.65.rest1), channel_id=1, source_target_pairs={{0,7},{1,0},{2,1},{3,2},{4,3},{5,4},{6,5},{7,6},{8,9},{9,10},{10,1... | collective-permute-start | bytes 589832 | tf_op jit(solution)/shard_map/ppermute | solution.py:457
  110.2 11.4 %collective-permute-start.8 = (f32[384,256]{1,0:T(8,128)S(1)}, f32[384,256]{1,0:T(8,128)S(1)}, u32[]{:S(2)}, u32[]{:S(2)}) collective-permute-start(f32[384,256]{1,0:T(8,128)S(1)} %get-tuple-element.66), channel_id=1, source_target_pairs={{0,8},{8,0},{16,24},{24,16},{32,40},{40,32},{48,56},{56,48},{64,72... | collective-permute-start | bytes 1179656 | tf_op jit(solution)/shard_map/ppermute | solution.py:447

commit v11 on v10

--- a/solution.py
+++ b/solution.py
@@ -419,15 +419,38 @@
     basis[...] = turned_rows(ya, yb, q[...], 2 * rows, height)
 
 
-def place_kernel(got, mine_data, mine_basis, data, basis):
-    swap = on_core_1()
-    rows = mine_data.shape[0]
-    for mine, theirs, out in (
-        (mine_data[...], got[:rows], data),
-        (mine_basis[...], got[rows:], basis),
-    ):
-        out[:, :N] = jnp.where(swap, mine, theirs)
-        out[:, N:] = jnp.where(swap, theirs, mine)
+def place_kernel(got, mine_data, mine_basis, data, basis, sems):
+    core = lax.axis_index("rows") % 2
+    mine_at = pl.ds(pl.multiple_of((1 - core) * N, N), N)
+    got_at = pl.ds(pl.multiple_of(core * N, N), N)
+    rows, height = mine_data.shape[0], mine_basis.shape[0]
+    pairs = (
+        (mine_data, data.at[:, mine_at]),
+        (got.at[pl.ds(0, rows)], data.at[:, got_at]),
+        (mine_basis, basis.at[:, mine_at]),
+        (got.at[pl.ds(rows, height)], basis.at[:, got_at]),
+    )
+    copies = [
+        pltpu.make_async_copy(source, target, sems.at[k])
+        for k, (source, target) in enumerate(pairs)
+    ]
+    for copy in copies:
+        copy.start()
+    for copy in copies:
+        copy.wait()
+
+
+def place(got, mine_data, mine_basis, width):
+    rows, height = mine_data.shape[0], mine_basis.shape[0]
+    out = pl.BlockSpec(memory_space=pl.ANY)
+    return pl.pallas_call(
+        place_kernel,
+        out_shape=(shape(rows, width), shape(height, width)),
+        in_specs=[VMEM] * 3,
+        out_specs=(out, out),
+        scratch_shapes=[pltpu.SemaphoreType.DMA((4,))],
+        compiler_params=pltpu.CompilerParams(vmem_limit_bytes=40 * 2**20),
+    )(got, mine_data, mine_basis)
 
 
 def chip_groups(size):
@@ -584,14 +607,7 @@
     mine_data, mine_basis = call(
         mine_kernel, (shape(rows, N), shape(height, N)), [], ya, yb, q
     )
-    return call(
-        place_kernel,
-        (shape(rows, width), shape(height, width)),
-        [],
-        got,
-        mine_data,
-        mine_basis,
-    )
+    return place(got, mine_data, mine_basis, width)
 
 
 def solution(mesh):

time: 123 us -> 123 us (level)
    pallas_call x15 -> x14, Pallas kernels: 24.3 us -> 23.3 us  [call(): pl.pallas_call(kernel, out_shape=out_shape, in_specs=[VMEM] * len(operand...]
where the time goes in v11:
time: 123 us
  starting transfers between devices  46.5 us (38%)
  blocking collectives  30 us (24%)
  Pallas kernels  24.2 us (20%)
  waiting for transfers between devices  18.3 us (15%)
  local copies, waits for them, and re-layouts  1.98 us (2%)
    all_to_all x2, blocking collectives, trade(): return lax.all_to_all(parts, 'rows', 0, 0, axis_index_groups=groups)  30 us
    pallas_call x14, Pallas kernels, call(): pl.pallas_call(kernel, out_shape=out_shape, in_specs=[VMEM] * len(operand...  23.3 us
    ppermute x6, starting transfers between devices, along_pairs(): return lax.ppermute(x, ('rows', 'pairs'), route)  18.4 us
    all_to_all x3, starting transfers between devices, trade(): return lax.all_to_all(parts, 'rows', 0, 0, axis_index_groups=groups)  15.9 us
    ppermute x3, starting transfers between devices, across(): lax.ppermute(x, 'rows', [(i, i ^ bit) for i in range(lax.axis_size('rows'...  12.3 us
    all_to_all x3, waiting for transfers between devices, trade(): return lax.all_to_all(parts, 'rows', 0, 0, axis_index_groups=groups)  7.25 us
    ppermute x6, waiting for transfers between devices, along_pairs(): return lax.ppermute(x, ('rows', 'pairs'), route)  6.29 us
    ppermute x3, waiting for transfers between devices, across(): lax.ppermute(x, 'rows', [(i, i ^ bit) for i in range(lax.axis_size('rows'...  4.8 us
  transfers between devices with their start and end apart: 12, of which 9 were waited for; matrix products, arithmetic and copies ran while one was open for 1% of the time, Pallas kernels for 5%

profile of v11, /device:TPU:7, one launch (start us, length us, event | category | flops | bytes accessed | tf_op | source)
XLA Modules:
  0.0 122.7 jit_solution(1253324663732235615)
XLA Ops:
  0.6 0.0 copy-start
  0.6 1.0 copy-done
  1.7 0.1 shard_map.59
  1.7 0.8 collective-permute-start
  2.5 1.1 collective-permute-done
  3.7 2.9 %collective-permute-start.1 = (f32[512,256]{1,0:T(8,128)S(1)}, f32[512,256]{1,0:T(8,128)S(1)}, u32[]{:S(2)}, u32[]{:S(2)}) collective-permute-start(f32[512,256]{1,0:T(8,128)S(1)} %maximum_multiply_fusion.x), channel_id=1, source_target_pairs={{0,7},{1,0},{2,1},{3,2},{4,3},{5,4},{6,5},{7,6},{8,9},{9,10},{10,1... | collective-permute-start | bytes 1572872 | tf_op jit(solution)/shard_map/ppermute | solution.py:480
  6.6 1.2 shard_map.60
  7.9 8.4 %all-to-all-start = ((f32[16,24,128]{2,1,0:T(8,128)}), f32[16,24,128]{2,1,0:T(8,128)S(1)}, u32[]{:S(2)}, u32[]{:S(2)}) async-start(f32[16,24,128]{2,1,0:T(8,128)} %bitcast.3), calls=%async_computation | async-start | bytes 393216 | tf_op jit(solution)/shard_map/all_to_all | solution.py:462
  16.3 0.1 compare_select_fusion
  16.4 0.0 copy-start.1
  16.4 0.0 collective-permute-done.1.near
  16.4 0.0 copy-start.2
  16.4 0.7 shard_map.61
  17.1 1.5 %collective-permute-start.2 = (f32[2,128,128]{2,1,0:T(8,128)S(1)}, f32[2,128,128]{2,1,0:T(8,128)S(1)}, u32[]{:S(2)}, u32[]{:S(2)}) collective-permute-start(f32[2,128,128]{2,1,0:T(8,128)S(1)} %get-tuple-element.41), channel_id=1, source_target_pairs={{0,16},{8,24},{16,0},{24,8},{32,48},{40,56},{48,32},{56,40},{64,80... | collective-permute-start | bytes 393224 | tf_op jit(solution)/shard_map/ppermute | solution.py:470
  18.6 0.4 fusion.2
  19.0 0.1 copy.10
  19.1 2.7 %collective-permute-done.2.got = f32[2,128,128]{2,1,0:T(8,128)S(1)} collective-permute-done((f32[2,128,128]{2,1,0:T(8,128)S(1)}, f32[2,128,128]{2,1,0:T(8,128)S(1)}, u32[]{:S(2)}, u32[]{:S(2)}) %collective-permute-start.2) | collective-permute-done | bytes 131104 | tf_op jit(solution)/shard_map/ppermute | solution.py:470
  21.8 5.5 %all-to-all-done.parts = f32[16,24,128]{2,1,0:T(8,128)S(1)} async-done(((f32[16,24,128]{2,1,0:T(8,128)}), f32[16,24,128]{2,1,0:T(8,128)S(1)}, u32[]{:S(2)}, u32[]{:S(2)}) %all-to-all-start) | async-done | bytes 196640 | tf_op jit(solution)/shard_map/all_to_all | solution.py:462
  27.3 13.0 %all_to_all.25.landed = f32[16,40,128]{2,1,0:T(8,128)S(1)} all-to-all(f32[16,40,128]{2,1,0:T(8,128)S(1)} %shard_map.62), channel_id=1, replica_groups={{0,16,32,48,64,80,96,112,128,144,160,176,192,208,224,240},{8,24,40,56,7..., dimensions={0} | all-to-all | bytes 655360 | tf_op jit(solution)/shard_map/all_to_all | solution.py:462
  40.4 2.7 %shard_map.63.q = f32[256,256]{1,0:T(8,128)S(1)} custom-call(f32[16,40,128]{2,1,0:T(8,128)S(1)} %all_to_all.25.landed, f32[8,256]{1,0:T(8,128)S(1)} %reshape.69.along, f32[256,8]{1,0:T(8,128)S(1)} %bitcast.13), custom_call_target="tpu_custom_call" | custom-call | tf_op jit(solution)/shard_map/pallas_call | solution.py:32
  43.1 0.9 shard_map.64
  44.0 3.9 %all-to-all-start.2 = ((f32[16,16,128]{2,1,0:T(8,128)}), f32[16,16,128]{2,1,0:T(8,128)S(1)}, u32[]{:S(2)}, u32[]{:S(2)}) async-start(f32[16,16,128]{2,1,0:T(8,128)} %shard_map.64), calls=%async_computation.2 | async-start | bytes 262144 | tf_op jit(solution)/shard_map/all_to_all | solution.py:462
  47.9 0.7 shard_map.65
  48.6 3.7 %collective-permute-start.3 = (f32[384,128]{1,0:T(8,128)S(1)}, f32[384,128]{1,0:T(8,128)S(1)}, u32[]{:S(2)}, u32[]{:S(2)}) collective-permute-start(f32[384,128]{1,0:T(8,128)S(1)} %shard_map.65), channel_id=1, source_target_pairs={{0,7},{1,0},{2,1},{3,2},{4,3},{5,4},{6,5},{7,6},{8,9},{9,10},{10,1... | collective-permute-start | bytes 589832 | tf_op jit(solution)/shard_map/ppermute | solution.py:480
  52.3 1.8 %shard_map.66 = (f32[640,128]{1,0:T(8,128)S(1)}, f32[256,128]{1,0:T(8,128)S(1)}) custom-call(f32[16,40,128]{2,1,0:T(8,128)S(1)} %all_to_all.25.landed, f32[256,256]{1,0:T(8,128)S(1)} %shard_map.63.q, f32[512,256]{1,0:T(8,128)S(1)} %maximum_multiply_fusion.x, f32[256,256]{1,0:T(8,128)S(1)} %get-tuple-element.47.unit), custom_call_target="tpu_custom_call" | custom-call | tf_op jit(solution)/shard_map/pallas_call | solution.py:32
  54.1 0.8 collective-permute-done.3.ship
  54.9 1.5 %all-to-all-done.2.mixed = f32[16,16,128]{2,1,0:T(8,128)S(1)} async-done(((f32[16,16,128]{2,1,0:T(8,128)}), f32[16,16,128]{2,1,0:T(8,128)S(1)}, u32[]{:S(2)}, u32[]{:S(2)}) %all-to-all-start.2) | async-done | bytes 131104 | tf_op jit(solution)/shard_map/all_to_all | solution.py:462
  56.4 4.0 %shard_map.67 = (f32[512,128]{1,0:T(8,128)S(1)}, f32[512,128]{1,0:T(8,128)S(1)}, f32[256,256]{1,0:T(8,128)S(1)}, f32[256,256]{1,0:T(8,128)S(1)}) custom-call(f32[16,16,128]{2,1,0:T(8,128)S(1)} %all-to-all-done.2.mixed, f32[384,128]{1,0:T(8,128)S(1)} %collective-permute-done.3.ship, f32[640,128]{1,0:T(8,128)S(1)} %get-tuple-element.48.kept, ...), custom_call_target="tpu_custom_call" | custom-call | tf_op jit(solution)/shard_map/pallas_call | solution.py:32
  60.4 1.8 %collective-permute-start.4 = (f32[512,128]{1,0:T(8,128)S(1)}, f32[512,128]{1,0:T(8,128)S(1)}, u32[]{:S(2)}, u32[]{:S(2)}) collective-permute-start(f32[512,128]{1,0:T(8,128)S(1)} %get-tuple-element.49.x0), channel_id=1, source_target_pairs={{0,1},{1,2},{2,3},{3,4},{4,5},{5,6},{6,7},{7,0},{8,15},{9,8},{10,9... | collective-permute-start | bytes 786440 | tf_op jit(solution)/shard_map/ppermute | solution.py:480
  62.1 3.4 %collective-permute-start.5 = (f32[512,128]{1,0:T(8,128)S(1)}, f32[512,128]{1,0:T(8,128)S(1)}, u32[]{:S(2)}, u32[]{:S(2)}) collective-permute-start(f32[512,128]{1,0:T(8,128)S(1)} %get-tuple-element.50.x1), channel_id=1, source_target_pairs={{0,7},{1,0},{2,1},{3,2},{4,3},{5,4},{6,5},{7,6},{8,9},{9,10},{10,1... | collective-permute-start | bytes 786440 | tf_op jit(solution)/shard_map/ppermute | solution.py:480
  65.5 1.5 %shard_map.68 = (f32[384,128]{1,0:T(8,128)S(1)}, f32[384,128]{1,0:T(8,128)S(1)}, f32[128,128]{1,0:T(8,128)S(1)}) custom-call(f32[256,128]{1,0:T(8,128)S(1)} %get-tuple-element.51.kept, f32[256,256]{1,0:T(8,128)S(1)} %get-tuple-element.52.unit, f32[384,128]{1,0:T(8,128)S(1)} %collective-permute-done.3.ship, f32[256,256]{1,0:T(8,128)S(1)} %get-tuple-element.53.q, ...), custom_call_target="tpu_custom_call" | custom-call | tf_op jit(solution)/shard_map/pallas_call | solution.py:32
  67.0 2.3 %collective-permute-done.4.far0 = f32[512,128]{1,0:T(8,128)S(1)} collective-permute-done((f32[512,128]{1,0:T(8,128)S(1)}, f32[512,128]{1,0:T(8,128)S(1)}, u32[]{:S(2)}, u32[]{:S(2)}) %collective-permute-start.4) | collective-permute-done | bytes 262176 | tf_op jit(solution)/shard_map/ppermute | solution.py:480
  69.3 0.0 collective-permute-done.5.near1
  69.3 0.8 shard_map.69
  70.1 17.0 %all_to_all.26 = f32[16,40,128]{2,1,0:T(8,128)S(1)} all-to-all(f32[16,40,128]{2,1,0:T(8,128)S(1)} %bitcast.19), channel_id=1, replica_groups={{0,16,32,48,64,80,96,112,128,144,160,176,192,208,224,240},{8,24,40,56,7..., dimensions={0} | all-to-all | bytes 655360 | tf_op jit(solution)/shard_map/all_to_all | solution.py:462
  87.1 0.7 broadcast_in_dim.20
  87.9 3.5 %all-to-all-start.4 = ((f32[16,40,128]{2,1,0:T(8,128)}), f32[16,40,128]{2,1,0:T(8,128)S(1)}, u32[]{:S(2)}, u32[]{:S(2)}) async-start(f32[16,40,128]{2,1,0:T(8,128)} %broadcast_in_dim.20), calls=%async_computation.4 | async-start | bytes 655360 | tf_op jit(solution)/shard_map/all_to_all | solution.py:462
  91.4 0.1 collective-permute-start.6
  91.5 6.6 %collective-permute-start.7 = (f32[384,128]{1,0:T(8,128)S(1)}, f32[384,128]{1,0:T(8,128)S(1)}, u32[]{:S(2)}, u32[]{:S(2)}) collective-permute-start(f32[384,128]{1,0:T(8,128)S(1)} %get-tuple-element.65.rest1), channel_id=1, source_target_pairs={{0,7},{1,0},{2,1},{3,2},{4,3},{5,4},{6,5},{7,6},{8,9},{9,10},{10,1... | collective-permute-start | bytes 589832 | tf_op jit(solution)/shard_map/ppermute | solution.py:480
  98.1 3.2 %collective-permute-done.6.far_rest = f32[384,128]{1,0:T(8,128)S(1)} collective-permute-done((f32[384,128]{1,0:T(8,128)S(1)}, f32[384,128]{1,0:T(8,128)S(1)}, u32[]{:S(2)}, u32[]{:S(2)}) %collective-permute-start.6) | collective-permute-done | bytes 196640 | tf_op jit(solution)/shard_map/ppermute | solution.py:480
  101.3 0.0 collective-permute-done.7.near_rest
  101.3 0.3 all-to-all-done.4
  101.6 4.0 %shard_map.70.q_in = f32[2,256,128]{2,1,0:T(8,128)S(1)} custom-call(f32[5,128,128]{2,1,0:T(8,128)S(1)} %bitcast.17, f32[384,128]{1,0:T(8,128)S(1)} %collective-permute-done.6.far_rest, f32[384,128]{1,0:T(8,128)S(1)} %get-tuple-element.64.rest0, f32[384,128]{1,0:T(8,128)S(1)} %get-tuple-element.65.rest1, f32[384,128]{1,0:T(8,128)S(1)} %collective-permute-done.7.near_rest, ...), custom_call_target="tpu_custom_call" | custom-call | tf_op jit(solution)/shard_map/pallas_call | solution.py:32
  105.6 4.6 %shard_map.71 = (f32[384,256]{1,0:T(8,128)S(1)}, f32[768,128]{1,0:T(8,128)S(1)}, f32[768,128]{1,0:T(8,128)S(1)}, f32[256,256]{1,0:T(8,128)S(1)}) custom-call(f32[5,128,128]{2,1,0:T(8,128)S(1)} %bitcast.18, f32[128,128]{1,0:T(8,128)S(1)} %get-tuple-element.63.inner, f32[512,128]{1,0:T(8,128)S(1)} %collective-permute-done.4.far0, ...), custom_call_target="tpu_custom_call" | custom-call | tf_op jit(solution)/shard_map/pallas_call | solution.py:32
  110.2 10.1 %collective-permute-start.8 = (f32[384,256]{1,0:T(8,128)S(1)}, f32[384,256]{1,0:T(8,128)S(1)}, u32[]{:S(2)}, u32[]{:S(2)}) collective-permute-start(f32[384,256]{1,0:T(8,128)S(1)} %get-tuple-element.66), channel_id=1, source_target_pairs={{0,8},{8,0},{16,24},{24,16},{32,40},{40,32},{48,56},{56,48},{64,72... | collective-permute-start | bytes 1179656 | tf_op jit(solution)/shard_map/ppermute | solution.py:470
  120.3 0.3 shard_map.72
  120.6 1.0 collective-permute-done.8.got
  121.6 0.9 shard_map.73
  (14 shorter events, 0.2 us)
Async XLA Ops:
  0.6 1.0 copy-start
  1.7 0.8 copy-start.3
  1.7 1.9 %collective-permute-start = (f32[256,256]{1,0:T(8,128)S(1)}, f32[256,256]{1,0:T(8,128)S(1)}, u32[]{:S(2)}, u32[]{:S(2)}) collective-permute-start(f32[256,256]{1,0:T(8,128)S(1)} %get-tuple-element.38), channel_id=1, source_target_pairs={{0,8},{8,0},{16,24},{24,16},{32,40},{40,32},{48,56},{56,48},{64,72... | collective-permute-start | bytes 786440 | tf_op jit(solution)/shard_map/ppermute | solution.py:470
  3.7 12.7 %collective-permute-start.1 = (f32[512,256]{1,0:T(8,128)S(1)}, f32[512,256]{1,0:T(8,128)S(1)}, u32[]{:S(2)}, u32[]{:S(2)}) collective-permute-start(f32[512,256]{1,0:T(8,128)S(1)} %maximum_multiply_fusion.x), channel_id=1, source_target_pairs={{0,7},{1,0},{2,1},{3,2},{4,3},{5,4},{6,5},{7,6},{8,9},{9,10},{10,1... | collective-permute-start | bytes 1572872 | tf_op jit(solution)/shard_map/ppermute | solution.py:480
  7.9 19.5 %all-to-all-start = ((f32[16,24,128]{2,1,0:T(8,128)}), f32[16,24,128]{2,1,0:T(8,128)S(1)}, u32[]{:S(2)}, u32[]{:S(2)}) async-start(f32[16,24,128]{2,1,0:T(8,128)} %bitcast.3), calls=%async_computation | async-start | bytes 393216 | tf_op jit(solution)/shard_map/all_to_all | solution.py:462
  16.4 2.2 %copy-start.1 = (f32[256,512]{1,0:T(8,128)S(1)}, f32[256,512]{1,0:T(8,128)}, u32[]{:S(2)}) copy-start(f32[256,512]{1,0:T(8,128)} %constant.68.clone) | copy-start | bytes 1572868
  16.4 2.2 %copy-start.2 = (s32[4,256]{1,0:T(4,128)S(1)}, s32[4,256]{1,0:T(4,128)}, u32[]{:S(2)}) copy-start(s32[4,256]{1,0:T(4,128)} %param.6) | copy-start | bytes 12292
  17.1 4.7 %collective-permute-start.2 = (f32[2,128,128]{2,1,0:T(8,128)S(1)}, f32[2,128,128]{2,1,0:T(8,128)S(1)}, u32[]{:S(2)}, u32[]{:S(2)}) collective-permute-start(f32[2,128,128]{2,1,0:T(8,128)S(1)} %get-tuple-element.41), channel_id=1, source_target_pairs={{0,16},{8,24},{16,0},{24,8},{32,48},{40,56},{48,32},{56,40},{64,80... | collective-permute-start | bytes 393224 | tf_op jit(solution)/shard_map/ppermute | solution.py:470
  44.0 12.4 %all-to-all-start.2 = ((f32[16,16,128]{2,1,0:T(8,128)}), f32[16,16,128]{2,1,0:T(8,128)S(1)}, u32[]{:S(2)}, u32[]{:S(2)}) async-start(f32[16,16,128]{2,1,0:T(8,128)} %shard_map.64), calls=%async_computation.2 | async-start | bytes 262144 | tf_op jit(solution)/shard_map/all_to_all | solution.py:462
  48.6 6.3 %collective-permute-start.3 = (f32[384,128]{1,0:T(8,128)S(1)}, f32[384,128]{1,0:T(8,128)S(1)}, u32[]{:S(2)}, u32[]{:S(2)}) collective-permute-start(f32[384,128]{1,0:T(8,128)S(1)} %shard_map.65), channel_id=1, source_target_pairs={{0,7},{1,0},{2,1},{3,2},{4,3},{5,4},{6,5},{7,6},{8,9},{9,10},{10,1... | collective-permute-start | bytes 589832 | tf_op jit(solution)/shard_map/ppermute | solution.py:480
  60.4 8.9 %collective-permute-start.4 = (f32[512,128]{1,0:T(8,128)S(1)}, f32[512,128]{1,0:T(8,128)S(1)}, u32[]{:S(2)}, u32[]{:S(2)}) collective-permute-start(f32[512,128]{1,0:T(8,128)S(1)} %get-tuple-element.49.x0), channel_id=1, source_target_pairs={{0,1},{1,2},{2,3},{3,4},{4,5},{5,6},{6,7},{7,0},{8,15},{9,8},{10,9... | collective-permute-start | bytes 786440 | tf_op jit(solution)/shard_map/ppermute | solution.py:480
  62.1 7.1 %collective-permute-start.5 = (f32[512,128]{1,0:T(8,128)S(1)}, f32[512,128]{1,0:T(8,128)S(1)}, u32[]{:S(2)}, u32[]{:S(2)}) collective-permute-start(f32[512,128]{1,0:T(8,128)S(1)} %get-tuple-element.50.x1), channel_id=1, source_target_pairs={{0,7},{1,0},{2,1},{3,2},{4,3},{5,4},{6,5},{7,6},{8,9},{9,10},{10,1... | collective-permute-start | bytes 786440 | tf_op jit(solution)/shard_map/ppermute | solution.py:480
  87.9 13.7 %all-to-all-start.4 = ((f32[16,40,128]{2,1,0:T(8,128)}), f32[16,40,128]{2,1,0:T(8,128)S(1)}, u32[]{:S(2)}, u32[]{:S(2)}) async-start(f32[16,40,128]{2,1,0:T(8,128)} %broadcast_in_dim.20), calls=%async_computation.4 | async-start | bytes 655360 | tf_op jit(solution)/shard_map/all_to_all | solution.py:462
  91.4 9.8 %collective-permute-start.6 = (f32[384,128]{1,0:T(8,128)S(1)}, f32[384,128]{1,0:T(8,128)S(1)}, u32[]{:S(2)}, u32[]{:S(2)}) collective-permute-start(f32[384,128]{1,0:T(8,128)S(1)} %get-tuple-element.64.rest0), channel_id=1, source_target_pairs={{0,1},{1,2},{2,3},{3,4},{4,5},{5,6},{6,7},{7,0},{8,15},{9,8},{10,9... | collective-permute-start | bytes 589832 | tf_op jit(solution)/shard_map/ppermute | solution.py:480
  91.5 9.8 %collective-permute-start.7 = (f32[384,128]{1,0:T(8,128)S(1)}, f32[384,128]{1,0:T(8,128)S(1)}, u32[]{:S(2)}, u32[]{:S(2)}) collective-permute-start(f32[384,128]{1,0:T(8,128)S(1)} %get-tuple-element.65.rest1), channel_id=1, source_target_pairs={{0,7},{1,0},{2,1},{3,2},{4,3},{5,4},{6,5},{7,6},{8,9},{9,10},{10,1... | collective-permute-start | bytes 589832 | tf_op jit(solution)/shard_map/ppermute | solution.py:480
  110.2 11.4 %collective-permute-start.8 = (f32[384,256]{1,0:T(8,128)S(1)}, f32[384,256]{1,0:T(8,128)S(1)}, u32[]{:S(2)}, u32[]{:S(2)}) collective-permute-start(f32[384,256]{1,0:T(8,128)S(1)} %get-tuple-element.66), channel_id=1, source_target_pairs={{0,8},{8,0},{16,24},{24,16},{32,40},{40,32},{48,56},{56,48},{64,72... | collective-permute-start | bytes 1179656 | tf_op jit(solution)/shard_map/ppermute | solution.py:470
